TPU v7x, 768 devices: a whole 4x8x12 slice. The times are simulated.
768 devices in a mesh: comp: 8 (over y), dom: 96 (over z, x, core).
Axes of the slice: x: 4, y: 8, z: 12, core: 2. Of those that a mesh axis runs over, the one named last changes fastest.
Arguments:
- atm_fields: bfloat16 [24, 1572864], P(None, ('comp', 'dom')), may hold values from -6 to 6
- send_cols: int32 [8, 96, 8, 4, 256], P('comp', 'dom'), may hold values from 0 to 2047
- live_blocks: int32 [8, 96, 8], P('comp', 'dom'), may hold values from 1 to 4, as said below
- remap_weights: bfloat16 [8, 96, 8, 4, 256, 256], P('comp', 'dom'), may hold values from -0.375 to 0.375
- row_map: int32 [8, 96, 8, 4, 256], P('comp', 'dom'), may hold values from 0 to 4095
- ocean_depth: float32 [3072, 1024], P('dom', 'comp'), may hold values from 0.25 to 8
- wet_mask: int32 [3072, 1024], P('dom', 'comp'), may hold values 0 or 1
- sea_level: float32 [3072, 1024], P('dom', 'comp'), may hold values from -3 to 3
- east_vel: float32 [3072, 1024], P('dom', 'comp'), may hold values from -0.3 to 0.3
- north_vel: float32 [3072, 1024], P('dom', 'comp'), may hold values from -0.3 to 0.3
Outputs:
- ocean_fluxes: float32 [24, 3072, 1024], P(None, 'dom', 'comp')
- ocean_state: float32 [3, 3072, 1024], P(None, 'dom', 'comp')
Inputs may be any that keep to these rules, and one draw needn't show every extreme that they name: `live_blocks`: every receiving device has exactly 4 live blocks from at least one source group.
All inputs are finite; a program needn't handle non-finite values. No bound on the sum of `wet_mask` on one device may be relied on, other than what follows from the above.
Results may differ from a plain program's by a relative error of at most 0.0003.
Values may be sent and summed in bfloat16 or wider, within the bound.
No kernel may reach another device: no remote copies, remote signals or barrier semaphores. Data moves between devices by JAX's collectives and lax.ppermute only.
A program may use at most 64 MiB of HBM per device.

v0:
```python
import functools

import jax
import jax.numpy as jnp
from jax import lax
from jax.sharding import Mesh
from jax.sharding import PartitionSpec as P

NSUB = 4
COMP_DOM = ("comp", "dom_0", "dom_1", "dom_2")
DOM = ("dom_0", "dom_1", "dom_2")


courant = 0.5
friction = 0.05


def padded(cells, sides, width):
    for axis, dim in sides:
        count = lax.axis_size(axis)
        ends = count - 1
        head = lax.slice_in_dim(cells, 0, width, axis=dim)
        tail = lax.slice_in_dim(cells, cells.shape[dim] - width, cells.shape[dim], axis=dim)
        cells = jnp.concatenate(
            [
                lax.ppermute(tail, axis, [(i, (i + 1) % count) for i in range(ends)]),
                cells,
                lax.ppermute(head, axis, [((i + 1) % count, i) for i in range(ends)]),
            ],
            axis=dim,
        )
    return cells


def by_axis(array, axes):
    return functools.reduce(lax.pmax, axes, array)


def level_update(level, flux_x, flux_y, fresh, wetness, step_dt):
    diverge = 0.5 * (flux_x[1:-1, 2:] - flux_x[1:-1, :-2] + (flux_y[2:, 1:-1] - flux_y[:-2, 1:-1]))
    return wetness[1:-1, 1:-1] * (level[1:-1, 1:-1] + step_dt * (fresh[1:-1, 1:-1] - diverge))


def velocity_update(east, north, level_ext, rotation, push_x, push_y, wetness, step_dt):
    grad_x = 0.5 * (level_ext[1:-1, 2:] - level_ext[1:-1, :-2])
    grad_y = 0.5 * (level_ext[2:, 1:-1] - level_ext[:-2, 1:-1])
    new_east = wetness * (east + step_dt * (rotation * north - grad_x + push_x - friction * east))
    new_north = wetness * (
        north + step_dt * (-rotation * east - grad_y + push_y - friction * north)
    )
    return (new_east, new_north)


def deposit(total, blocks, weights, alive, targets):
    contrib = jnp.einsum("sknb,skob->skno", blocks, weights, preferred_element_type=jnp.float32)
    contrib = contrib * alive[:, :, None, None]
    flat = jnp.transpose(contrib, (2, 0, 1, 3)).reshape(total.shape[0], -1)
    return total.at[:, targets.reshape(-1)].add(flat)


def shards(
    atm_fields,
    send_cols,
    live_blocks,
    remap_weights,
    row_map,
    ocean_depth,
    wet_mask,
    sea_level,
    east_vel,
    north_vel,
):
    weights = remap_weights[0, 0]
    targets = row_map[0, 0]
    live = live_blocks[0, 0]
    capacity = weights.shape[1]
    nfield = atm_fields.shape[0]
    nrows_dev, ncols_dev = ocean_depth.shape
    slots = jnp.arange(capacity, dtype=jnp.int32)
    alive = (slots[None, :] < live[:, None]).astype(jnp.float32)
    wetness = wet_mask.astype(jnp.float32)
    empty = jnp.zeros((nfield, nrows_dev * ncols_dev), jnp.float32)
    columns = send_cols[0, 0]
    picked = jnp.take(atm_fields, columns.reshape(-1), axis=1)
    picked = picked.reshape(nfield, columns.shape[0], capacity, -1)
    picked = jnp.transpose(picked, (1, 2, 0, 3))
    received = lax.all_to_all(picked, "comp", split_axis=0, concat_axis=0, tiled=True)
    fluxes = deposit(empty, received, weights, alive, targets)
    fluxes = fluxes.reshape(nfield, nrows_dev, ncols_dev)
    push_x = fluxes[0] / ocean_depth
    push_y = fluxes[1] / ocean_depth
    fresh = fluxes[2]
    statics = jnp.stack([ocean_depth, wetness, fresh])
    statics_ext = padded(statics, (("comp", 2), (DOM, 1)), 2)
    total_rows = nrows_dev * lax.axis_size(DOM)
    global_rows = lax.axis_index(DOM) * nrows_dev + jnp.arange(nrows_dev, dtype=jnp.int32)
    rotation = (0.1 + 0.4 * (global_rows.astype(jnp.float32) + 0.5) / total_rows)[:, None]
    root_depth = jnp.sqrt(ocean_depth)
    level, east, north = (sea_level, east_vel, north_vel)
    for substep in range(NSUB):
        local_speed = jnp.max(root_depth + wetness * (jnp.abs(east) + jnp.abs(north)))
        fastest = by_axis(local_speed, COMP_DOM)
        step_dt = courant / fastest
        state = jnp.stack([level, east, north])
        state_ext = padded(state, (("comp", 2), (DOM, 1)), 2)
        depth_ext, wet_ext, fresh_ext = (statics_ext[0], statics_ext[1], statics_ext[2])
        flux_x = depth_ext * state_ext[1] * wet_ext
        flux_y = depth_ext * state_ext[2] * wet_ext
        level_ext = level_update(state_ext[0], flux_x, flux_y, fresh_ext, wet_ext, step_dt)
        new_level = level_ext[1:-1, 1:-1]
        east, north = velocity_update(
            east, north, level_ext, rotation, push_x, push_y, wetness, step_dt
        )
        level = new_level
    return (fluxes, jnp.stack([level, east, north]))


def solution(mesh):
    split = Mesh(
        mesh.devices.reshape(mesh.shape["comp"], 12, 4, 2), ("comp", "dom_0", "dom_1", "dom_2")
    )
    return jax.shard_map(
        shards,
        mesh=split,
        in_specs=(
            P(None, COMP_DOM),
            P("comp", DOM, None, None, None),
            P("comp", DOM, None),
            P("comp", DOM, None, None, None, None),
            P("comp", DOM, None, None, None),
            P(DOM, "comp"),
            P(DOM, "comp"),
            P(DOM, "comp"),
            P(DOM, "comp"),
            P(DOM, "comp"),
        ),
        out_specs=(P(None, DOM, "comp"), P(None, DOM, "comp")),
        check_vma=False,
    )
```

profile of v0, /device:TPU:1, one launch (start us, length us, event | category | flops | bytes accessed | tf_op | source)
XLA Modules:
  0.0 407.0 jit_solution(5072814031508105)
XLA Ops:
  3.5 24.0 %gather_fusion = bf16[8192,24]{1,0:T(8,128)(2,1)S(1)} fusion(bf16[24,2048]{0,1:T(8,128)(2,1)S(1)} %copy.14, s32[8192]{0:T(1024)S(1)} %broadcast_clamp_fusion), kind=kCustom, calls=%fused_computation | custom fusion | bytes 819200 | tf_op jit(solution)/shard_map/jit(_take)/gather | solution.py:84
  29.2 7.7 %all-to-all-start = ((bf16[8,4,24,256]{3,2,1,0:T(8,128)(2,1)}), bf16[8,4,24,256]{3,2,1,0:T(8,128)(2,1)S(1)}, u32[]{:S(2)}, u32[]{:S(2)}) async-start(bf16[8,4,24,256]{3,2,1,0:T(8,128)(2,1)} %select_bitcast_fusion), calls=%async_computation | async-start | bytes 786432 | tf_op jit(solution)/shard_map/all_to_all | solution.py:87
  36.9 3.4 collective-permute-start.4
  40.9 1.3 collective-permute-start.5
  42.2 15.3 %pmax.112 = f32[]{:T(128)} all-reduce(f32[]{:T(128)} %add_reduce_fusion.3), channel_id=1, replica_groups=mesh['comp'=8,'dom_0'=12,'dom_1'=4,'dom_2'=2] {'comp'}, use_global_device_ids=true, to_apply=%region_2.3 | all-reduce | flops 1 | bytes 8 | tf_op jit(solution)/shard_map/pmax | solution.py:36
  57.6 28.3 %pmax.113 = f32[]{:T(128)} all-reduce(f32[]{:T(128)} %pmax.112), channel_id=1, replica_groups=mesh['comp'=8,'dom_0'=12,'dom_1'=4,'dom_2'=2] {'dom_0'}, use_global_device_ids=true, to_apply=%region_3.4 | all-reduce | flops 1 | bytes 8 | tf_op jit(solution)/shard_map/pmax | solution.py:36
  86.0 9.1 %pmax.114 = f32[]{:T(128)} all-reduce(f32[]{:T(128)} %pmax.113), channel_id=1, replica_groups=mesh['comp'=8,'dom_0'=12,'dom_1'=4,'dom_2'=2] {'dom_1'}, use_global_device_ids=true, to_apply=%region_4.5 | all-reduce | flops 1 | bytes 8 | tf_op jit(solution)/shard_map/pmax | solution.py:36
  95.2 15.2 %pmax.115 = f32[]{:T(128)} all-reduce(f32[]{:T(128)} %pmax.114), channel_id=1, replica_groups=mesh['comp'=8,'dom_0'=12,'dom_1'=4,'dom_2'=2] {'dom_2'}, use_global_device_ids=true, to_apply=%region_5.6 | all-reduce | flops 1 | bytes 8 | tf_op jit(solution)/shard_map/pmax | solution.py:36
  111.2 1.9 collective-permute-start.6
  113.1 2.4 collective-permute-start.7
  115.5 3.4 fusion.5
  119.7 2.6 copy.18
  122.3 44.8 %scatter_custom_fusion = f32[24,4096]{0,1:T(8,128)S(1)} fusion(s32[8192]{0:T(1024)S(1)} %bitcast.152, f32[8192,24]{1,0:T(8,128)} %copy.18, f32[]{:T(128)} %constant.17.clone.1), kind=kCustom, calls=%fused_computation.9 | custom fusion | flops 196608 | bytes 393728 | tf_op jit(solution)/shard_map/scatter-add | solution.py:58
  167.1 2.8 slice_reduce_fusion.1
  170.0 2.8 collective-permute-start
  172.8 1.3 collective-permute-start.1
  174.2 4.1 %collective-permute-done.1 = f32[3,32,2]{2,1,0:T(8,128)S(1)} collective-permute-done((f32[3,32,2]{2,1,0:T(8,128)S(1)}, f32[3,32,2]{2,1,0:T(8,128)S(1)}, u32[]{:S(2)}, u32[]{:S(2)}) %collective-permute-start.1) | collective-permute-done | bytes 800 | tf_op jit(solution)/shard_map/ppermute | solution.py:28
  178.4 3.9 collective-permute-start.2
  182.3 1.9 collective-permute-start.3
  184.2 3.0 collective-permute-done.3
  188.3 2.8 collective-permute-start.8
  191.2 1.3 collective-permute-start.9
  192.5 3.8 collective-permute-done.9
  196.4 3.5 collective-permute-start.10
  199.9 1.9 collective-permute-start.11
  201.8 14.3 %pmax.116 = f32[]{:T(128)} all-reduce(f32[]{:T(128)} %get-tuple-element.15), channel_id=1, replica_groups=mesh['comp'=8,'dom_0'=12,'dom_1'=4,'dom_2'=2] {'comp'}, use_global_device_ids=true, to_apply=%region_7.8 | all-reduce | flops 1 | bytes 8 | tf_op jit(solution)/shard_map/pmax | solution.py:36
  216.1 19.9 %pmax.117 = f32[]{:T(128)} all-reduce(f32[]{:T(128)} %pmax.116), channel_id=1, replica_groups=mesh['comp'=8,'dom_0'=12,'dom_1'=4,'dom_2'=2] {'dom_0'}, use_global_device_ids=true, to_apply=%region_8.9 | all-reduce | flops 1 | bytes 8 | tf_op jit(solution)/shard_map/pmax | solution.py:36
  236.0 11.6 %pmax.118 = f32[]{:T(128)} all-reduce(f32[]{:T(128)} %pmax.117), channel_id=1, replica_groups=mesh['comp'=8,'dom_0'=12,'dom_1'=4,'dom_2'=2] {'dom_1'}, use_global_device_ids=true, to_apply=%region_9.10 | all-reduce | flops 1 | bytes 8 | tf_op jit(solution)/shard_map/pmax | solution.py:36
  247.6 13.1 %pmax.119 = f32[]{:T(128)} all-reduce(f32[]{:T(128)} %pmax.118), channel_id=1, replica_groups=mesh['comp'=8,'dom_0'=12,'dom_1'=4,'dom_2'=2] {'dom_2'}, use_global_device_ids=true, to_apply=%region_10.11 | all-reduce | flops 1 | bytes 8 | tf_op jit(solution)/shard_map/pmax | solution.py:36
  262.5 1.6 collective-permute-start.12
  264.2 1.3 collective-permute-start.13
  265.5 3.8 collective-permute-done.13
  269.4 5.0 %collective-permute-start.14 = (f32[3,2,132]{2,1,0:T(2,128)S(1)}, f32[3,2,132]{2,1,0:T(2,128)S(1)}, u32[]{:S(2)}, u32[]{:S(2)}) collective-permute-start(f32[3,2,132]{2,1,0:T(2,128)S(1)} %get-tuple-element.30), channel_id=1, source_target_pairs={{0,1},{1,2},{2,3},{3,4},{4,5},{5,6},{6,7},{7,8},{8,9},{9,10},{10,1... | collective-permute-start | bytes 9512 | tf_op jit(solution)/shard_map/ppermute | solution.py:26
  274.4 1.9 collective-permute-start.15
  276.3 16.0 %pmax.120 = f32[]{:T(128)} all-reduce(f32[]{:T(128)} %get-tuple-element.12), channel_id=1, replica_groups=mesh['comp'=8,'dom_0'=12,'dom_1'=4,'dom_2'=2] {'comp'}, use_global_device_ids=true, to_apply=%region_12.13 | all-reduce | flops 1 | bytes 8 | tf_op jit(solution)/shard_map/pmax | solution.py:36
  292.3 18.6 %pmax.121 = f32[]{:T(128)} all-reduce(f32[]{:T(128)} %pmax.120), channel_id=1, replica_groups=mesh['comp'=8,'dom_0'=12,'dom_1'=4,'dom_2'=2] {'dom_0'}, use_global_device_ids=true, to_apply=%region_13.14 | all-reduce | flops 1 | bytes 8 | tf_op jit(solution)/shard_map/pmax | solution.py:36
  311.0 6.9 %pmax.122 = f32[]{:T(128)} all-reduce(f32[]{:T(128)} %pmax.121), channel_id=1, replica_groups=mesh['comp'=8,'dom_0'=12,'dom_1'=4,'dom_2'=2] {'dom_1'}, use_global_device_ids=true, to_apply=%region_14.15 | all-reduce | flops 1 | bytes 8 | tf_op jit(solution)/shard_map/pmax | solution.py:36
  317.8 15.5 %pmax.123 = f32[]{:T(128)} all-reduce(f32[]{:T(128)} %pmax.122), channel_id=1, replica_groups=mesh['comp'=8,'dom_0'=12,'dom_1'=4,'dom_2'=2] {'dom_2'}, use_global_device_ids=true, to_apply=%region_15.16 | all-reduce | flops 1 | bytes 8 | tf_op jit(solution)/shard_map/pmax | solution.py:36
  335.1 1.4 collective-permute-start.16
  336.5 1.3 collective-permute-start.17
  337.8 4.1 %collective-permute-done.17 = f32[3,32,2]{2,1,0:T(8,128)S(1)} collective-permute-done((f32[3,32,2]{2,1,0:T(8,128)S(1)}, f32[3,32,2]{2,1,0:T(8,128)S(1)}, u32[]{:S(2)}, u32[]{:S(2)}) %collective-permute-start.17) | collective-permute-done | bytes 800 | tf_op jit(solution)/shard_map/ppermute | solution.py:28
  342.0 5.0 %collective-permute-start.18 = (f32[3,2,132]{2,1,0:T(2,128)S(1)}, f32[3,2,132]{2,1,0:T(2,128)S(1)}, u32[]{:S(2)}, u32[]{:S(2)}) collective-permute-start(f32[3,2,132]{2,1,0:T(2,128)S(1)} %get-tuple-element.28), channel_id=1, source_target_pairs={{0,1},{1,2},{2,3},{3,4},{4,5},{5,6},{6,7},{7,8},{8,9},{9,10},{10,1... | collective-permute-start | bytes 9512 | tf_op jit(solution)/shard_map/ppermute | solution.py:26
  347.0 1.9 collective-permute-start.19
  348.9 16.0 %pmax.124 = f32[]{:T(128)} all-reduce(f32[]{:T(128)} %get-tuple-element.9), channel_id=1, replica_groups=mesh['comp'=8,'dom_0'=12,'dom_1'=4,'dom_2'=2] {'comp'}, use_global_device_ids=true, to_apply=%region_17.18 | all-reduce | flops 1 | bytes 8 | tf_op jit(solution)/shard_map/pmax | solution.py:36
  364.9 16.7 %pmax.125 = f32[]{:T(128)} all-reduce(f32[]{:T(128)} %pmax.124), channel_id=1, replica_groups=mesh['comp'=8,'dom_0'=12,'dom_1'=4,'dom_2'=2] {'dom_0'}, use_global_device_ids=true, to_apply=%region_18.19 | all-reduce | flops 1 | bytes 8 | tf_op jit(solution)/shard_map/pmax | solution.py:36
  381.6 8.1 %pmax.126 = f32[]{:T(128)} all-reduce(f32[]{:T(128)} %pmax.125), channel_id=1, replica_groups=mesh['comp'=8,'dom_0'=12,'dom_1'=4,'dom_2'=2] {'dom_1'}, use_global_device_ids=true, to_apply=%region_19.20 | all-reduce | flops 1 | bytes 8 | tf_op jit(solution)/shard_map/pmax | solution.py:36
  389.6 1.4 copy.19
  391.0 14.3 %pmax.127 = f32[]{:T(128)} all-reduce(f32[]{:T(128)} %pmax.126), channel_id=1, replica_groups=mesh['comp'=8,'dom_0'=12,'dom_1'=4,'dom_2'=2] {'dom_2'}, use_global_device_ids=true, to_apply=%region_20.21 | all-reduce | flops 1 | bytes 8 | tf_op jit(solution)/shard_map/pmax | solution.py:36
  (83 shorter events, 10.9 us)
Async XLA Ops:
  27.5 9.3 %copy-start.2 = (f32[32,128]{1,0:T(8,128)S(1)}, f32[32,128]{1,0:T(8,128)}, u32[]{:S(2)}) copy-start(f32[32,128]{1,0:T(8,128)} %param.18) | copy-start | bytes 49156
  27.5 9.3 %copy-start.3 = (f32[32,128]{1,0:T(8,128)S(1)}, f32[32,128]{1,0:T(8,128)}, u32[]{:S(2)}) copy-start(f32[32,128]{1,0:T(8,128)} %param.19) | copy-start | bytes 49156
  27.5 9.3 %copy-start.4 = (f32[32,128]{1,0:T(8,128)S(1)}, f32[32,128]{1,0:T(8,128)}, u32[]{:S(2)}) copy-start(f32[32,128]{1,0:T(8,128)} %param.17) | copy-start | bytes 49156
  27.5 12.8 %copy-start = (f32[32,128]{1,0:T(8,128)S(1)}, f32[32,128]{1,0:T(8,128)}, u32[]{:S(2)}) copy-start(f32[32,128]{1,0:T(8,128)} %param.15) | copy-start | bytes 49156
  27.5 12.8 %copy-start.1 = (s32[32,128]{1,0:T(8,128)S(1)}, s32[32,128]{1,0:T(8,128)}, u32[]{:S(2)}) copy-start(s32[32,128]{1,0:T(8,128)} %param.16) | copy-start | bytes 49156
  27.6 30.0 %copy-start.5 = (s32[1,1,8,4,256]{4,3,2,1,0:T(4,128)S(1)}, s32[1,1,8,4,256]{4,3,2,1,0:T(4,128)}, u32[]{:S(2)}) copy-start(s32[1,1,8,4,256]{4,3,2,1,0:T(4,128)} %param.14) | copy-start | bytes 98308
  27.6 67.5 %copy-start.6 = (s32[1,1,8]{2,1,0:T(1,128)S(1)}, s32[1,1,8]{2,1,0:T(1,128)}, u32[]{:S(2)}) copy-start(s32[1,1,8]{2,1,0:T(1,128)} %param.12) | copy-start | bytes 100
  29.2 86.4 %all-to-all-start = ((bf16[8,4,24,256]{3,2,1,0:T(8,128)(2,1)}), bf16[8,4,24,256]{3,2,1,0:T(8,128)(2,1)S(1)}, u32[]{:S(2)}, u32[]{:S(2)}) async-start(bf16[8,4,24,256]{3,2,1,0:T(8,128)(2,1)} %select_bitcast_fusion), calls=%async_computation | async-start | bytes 786432 | tf_op jit(solution)/shard_map/all_to_all | solution.py:87
  36.9 74.1 %collective-permute-start.4 = (f32[3,32,2]{2,1,0:T(8,128)S(1)}, f32[3,32,2]{2,1,0:T(8,128)S(1)}, u32[]{:S(2)}, u32[]{:S(2)}) collective-permute-start(f32[3,32,2]{2,1,0:T(8,128)S(1)} %get-tuple-element.50), channel_id=1, source_target_pairs={{0,96},{96,192},{192,288},{288,384},{384,480},{480,576},{576,672},... | collective-permute-start | bytes 2312 | tf_op jit(solution)/shard_map/ppermute | solution.py:26
  40.9 70.2 %collective-permute-start.5 = (f32[3,32,2]{2,1,0:T(8,128)S(1)}, f32[3,32,2]{2,1,0:T(8,128)S(1)}, u32[]{:S(2)}, u32[]{:S(2)}) collective-permute-start(f32[3,32,2]{2,1,0:T(8,128)S(1)} %get-tuple-element.51), channel_id=1, source_target_pairs={{96,0},{192,96},{288,192},{384,288},{480,384},{576,480},{672,576},... | collective-permute-start | bytes 2312 | tf_op jit(solution)/shard_map/ppermute | solution.py:28
  111.2 62.9 %collective-permute-start.6 = (f32[3,2,132]{2,1,0:T(2,128)S(1)}, f32[3,2,132]{2,1,0:T(2,128)S(1)}, u32[]{:S(2)}, u32[]{:S(2)}) collective-permute-start(f32[3,2,132]{2,1,0:T(2,128)S(1)} %get-tuple-element.36), channel_id=1, source_target_pairs={{0,1},{1,2},{2,3},{3,4},{4,5},{5,6},{6,7},{7,8},{8,9},{9,10},{10,1... | collective-permute-start | bytes 9512 | tf_op jit(solution)/shard_map/ppermute | solution.py:26
  113.1 61.0 %collective-permute-start.7 = (f32[3,2,132]{2,1,0:T(2,128)S(1)}, f32[3,2,132]{2,1,0:T(2,128)S(1)}, u32[]{:S(2)}, u32[]{:S(2)}) collective-permute-start(f32[3,2,132]{2,1,0:T(2,128)S(1)} %get-tuple-element.37), channel_id=1, source_target_pairs={{1,0},{2,1},{3,2},{4,3},{5,4},{6,5},{7,6},{8,7},{9,8},{10,9},{11,1... | collective-permute-start | bytes 9512 | tf_op jit(solution)/shard_map/ppermute | solution.py:28
  170.0 4.2 %collective-permute-start = (f32[3,32,2]{2,1,0:T(8,128)S(1)}, f32[3,32,2]{2,1,0:T(8,128)S(1)}, u32[]{:S(2)}, u32[]{:S(2)}) collective-permute-start(f32[3,32,2]{2,1,0:T(8,128)S(1)} %get-tuple-element.48), channel_id=1, source_target_pairs={{0,96},{96,192},{192,288},{288,384},{384,480},{480,576},{576,672},... | collective-permute-start | bytes 2312 | tf_op jit(solution)/shard_map/ppermute | solution.py:26
  172.8 5.5 %collective-permute-start.1 = (f32[3,32,2]{2,1,0:T(8,128)S(1)}, f32[3,32,2]{2,1,0:T(8,128)S(1)}, u32[]{:S(2)}, u32[]{:S(2)}) collective-permute-start(f32[3,32,2]{2,1,0:T(8,128)S(1)} %get-tuple-element.49), channel_id=1, source_target_pairs={{96,0},{192,96},{288,192},{384,288},{480,384},{576,480},{672,576},... | collective-permute-start | bytes 2312 | tf_op jit(solution)/shard_map/ppermute | solution.py:28
  178.4 5.8 %collective-permute-start.2 = (f32[3,2,132]{2,1,0:T(2,128)S(1)}, f32[3,2,132]{2,1,0:T(2,128)S(1)}, u32[]{:S(2)}, u32[]{:S(2)}) collective-permute-start(f32[3,2,132]{2,1,0:T(2,128)S(1)} %get-tuple-element.34), channel_id=1, source_target_pairs={{0,1},{1,2},{2,3},{3,4},{4,5},{5,6},{6,7},{7,8},{8,9},{9,10},{10,1... | collective-permute-start | bytes 9512 | tf_op jit(solution)/shard_map/ppermute | solution.py:26
  182.3 4.9 %collective-permute-start.3 = (f32[3,2,132]{2,1,0:T(2,128)S(1)}, f32[3,2,132]{2,1,0:T(2,128)S(1)}, u32[]{:S(2)}, u32[]{:S(2)}) collective-permute-start(f32[3,2,132]{2,1,0:T(2,128)S(1)} %get-tuple-element.35), channel_id=1, source_target_pairs={{1,0},{2,1},{3,2},{4,3},{5,4},{6,5},{7,6},{8,7},{9,8},{10,9},{11,1... | collective-permute-start | bytes 9512 | tf_op jit(solution)/shard_map/ppermute | solution.py:28
  188.3 4.2 %collective-permute-start.8 = (f32[3,32,2]{2,1,0:T(8,128)S(1)}, f32[3,32,2]{2,1,0:T(8,128)S(1)}, u32[]{:S(2)}, u32[]{:S(2)}) collective-permute-start(f32[3,32,2]{2,1,0:T(8,128)S(1)} %get-tuple-element.46), channel_id=1, source_target_pairs={{0,96},{96,192},{192,288},{288,384},{384,480},{480,576},{576,672},... | collective-permute-start | bytes 2312 | tf_op jit(solution)/shard_map/ppermute | solution.py:26
  191.2 5.1 %collective-permute-start.9 = (f32[3,32,2]{2,1,0:T(8,128)S(1)}, f32[3,32,2]{2,1,0:T(8,128)S(1)}, u32[]{:S(2)}, u32[]{:S(2)}) collective-permute-start(f32[3,32,2]{2,1,0:T(8,128)S(1)} %get-tuple-element.47), channel_id=1, source_target_pairs={{96,0},{192,96},{288,192},{384,288},{480,384},{576,480},{672,576},... | collective-permute-start | bytes 2312 | tf_op jit(solution)/shard_map/ppermute | solution.py:28
  196.4 65.0 %collective-permute-start.10 = (f32[3,2,132]{2,1,0:T(2,128)S(1)}, f32[3,2,132]{2,1,0:T(2,128)S(1)}, u32[]{:S(2)}, u32[]{:S(2)}) collective-permute-start(f32[3,2,132]{2,1,0:T(2,128)S(1)} %get-tuple-element.32), channel_id=1, source_target_pairs={{0,1},{1,2},{2,3},{3,4},{4,5},{5,6},{6,7},{7,8},{8,9},{9,10},{10,1... | collective-permute-start | bytes 9512 | tf_op jit(solution)/shard_map/ppermute | solution.py:26
  199.9 61.6 %collective-permute-start.11 = (f32[3,2,132]{2,1,0:T(2,128)S(1)}, f32[3,2,132]{2,1,0:T(2,128)S(1)}, u32[]{:S(2)}, u32[]{:S(2)}) collective-permute-start(f32[3,2,132]{2,1,0:T(2,128)S(1)} %get-tuple-element.33), channel_id=1, source_target_pairs={{1,0},{2,1},{3,2},{4,3},{5,4},{6,5},{7,6},{8,7},{9,8},{10,9},{11,1... | collective-permute-start | bytes 9512 | tf_op jit(solution)/shard_map/ppermute | solution.py:28
  262.5 2.9 collective-permute-start.12
  264.2 5.1 %collective-permute-start.13 = (f32[3,32,2]{2,1,0:T(8,128)S(1)}, f32[3,32,2]{2,1,0:T(8,128)S(1)}, u32[]{:S(2)}, u32[]{:S(2)}) collective-permute-start(f32[3,32,2]{2,1,0:T(8,128)S(1)} %get-tuple-element.45), channel_id=1, source_target_pairs={{96,0},{192,96},{288,192},{384,288},{480,384},{576,480},{672,576},... | collective-permute-start | bytes 2312 | tf_op jit(solution)/shard_map/ppermute | solution.py:28
  269.4 64.6 %collective-permute-start.14 = (f32[3,2,132]{2,1,0:T(2,128)S(1)}, f32[3,2,132]{2,1,0:T(2,128)S(1)}, u32[]{:S(2)}, u32[]{:S(2)}) collective-permute-start(f32[3,2,132]{2,1,0:T(2,128)S(1)} %get-tuple-element.30), channel_id=1, source_target_pairs={{0,1},{1,2},{2,3},{3,4},{4,5},{5,6},{6,7},{7,8},{8,9},{9,10},{10,1... | collective-permute-start | bytes 9512 | tf_op jit(solution)/shard_map/ppermute | solution.py:26
  274.4 59.6 %collective-permute-start.15 = (f32[3,2,132]{2,1,0:T(2,128)S(1)}, f32[3,2,132]{2,1,0:T(2,128)S(1)}, u32[]{:S(2)}, u32[]{:S(2)}) collective-permute-start(f32[3,2,132]{2,1,0:T(2,128)S(1)} %get-tuple-element.31), channel_id=1, source_target_pairs={{1,0},{2,1},{3,2},{4,3},{5,4},{6,5},{7,6},{8,7},{9,8},{10,9},{11,1... | collective-permute-start | bytes 9512 | tf_op jit(solution)/shard_map/ppermute | solution.py:28
  335.1 2.7 collective-permute-start.16
  336.5 5.4 %collective-permute-start.17 = (f32[3,32,2]{2,1,0:T(8,128)S(1)}, f32[3,32,2]{2,1,0:T(8,128)S(1)}, u32[]{:S(2)}, u32[]{:S(2)}) collective-permute-start(f32[3,32,2]{2,1,0:T(8,128)S(1)} %get-tuple-element.43), channel_id=1, source_target_pairs={{96,0},{192,96},{288,192},{384,288},{480,384},{576,480},{672,576},... | collective-permute-start | bytes 2312 | tf_op jit(solution)/shard_map/ppermute | solution.py:28
  342.0 64.0 %collective-permute-start.18 = (f32[3,2,132]{2,1,0:T(2,128)S(1)}, f32[3,2,132]{2,1,0:T(2,128)S(1)}, u32[]{:S(2)}, u32[]{:S(2)}) collective-permute-start(f32[3,2,132]{2,1,0:T(2,128)S(1)} %get-tuple-element.28), channel_id=1, source_target_pairs={{0,1},{1,2},{2,3},{3,4},{4,5},{5,6},{6,7},{7,8},{8,9},{9,10},{10,1... | collective-permute-start | bytes 9512 | tf_op jit(solution)/shard_map/ppermute | solution.py:26
  347.0 59.0 %collective-permute-start.19 = (f32[3,2,132]{2,1,0:T(2,128)S(1)}, f32[3,2,132]{2,1,0:T(2,128)S(1)}, u32[]{:S(2)}, u32[]{:S(2)}) collective-permute-start(f32[3,2,132]{2,1,0:T(2,128)S(1)} %get-tuple-element.29), channel_id=1, source_target_pairs={{1,0},{2,1},{3,2},{4,3},{5,4},{6,5},{7,6},{8,7},{9,8},{10,9},{11,1... | collective-permute-start | bytes 9512 | tf_op jit(solution)/shard_map/ppermute | solution.py:28
where the time goes:
time: 408 us; the launch traced here: 407 us
  blocking collectives  239 us (59%)
  starting transfers between devices  55.5 us (14%)
  other arithmetic  51.7 us (13%)
  local copies, waits for them, and re-layouts  34.8 us (9%)
  waiting for transfers between devices  18.8 us (5%)
    pmax x16, blocking collectives, by_axis(): return functools.reduce(lax.pmax, axes, array)  239 us
    scatter-add x1, other arithmetic, deposit(): return total.at[:, targets.reshape(-1)].add(flat)  44.8 us
    ppermute x10, starting transfers between devices, padded(): lax.ppermute(tail, axis, [(i, (i + 1) % count) for i in range(ends)])  31.3 us
    gather x2, local copies, waits for them, and re-layouts, shards(): picked = jnp.take(atm_fields, columns.reshape(-1), axis=1)  24.8 us
    ppermute x10, waiting for transfers between devices, padded(): lax.ppermute(head, axis, [((i + 1) % count, i) for i in range(ends)])  18.8 us
    ppermute x10, starting transfers between devices, padded(): lax.ppermute(head, axis, [((i + 1) % count, i) for i in range(ends)])  16.5 us
  transfers between devices with their start and end apart: 21, of which 5 were waited for; matrix products, arithmetic and copies ran while one was open for 14% of the time, Pallas kernels for 0%

commit v1 on v0

v1 whole, which is shorter than its diff:
```python
import functools

import jax
import jax.numpy as jnp
from jax import lax
from jax.experimental import pallas as pl
from jax.experimental.pallas import tpu as pltpu
from jax.sharding import Mesh
from jax.sharding import PartitionSpec as P

NSUB = 4
DOM_SHAPE = (12, 4, 2)
COMP_DOM = ("comp", "dom_0", "dom_1", "dom_2")
DOM = ("dom_0", "dom_1", "dom_2")
PLANE = ("comp", "dom_1")
COLUMN = ("dom_0", "dom_2")
BF16 = jnp.bfloat16
F32 = jnp.float32

courant = 0.5
friction = 0.05

EDGE = 8


def params(mib=48, **kwargs):
    return pltpu.CompilerParams(vmem_limit_bytes=mib * 1024 * 1024, **kwargs)


def axes_size(axes):
    return functools.reduce(lambda a, b: a * b, [lax.axis_size(a) for a in axes])


def neighbours(array, axes):
    count = axes_size(axes)
    after = lax.ppermute(array[1], axes, [(i + 1, i) for i in range(count - 1)])
    before = lax.ppermute(array[0], axes, [(i, i + 1) for i in range(count - 1)])
    return after, before


def pick_kernel(fields_ref, cols_ref, out_ref, table_ref):
    nfield, ncol = fields_ref.shape
    high = ncol // 256

    @pl.when(pl.program_id(0) == 0)
    def _():
        rows = [fields_ref[:, h * 256 : (h + 1) * 256].astype(F32) for h in range(high)]
        table_ref[...] = jnp.concatenate(rows, axis=0).astype(BF16)

    cols = cols_ref[0]
    width = cols.shape[1]
    low = cols & 255
    upper = cols >> 8
    onehot = jnp.where(lax.broadcasted_iota(jnp.int32, (256, width), 0) == low, 1.0, 0.0).astype(BF16)
    both = jnp.dot(table_ref[...], onehot, preferred_element_type=F32)
    picked = both[:nfield]
    for h in range(1, high):
        picked = jnp.where(upper == h, both[h * nfield : (h + 1) * nfield], picked)
    out_ref[0] = picked.astype(BF16)


def pick(fields, cols):
    groups, _, width = cols.shape
    nfield, ncol = fields.shape
    return pl.pallas_call(
        pick_kernel,
        grid=(groups,),
        in_specs=[
            pl.BlockSpec((nfield, ncol), lambda c: (0, 0)),
            pl.BlockSpec((1, 1, width), lambda c: (c, 0, 0)),
        ],
        out_specs=pl.BlockSpec((1, nfield, width), lambda c: (c, 0, 0)),
        out_shape=jax.ShapeDtypeStruct((groups, nfield, width), BF16),
        scratch_shapes=[pltpu.VMEM((nfield * (ncol // 256), 256), BF16)],
        compiler_params=params(),
    )(fields, cols)


def remap_kernel(live_ref, picked_ref, weights_ref, cells_ref, depth_ref, flux_ref, push_ref, spread_ref, total_ref):
    step = pl.program_id(0)
    nfield = picked_ref.shape[1]
    blocks = weights_ref.shape[1]
    live = live_ref[step]
    cells = cells_ref[0]
    picked = picked_ref[0]
    lows = []
    for k in range(blocks):
        part = slice(k * 256, (k + 1) * 256)
        contrib = lax.dot_general(
            picked[:, part], weights_ref[0, k], (((1,), (1,)), ((), ())), preferred_element_type=F32
        )
        big = contrib.astype(BF16).astype(F32)
        pair = jnp.concatenate([big, contrib - big], axis=0).astype(BF16)
        cell = cells[:, part]
        alive = jnp.int32(k) < live
        upper = jnp.where(alive, (cell >> 7) & 15, -1)
        for h in range(16):
            spread_ref[h * 2 * nfield : (h + 1) * 2 * nfield, part] = jnp.where(upper == h, pair, jnp.zeros_like(pair))
    low = ((cells >> 11) << 7) | (cells & 127)
    width = cells.shape[1]
    onehot = jnp.where(lax.broadcasted_iota(jnp.int32, (256, width), 0) == low, 1.0, 0.0).astype(BF16)
    added = lax.dot_general(spread_ref[...], onehot, (((1,), (1,)), ((), ())), preferred_element_type=F32)

    @pl.when(step == 0)
    def _():
        total_ref[...] = added

    @pl.when(step > 0)
    def _():
        total_ref[...] += added

    @pl.when(step == pl.num_programs(0) - 1)
    def _():
        for h in range(16):
            base = h * 2 * nfield
            row = total_ref[base : base + nfield, :] + total_ref[base + nfield : base + 2 * nfield, :]
            flux_ref[:, h, :] = row[:, :128]
            flux_ref[:, h + 16, :] = row[:, 128:]
        depth = depth_ref[...]
        push_ref[0] = flux_ref[0] / depth
        push_ref[1] = flux_ref[1] / depth
        push_ref[2] = flux_ref[2]


def remap(live, picked, weights, cells, depth):
    groups, nfield, width = picked.shape
    blocks = weights.shape[1]
    rows, cols = depth.shape
    return pl.pallas_call(
        remap_kernel,
        grid_spec=pltpu.PrefetchScalarGridSpec(
            num_scalar_prefetch=1,
            grid=(groups,),
            in_specs=[
                pl.BlockSpec((1, nfield, width), lambda c, live: (c, 0, 0)),
                pl.BlockSpec((1, blocks, 256, 256), lambda c, live: (c, 0, 0, 0)),
                pl.BlockSpec((1, 1, width), lambda c, live: (c, 0, 0)),
                pl.BlockSpec((rows, cols), lambda c, live: (0, 0)),
            ],
            out_specs=[
                pl.BlockSpec((nfield, rows, cols), lambda c, live: (0, 0, 0)),
                pl.BlockSpec((3, rows, cols), lambda c, live: (0, 0, 0)),
            ],
            scratch_shapes=[
                pltpu.VMEM((32 * nfield, width), BF16),
                pltpu.VMEM((32 * nfield, 256), F32),
            ],
        ),
        out_shape=[
            jax.ShapeDtypeStruct((nfield, rows, cols), F32),
            jax.ShapeDtypeStruct((3, rows, cols), F32),
        ],
        compiler_params=params(),
    )(live, picked, weights, cells, depth)


def sides(east, west):
    lane = lax.broadcasted_iota(jnp.int32, east.shape, east.ndim - 1)
    return jnp.where(lane < 64, east, west)


def edges_kernel(own_ref, east_ref, west_ref, top_ref, bottom_ref):
    rows = own_ref.shape[1]
    for ref, part in ((top_ref, slice(0, EDGE)), (bottom_ref, slice(rows - EDGE, rows))):
        ref[:, :, :128] = own_ref[:, part, :]
        ref[:, :, 128:] = sides(east_ref[:, part, :], west_ref[:, part, :])


def edge_rows(own, east, west):
    shape = jax.ShapeDtypeStruct((own.shape[0], EDGE, 256), F32)
    return pl.pallas_call(edges_kernel, out_shape=[shape, shape], compiler_params=params())(own, east, west)


def extend(out_ref, at, own, east, west, after, before):
    rows = own.shape[0]
    out_ref[at, :rows, :128] = own
    out_ref[at, :rows, 128:] = sides(east, west)
    out_ref[at, rows : rows + EDGE, :] = after
    out_ref[at, rows + EDGE :, :] = before


def halo(own):
    east, west = neighbours((own, own), ("comp",))
    top, bottom = edge_rows(own, east, west)
    after, before = neighbours((bottom, top), DOM)
    return east, west, after, before


def speed_kernel(depth_ref, wet_ref, level_ref, east_ref, north_ref, state_ref, peak_ref):
    wet = wet_ref[...].astype(F32)
    state_ref[0] = depth_ref[...]
    state_ref[1] = wet
    state_ref[2] = level_ref[...]
    state_ref[3] = east_ref[...]
    state_ref[4] = north_ref[...]
    speed = jnp.sqrt(depth_ref[...]) + wet * (jnp.abs(east_ref[...]) + jnp.abs(north_ref[...]))
    peak_ref[...] = jnp.broadcast_to(jnp.max(speed, keepdims=True), peak_ref.shape)


def static_kernel(own_ref, east_ref, west_ref, after_ref, before_ref, out_ref):
    for at in range(own_ref.shape[0]):
        extend(out_ref, at, own_ref[at], east_ref[at], west_ref[at], after_ref[at], before_ref[at])


def subcycle(first_row, total_rows, depth, wet, level, east, north, push_x, push_y, fresh, peak):
    nrow, ncol = depth.shape
    rows = nrow - 2 * EDGE
    step_dt = courant / peak
    row = lax.broadcasted_iota(jnp.int32, depth.shape, 0)
    row = first_row + jnp.where(row < rows + EDGE, row, row - nrow)
    rotation = 0.1 + 0.4 * (row.astype(F32) + 0.5) / total_rows

    def across(x):
        return pltpu.roll(x, ncol - 1, 1) - pltpu.roll(x, 1, 1)

    def along(x):
        return pltpu.roll(x, nrow - 1, 0) - pltpu.roll(x, 1, 0)

    flux_x = depth * east * wet
    flux_y = depth * north * wet
    diverge = 0.5 * (across(flux_x) + along(flux_y))
    level = wet * (level + step_dt * (fresh - diverge))
    grad_x = 0.5 * across(level)
    grad_y = 0.5 * along(level)
    new_east = wet * (east + step_dt * (rotation * north - grad_x + push_x - friction * east))
    new_north = wet * (north + step_dt * (-rotation * east - grad_y + push_y - friction * north))
    return level, new_east, new_north


def finish(depth, wet, level, east, north, state_ref, peak_ref):
    state_ref[0] = level
    state_ref[1] = east
    state_ref[2] = north
    rows = depth.shape[0] - 2 * EDGE
    own = (slice(0, rows), slice(0, 128))
    speed = jnp.sqrt(depth[own]) + wet[own] * (jnp.abs(east[own]) + jnp.abs(north[own]))
    peak_ref[...] = jnp.broadcast_to(jnp.max(speed, keepdims=True), peak_ref.shape)


def first_kernel(total_rows, row_ref, static_ref, own_ref, east_ref, west_ref, after_ref, before_ref, seen_ref, force_ref, state_ref, peak_ref):
    for at in range(3):
        extend(force_ref, at, own_ref[at], east_ref[at], west_ref[at], after_ref[at], before_ref[at])
    peak = jnp.max(seen_ref[...], keepdims=True)
    depth, wet = static_ref[0], static_ref[1]
    new = subcycle(
        row_ref[0], total_rows, depth, wet, static_ref[2], static_ref[3], static_ref[4],
        force_ref[0], force_ref[1], force_ref[2], peak,
    )
    finish(depth, wet, *new, state_ref, peak_ref)


def middle_kernel(total_rows, row_ref, static_ref, force_ref, old_ref, seen_ref, state_ref, peak_ref):
    peak = jnp.max(seen_ref[...], keepdims=True)
    depth, wet = static_ref[0], static_ref[1]
    new = subcycle(
        row_ref[0], total_rows, depth, wet, old_ref[0], old_ref[1], old_ref[2],
        force_ref[0], force_ref[1], force_ref[2], peak,
    )
    finish(depth, wet, *new, state_ref, peak_ref)


def last_kernel(total_rows, row_ref, static_ref, force_ref, old_ref, seen_ref, out_ref):
    peak = jnp.max(seen_ref[...], keepdims=True)
    new = subcycle(
        row_ref[0], total_rows, static_ref[0], static_ref[1], old_ref[0], old_ref[1], old_ref[2],
        force_ref[0], force_ref[1], force_ref[2], peak,
    )
    rows = out_ref.shape[1]
    for at in range(3):
        out_ref[at] = new[at][:rows, :128]


def call_small(kernel, scalars, arrays, out_shape):
    smem = [pl.BlockSpec(memory_space=pltpu.SMEM)] * len(scalars)
    vmem = [pl.BlockSpec(memory_space=pltpu.VMEM)] * len(arrays)
    return pl.pallas_call(kernel, in_specs=smem + vmem, out_shape=out_shape, compiler_params=params())(*scalars, *arrays)


def largest(peak):
    seen = lax.all_to_all(peak, PLANE, split_axis=0, concat_axis=0, tiled=True)
    second = jnp.broadcast_to(jnp.max(seen, axis=0, keepdims=True), (axes_size(COLUMN), 128))
    return lax.all_to_all(second, COLUMN, split_axis=0, concat_axis=0, tiled=True)


def shards(
    atm_fields,
    send_cols,
    live_blocks,
    remap_weights,
    row_map,
    ocean_depth,
    wet_mask,
    sea_level,
    east_vel,
    north_vel,
):
    groups = send_cols.shape[2]
    rows, cols = ocean_depth.shape
    total_rows = rows * axes_size(DOM)
    first_row = (lax.axis_index(DOM) * rows).reshape(1).astype(jnp.int32)
    peak_shape = jax.ShapeDtypeStruct((axes_size(PLANE), 128), F32)
    wide = (rows + 2 * EDGE, 2 * cols)

    picked = pick(atm_fields, send_cols.reshape(groups, 1, -1))
    own, peak = call_small(
        speed_kernel, (), (ocean_depth, wet_mask, sea_level, east_vel, north_vel),
        [jax.ShapeDtypeStruct((5, rows, cols), F32), peak_shape],
    )
    received = lax.all_to_all(picked, "comp", split_axis=0, concat_axis=0, tiled=True)
    seen = largest(peak)
    static = call_small(static_kernel, (), (own, *halo(own)), jax.ShapeDtypeStruct((5, *wide), F32))
    fluxes, push = remap(live_blocks.reshape(groups), received, remap_weights[0, 0], row_map.reshape(groups, 1, -1), ocean_depth)
    three = jax.ShapeDtypeStruct((3, *wide), F32)
    force, state, peak = call_small(
        functools.partial(first_kernel, total_rows), (first_row,), (static, push, *halo(push), seen), [three, three, peak_shape]
    )
    for _ in range(NSUB - 2):
        seen = largest(peak)
        state, peak = call_small(
            functools.partial(middle_kernel, total_rows), (first_row,), (static, force, state, seen), [three, peak_shape]
        )
    seen = largest(peak)
    state = call_small(
        functools.partial(last_kernel, total_rows), (first_row,), (static, force, state, seen),
        jax.ShapeDtypeStruct((3, rows, cols), F32),
    )
    return fluxes, state


def solution(mesh):
    split = Mesh(mesh.devices.reshape(mesh.shape["comp"], *DOM_SHAPE), COMP_DOM)
    return jax.shard_map(
        shards,
        mesh=split,
        in_specs=(
            P(None, COMP_DOM),
            P("comp", DOM, None, None, None),
            P("comp", DOM, None),
            P("comp", DOM, None, None, None, None),
            P("comp", DOM, None, None, None),
            P(DOM, "comp"),
            P(DOM, "comp"),
            P(DOM, "comp"),
            P(DOM, "comp"),
            P(DOM, "comp"),
        ),
        out_specs=(P(None, DOM, "comp"), P(None, DOM, "comp")),
        check_vma=False,
    )
```

time: 408 us -> 181 us (0.44)
  blocking collectives: 239 us -> 86.6 us
  other arithmetic: 51.7 us -> 0.2 us
  local copies, waits for them, and re-layouts: 34.8 us -> 10.3 us
  Pallas kernels: 0 us -> 15.4 us
  waiting for transfers between devices: 18.8 us -> 4.64 us
  starting transfers between devices: 55.5 us -> 62.2 us
    pmax x16 -> x0, blocking collectives: 239 us -> none  [by_axis(): return functools.reduce(lax.pmax, axes, array)]
    all_to_all x0 -> x6, blocking collectives: none -> 86.6 us  [the longest x3 49.4 us: largest(): lax.all_to_all(second, COLUMN, split_axis=0, concat_axis=0, tiled=True)]
    scatter-add x1 -> x0, other arithmetic: 44.8 us -> none  [deposit(): return total.at[:, targets.reshape(-1)].add(flat)]
    all_to_all x0 -> x2, starting transfers between devices: none -> 29.3 us  [the longest x1 16.7 us: largest(): lax.all_to_all(second, COLUMN, split_axis=0, concat_axis=0, tiled=True)]
    gather x2 -> x0, local copies, waits for them, and re-layouts: 24.8 us -> none  [shards(): picked = jnp.take(atm_fields, columns.reshape(-1), axis=1)]
    ppermute x20 -> x8, starting transfers between devices: 47.8 us -> 25.2 us  [the longest x4 13.2 us: neighbours(): lax.ppermute(array[0], axes, [(i, i + 1) for i in range(count - 1)])]
    ppermute x20 -> x8, waiting for transfers between devices: 18.8 us -> 0.02 us  [the longest x4 0.01 us: neighbours(): after = lax.ppermute(array[1], axes, [(i + 1, i) for i in range(count - 1)])]
    pallas_call x0 -> x10, Pallas kernels: none -> 15.4 us  [the longest x1 8.7 us: remap(): pl.pallas_call(remap_kernel, grid_spec=pltpu.PrefetchScalarGridSpec(num_s...]
  transfers between devices with their start and end apart: 21 -> 11, of which waited for: 5 -> 2; matrix products, arithmetic and copies ran while one was open for 14% -> 1% of each run, Pallas kernels for 0% -> 5%
where the time goes in v1:
time: 181 us; the launch traced here: 180 us
  blocking collectives  86.6 us (48%)
  starting transfers between devices  62.2 us (34%)
  Pallas kernels  15.4 us (9%)
  local copies, waits for them, and re-layouts  10.3 us (6%)
  waiting for transfers between devices  4.64 us (3%)
    all_to_all x3, blocking collectives, largest(): lax.all_to_all(second, COLUMN, split_axis=0, concat_axis=0, tiled=True)  49.4 us
    all_to_all x3, blocking collectives, largest(): seen = lax.all_to_all(peak, PLANE, split_axis=0, concat_axis=0, tiled=True)  37.2 us
    all_to_all x1, starting transfers between devices, largest(): lax.all_to_all(second, COLUMN, split_axis=0, concat_axis=0, tiled=True)  16.7 us
    ppermute x4, starting transfers between devices, neighbours(): lax.ppermute(array[0], axes, [(i, i + 1) for i in range(count - 1)])  13.2 us
    all_to_all x1, starting transfers between devices, largest(): seen = lax.all_to_all(peak, PLANE, split_axis=0, concat_axis=0, tiled=True)  12.5 us
    ppermute x4, starting transfers between devices, neighbours(): after = lax.ppermute(array[1], axes, [(i + 1, i) for i in range(count - 1)])  12 us
    pallas_call x1, Pallas kernels, remap(): pl.pallas_call(remap_kernel, grid_spec=pltpu.PrefetchScalarGridSpec(num_s...  8.7 us
    unnamed x18, local copies, waits for them, and re-layouts  8.03 us
  transfers between devices with their start and end apart: 11, of which 2 were waited for; matrix products, arithmetic and copies ran while one was open for 1% of the time, Pallas kernels for 5%

profile of v1, /device:TPU:1, one launch (start us, length us, event | category | flops | bytes accessed | tf_op | source)
XLA Modules:
  0.0 180.1 jit_solution(8782205871295857717)
XLA Ops:
  0.6 0.8 reshape.49.cols_ref
  1.4 0.0 copy-start.1
  1.4 0.9 copy-done.1
  2.3 4.1 %shard_map.113 = bf16[8,24,1024]{2,1,0:T(8,128)(2,1)} custom-call(bf16[24,2048]{1,0:T(8,128)(2,1)S(1)} %copy-done.1, s32[8,1,1024]{2,1,0:T(1,128)S(1)} %reshape.49.cols_ref), custom_call_target="tpu_custom_call" | custom-call | tf_op jit(solution)/shard_map/pallas_call | solution.py:65
  6.4 7.7 %all-to-all-start = ((bf16[8,24,1024]{2,1,0:T(8,128)(2,1)}), bf16[8,24,1024]{2,1,0:T(8,128)(2,1)S(1)}, u32[]{:S(2)}, u32[]{:S(2)}) async-start(bf16[8,24,1024]{2,1,0:T(8,128)(2,1)} %shard_map.113), calls=%async_computation | async-start | bytes 786432 | tf_op jit(solution)/shard_map/all_to_all | solution.py:309
  14.1 0.7 copy-done.2
  14.8 0.7 copy-done.4
  15.5 0.7 copy-done.5
  16.2 0.7 copy-done.6
  16.9 0.7 copy-done.7
  17.6 0.7 shard_map.115
  18.4 3.4 %collective-permute-start.1 = (f32[5,32,128]{2,1,0:T(8,128)S(1)}, f32[5,32,128]{2,1,0:T(8,128)S(1)}, u32[]{:S(2)}, u32[]{:S(2)}) collective-permute-start(f32[5,32,128]{2,1,0:T(8,128)S(1)} %get-tuple-element.18.own_ref), channel_id=1, source_target_pairs={{0,96},{96,192},{192,288},{288,384},{384,480},{480,576},{576,672},... | collective-permute-start | bytes 245768 | tf_op jit(solution)/shard_map/ppermute | solution.py:37
  21.7 1.3 collective-permute-start
  23.0 0.8 reshape.50.cells_ref
  23.8 1.0 all-to-all-done.picked_ref
  24.8 2.2 %copy-done = bf16[1,1,8,4,256,256]{5,4,3,2,1,0:T(8,128)(2,1)S(1)} copy-done((bf16[1,1,8,4,256,256]{5,4,3,2,1,0:T(8,128)(2,1)S(1)}, bf16[1,1,8,4,256,256]{5,4,3,2,1,0:T(8,128)(2,1)}, u32[]{:S(2)}) %copy-start) | copy-done | bytes 4194328
  27.0 0.7 copy-done.3
  27.7 0.7 copy-done.8
  28.4 8.7 %shard_map.114 = (f32[24,32,128]{2,1,0:T(8,128)}, f32[3,32,128]{2,1,0:T(8,128)S(1)}) custom-call(s32[8]{0:T(128)S(1)} %bitcast.27, bf16[8,24,1024]{2,1,0:T(8,128)(2,1)S(1)} %all-to-all-done.picked_ref, bf16[8,4,256,256]{3,2,1,0:T(8,128)(2,1)S(1)} %bitcast.19, s32[8,1,1024]{2,1,0:T(1,128)S(1)} %reshape.50.cells_ref, f32[32,128]{1,0:T(8,128)S(1)} %copy-done.3), custom_call_target="tpu_custom_call" | custom-call | tf_op jit(solution)/shard_map/pallas_call | solution.py:129
  37.1 3.0 %collective-permute-start.5 = (f32[3,32,128]{2,1,0:T(8,128)S(1)}, f32[3,32,128]{2,1,0:T(8,128)S(1)}, u32[]{:S(2)}, u32[]{:S(2)}) collective-permute-start(f32[3,32,128]{2,1,0:T(8,128)S(1)} %get-tuple-element.21.own_ref), channel_id=1, source_target_pairs={{0,96},{96,192},{192,288},{288,384},{384,480},{480,576},{576,672},... | collective-permute-start | bytes 147464 | tf_op jit(solution)/shard_map/ppermute | solution.py:37
  40.1 1.3 collective-permute-start.4
  41.4 12.5 %all-to-all-start.1 = ((f32[32,1,128]{2,1,0:T(1,128)}), f32[32,1,128]{2,1,0:T(1,128)S(1)}, u32[]{:S(2)}, u32[]{:S(2)}) async-start(f32[32,1,128]{2,1,0:T(1,128)} %bitcast.4), calls=%async_computation.1 | async-start | bytes 32768 | tf_op jit(solution)/shard_map/all_to_all | solution.py:280
  54.0 0.0 collective-permute-done.east_ref
  54.0 7.4 %collective-permute-start.2 = (f32[5,8,256]{2,1,0:T(8,128)S(1)}, f32[5,8,256]{2,1,0:T(8,128)S(1)}, u32[]{:S(2)}, u32[]{:S(2)}) collective-permute-start(f32[5,8,256]{2,1,0:T(8,128)S(1)} %get-tuple-element.19), channel_id=1, source_target_pairs={{1,0},{2,1},{3,2},{4,3},{5,4},{6,5},{7,6},{8,7},{9,8},{10,9},{11,1... | collective-permute-start | bytes 122888 | tf_op jit(solution)/shard_map/ppermute | solution.py:36
  61.4 3.3 %collective-permute-start.3 = (f32[5,8,256]{2,1,0:T(8,128)S(1)}, f32[5,8,256]{2,1,0:T(8,128)S(1)}, u32[]{:S(2)}, u32[]{:S(2)}) collective-permute-start(f32[5,8,256]{2,1,0:T(8,128)S(1)} %get-tuple-element.20), channel_id=1, source_target_pairs={{0,1},{1,2},{2,3},{3,4},{4,5},{5,6},{6,7},{7,8},{8,9},{9,10},{10,1... | collective-permute-start | bytes 122888 | tf_op jit(solution)/shard_map/ppermute | solution.py:37
  64.7 0.0 all-to-all-done.1
  64.7 0.1 reduce_max.36
  64.8 0.6 broadcast_in_dim.8
  65.4 16.7 %all-to-all-start.2 = ((f32[24,1,128]{2,1,0:T(1,128)}), f32[24,1,128]{2,1,0:T(1,128)S(1)}, u32[]{:S(2)}, u32[]{:S(2)}) async-start(f32[24,1,128]{2,1,0:T(1,128)} %broadcast_in_dim.8), calls=%async_computation.2 | async-start | bytes 24576 | tf_op jit(solution)/shard_map/all_to_all | solution.py:282
  82.1 0.0 collective-permute-done.5.west_ref
  82.2 2.1 %collective-permute-start.6 = (f32[3,8,256]{2,1,0:T(8,128)S(1)}, f32[3,8,256]{2,1,0:T(8,128)S(1)}, u32[]{:S(2)}, u32[]{:S(2)}) collective-permute-start(f32[3,8,256]{2,1,0:T(8,128)S(1)} %get-tuple-element.22), channel_id=1, source_target_pairs={{1,0},{2,1},{3,2},{4,3},{5,4},{6,5},{7,6},{8,7},{9,8},{10,9},{11,1... | collective-permute-start | bytes 73736 | tf_op jit(solution)/shard_map/ppermute | solution.py:36
  84.3 3.5 %collective-permute-start.7 = (f32[3,8,256]{2,1,0:T(8,128)S(1)}, f32[3,8,256]{2,1,0:T(8,128)S(1)}, u32[]{:S(2)}, u32[]{:S(2)}) collective-permute-start(f32[3,8,256]{2,1,0:T(8,128)S(1)} %get-tuple-element.23), channel_id=1, source_target_pairs={{0,1},{1,2},{2,3},{3,4},{4,5},{5,6},{6,7},{7,8},{8,9},{9,10},{10,1... | collective-permute-start | bytes 73736 | tf_op jit(solution)/shard_map/ppermute | solution.py:37
  87.8 0.0 collective-permute-done.2.after_ref
  87.8 0.0 collective-permute-done.3.before_ref
  87.8 3.7 %all-to-all-done.2 = f32[24,1,128]{2,1,0:T(1,128)S(1)} async-done(((f32[24,1,128]{2,1,0:T(1,128)}), f32[24,1,128]{2,1,0:T(1,128)S(1)}, u32[]{:S(2)}, u32[]{:S(2)}) %all-to-all-start.2) | async-done | bytes 12320 | tf_op jit(solution)/shard_map/all_to_all | solution.py:282
  91.5 0.3 shard_map.119
  91.8 14.1 %all_to_all.73 = f32[32,1,128]{2,1,0:T(1,128)S(1)} all-to-all(f32[32,1,128]{2,1,0:T(1,128)S(1)} %bitcast.24), channel_id=1, replica_groups=mesh['comp'=8,'dom_0'=12,'dom_1'=4,'dom_2'=2] {'comp','dom_1'}, dimensions={0} | all-to-all | bytes 32768 | tf_op jit(solution)/shard_map/all_to_all | solution.py:280
  105.9 0.1 reduce_max.37
  106.0 21.4 %all_to_all.74 = f32[24,1,128]{2,1,0:T(1,128)S(1)} all-to-all(f32[24,1,128]{2,1,0:T(1,128)S(1)} %broadcast_in_dim.9), channel_id=1, replica_groups=mesh['comp'=8,'dom_0'=12,'dom_1'=4,'dom_2'=2] {'dom_0','dom_2'}, dimensions={0} | all-to-all | bytes 24576 | tf_op jit(solution)/shard_map/all_to_all | solution.py:282
  127.4 0.3 shard_map.120
  127.7 11.6 %all_to_all.75 = f32[32,1,128]{2,1,0:T(1,128)S(1)} all-to-all(f32[32,1,128]{2,1,0:T(1,128)S(1)} %bitcast.25), channel_id=1, replica_groups=mesh['comp'=8,'dom_0'=12,'dom_1'=4,'dom_2'=2] {'comp','dom_1'}, dimensions={0} | all-to-all | bytes 32768 | tf_op jit(solution)/shard_map/all_to_all | solution.py:280
  139.3 0.1 reduce_max.38
  139.4 14.0 %all_to_all.76 = f32[24,1,128]{2,1,0:T(1,128)S(1)} all-to-all(f32[24,1,128]{2,1,0:T(1,128)S(1)} %broadcast_in_dim.10), channel_id=1, replica_groups=mesh['comp'=8,'dom_0'=12,'dom_1'=4,'dom_2'=2] {'dom_0','dom_2'}, dimensions={0} | all-to-all | bytes 24576 | tf_op jit(solution)/shard_map/all_to_all | solution.py:282
  153.4 0.3 shard_map.121
  153.7 11.6 %all_to_all.77 = f32[32,1,128]{2,1,0:T(1,128)S(1)} all-to-all(f32[32,1,128]{2,1,0:T(1,128)S(1)} %bitcast.26), channel_id=1, replica_groups=mesh['comp'=8,'dom_0'=12,'dom_1'=4,'dom_2'=2] {'comp','dom_1'}, dimensions={0} | all-to-all | bytes 32768 | tf_op jit(solution)/shard_map/all_to_all | solution.py:280
  165.3 0.1 reduce_max.39
  165.3 14.0 %all_to_all.78 = f32[24,1,128]{2,1,0:T(1,128)S(1)} all-to-all(f32[24,1,128]{2,1,0:T(1,128)S(1)} %broadcast_in_dim.11), channel_id=1, replica_groups=mesh['comp'=8,'dom_0'=12,'dom_1'=4,'dom_2'=2] {'dom_0','dom_2'}, dimensions={0} | all-to-all | bytes 24576 | tf_op jit(solution)/shard_map/all_to_all | solution.py:282
  179.3 0.8 shard_map.122
  (18 shorter events, 0.1 us)
Async XLA Ops:
  1.4 0.9 copy-start.1
  6.4 18.4 %all-to-all-start = ((bf16[8,24,1024]{2,1,0:T(8,128)(2,1)}), bf16[8,24,1024]{2,1,0:T(8,128)(2,1)S(1)}, u32[]{:S(2)}, u32[]{:S(2)}) async-start(bf16[8,24,1024]{2,1,0:T(8,128)(2,1)} %shard_map.113), calls=%async_computation | async-start | bytes 786432 | tf_op jit(solution)/shard_map/all_to_all | solution.py:309
  14.1 0.7 copy-start.2
  14.8 0.7 copy-start.4
  15.5 0.7 copy-start.5
  16.2 0.7 copy-start.6
  16.9 0.7 copy-start.7
  18.4 35.6 %collective-permute-start.1 = (f32[5,32,128]{2,1,0:T(8,128)S(1)}, f32[5,32,128]{2,1,0:T(8,128)S(1)}, u32[]{:S(2)}, u32[]{:S(2)}) collective-permute-start(f32[5,32,128]{2,1,0:T(8,128)S(1)} %get-tuple-element.18.own_ref), channel_id=1, source_target_pairs={{0,96},{96,192},{192,288},{288,384},{384,480},{480,576},{576,672},... | collective-permute-start | bytes 245768 | tf_op jit(solution)/shard_map/ppermute | solution.py:37
  21.7 32.2 %collective-permute-start = (f32[5,32,128]{2,1,0:T(8,128)S(1)}, f32[5,32,128]{2,1,0:T(8,128)S(1)}, u32[]{:S(2)}, u32[]{:S(2)}) collective-permute-start(f32[5,32,128]{2,1,0:T(8,128)S(1)} %get-tuple-element.18.own_ref), channel_id=1, source_target_pairs={{96,0},{192,96},{288,192},{384,288},{480,384},{576,480},{672,576},... | collective-permute-start | bytes 245768 | tf_op jit(solution)/shard_map/ppermute | solution.py:36
  24.8 2.2 %copy-start = (bf16[1,1,8,4,256,256]{5,4,3,2,1,0:T(8,128)(2,1)S(1)}, bf16[1,1,8,4,256,256]{5,4,3,2,1,0:T(8,128)(2,1)}, u32[]{:S(2)}) copy-start(bf16[1,1,8,4,256,256]{5,4,3,2,1,0:T(8,128)(2,1)} %param.13) | copy-start | bytes 12582916
  27.0 0.7 copy-start.3
  27.7 0.7 copy-start.8
  37.1 45.1 %collective-permute-start.5 = (f32[3,32,128]{2,1,0:T(8,128)S(1)}, f32[3,32,128]{2,1,0:T(8,128)S(1)}, u32[]{:S(2)}, u32[]{:S(2)}) collective-permute-start(f32[3,32,128]{2,1,0:T(8,128)S(1)} %get-tuple-element.21.own_ref), channel_id=1, source_target_pairs={{0,96},{96,192},{192,288},{288,384},{384,480},{480,576},{576,672},... | collective-permute-start | bytes 147464 | tf_op jit(solution)/shard_map/ppermute | solution.py:37
  40.1 42.0 %collective-permute-start.4 = (f32[3,32,128]{2,1,0:T(8,128)S(1)}, f32[3,32,128]{2,1,0:T(8,128)S(1)}, u32[]{:S(2)}, u32[]{:S(2)}) collective-permute-start(f32[3,32,128]{2,1,0:T(8,128)S(1)} %get-tuple-element.21.own_ref), channel_id=1, source_target_pairs={{96,0},{192,96},{288,192},{384,288},{480,384},{576,480},{672,576},... | collective-permute-start | bytes 147464 | tf_op jit(solution)/shard_map/ppermute | solution.py:36
  41.4 23.3 %all-to-all-start.1 = ((f32[32,1,128]{2,1,0:T(1,128)}), f32[32,1,128]{2,1,0:T(1,128)S(1)}, u32[]{:S(2)}, u32[]{:S(2)}) async-start(f32[32,1,128]{2,1,0:T(1,128)} %bitcast.4), calls=%async_computation.1 | async-start | bytes 32768 | tf_op jit(solution)/shard_map/all_to_all | solution.py:280
  54.0 33.7 %collective-permute-start.2 = (f32[5,8,256]{2,1,0:T(8,128)S(1)}, f32[5,8,256]{2,1,0:T(8,128)S(1)}, u32[]{:S(2)}, u32[]{:S(2)}) collective-permute-start(f32[5,8,256]{2,1,0:T(8,128)S(1)} %get-tuple-element.19), channel_id=1, source_target_pairs={{1,0},{2,1},{3,2},{4,3},{5,4},{6,5},{7,6},{8,7},{9,8},{10,9},{11,1... | collective-permute-start | bytes 122888 | tf_op jit(solution)/shard_map/ppermute | solution.py:36
  61.4 26.4 %collective-permute-start.3 = (f32[5,8,256]{2,1,0:T(8,128)S(1)}, f32[5,8,256]{2,1,0:T(8,128)S(1)}, u32[]{:S(2)}, u32[]{:S(2)}) collective-permute-start(f32[5,8,256]{2,1,0:T(8,128)S(1)} %get-tuple-element.20), channel_id=1, source_target_pairs={{0,1},{1,2},{2,3},{3,4},{4,5},{5,6},{6,7},{7,8},{8,9},{9,10},{10,1... | collective-permute-start | bytes 122888 | tf_op jit(solution)/shard_map/ppermute | solution.py:37
  65.4 26.1 %all-to-all-start.2 = ((f32[24,1,128]{2,1,0:T(1,128)}), f32[24,1,128]{2,1,0:T(1,128)S(1)}, u32[]{:S(2)}, u32[]{:S(2)}) async-start(f32[24,1,128]{2,1,0:T(1,128)} %broadcast_in_dim.8), calls=%async_computation.2 | async-start | bytes 24576 | tf_op jit(solution)/shard_map/all_to_all | solution.py:282
  82.2 9.3 %collective-permute-start.6 = (f32[3,8,256]{2,1,0:T(8,128)S(1)}, f32[3,8,256]{2,1,0:T(8,128)S(1)}, u32[]{:S(2)}, u32[]{:S(2)}) collective-permute-start(f32[3,8,256]{2,1,0:T(8,128)S(1)} %get-tuple-element.22), channel_id=1, source_target_pairs={{1,0},{2,1},{3,2},{4,3},{5,4},{6,5},{7,6},{8,7},{9,8},{10,9},{11,1... | collective-permute-start | bytes 73736 | tf_op jit(solution)/shard_map/ppermute | solution.py:36
  84.3 7.2 %collective-permute-start.7 = (f32[3,8,256]{2,1,0:T(8,128)S(1)}, f32[3,8,256]{2,1,0:T(8,128)S(1)}, u32[]{:S(2)}, u32[]{:S(2)}) collective-permute-start(f32[3,8,256]{2,1,0:T(8,128)S(1)} %get-tuple-element.23), channel_id=1, source_target_pairs={{0,1},{1,2},{2,3},{3,4},{4,5},{5,6},{6,7},{7,8},{8,9},{9,10},{10,1... | collective-permute-start | bytes 73736 | tf_op jit(solution)/shard_map/ppermute | solution.py:37

commit v2 on v0

v2 whole, which is shorter than its diff:
```python
import functools

import jax
import jax.numpy as jnp
from jax import lax
from jax.experimental import pallas as pl
from jax.experimental.pallas import tpu as pltpu
from jax.sharding import Mesh
from jax.sharding import PartitionSpec as P

NSUB = 4
DOM_SHAPE = (12, 4, 2)
COMP_DOM = ("comp", "dom_0", "dom_1", "dom_2")
DOM = ("dom_0", "dom_1", "dom_2")
PLANE = ("comp", "dom_1")
COLUMN = ("dom_0", "dom_2")
BF16 = jnp.bfloat16
F32 = jnp.float32

courant = 0.5
friction = 0.05

EDGE = 8
KEPT = 8
HIGH = 8
NT = (((1,), (1,)), ((), ()))
HBM = pl.BlockSpec(memory_space=pltpu.HBM)
SMEM = pl.BlockSpec(memory_space=pltpu.SMEM)
VMEM = pl.BlockSpec(memory_space=pltpu.VMEM)


def params(mib):
    return pltpu.CompilerParams(vmem_limit_bytes=mib * 1024 * 1024)


def axes_size(axes):
    return functools.reduce(lambda a, b: a * b, [lax.axis_size(a) for a in axes])


def neighbours(head, tail, axes):
    count = axes_size(axes)
    after = lax.ppermute(head, axes, [(i + 1, i) for i in range(count - 1)])
    before = lax.ppermute(tail, axes, [(i, i + 1) for i in range(count - 1)])
    return after, before


def fetch(refs, buffers, sems, first=0):
    copies = [pltpu.make_async_copy(ref, buf, sems.at[first + i]) for i, (ref, buf) in enumerate(zip(refs, buffers))]
    for copy in copies:
        copy.start()
    return copies


def rows16(row, count):
    tile = jnp.broadcast_to(row.astype(F32), (16, row.shape[1])).astype(BF16)
    return jnp.concatenate([tile] * (count // 16), axis=0)


def onehot(row, count):
    at = lax.broadcasted_iota(jnp.int32, (count, row.shape[1]), 0).astype(F32).astype(BF16)
    return jnp.where(at == rows16(row, count), jnp.ones_like(at), jnp.zeros_like(at))


def pick_kernel(fields_hbm, cols_hbm, out_ref, fields_ref, cols_ref, sems):
    for copy in fetch((fields_hbm, cols_hbm), (fields_ref, cols_ref), sems):
        copy.wait()
    nfield, ncol = fields_ref.shape
    high = ncol // 256
    rows = [fields_ref[:, h * 256 : (h + 1) * 256].astype(F32) for h in range(high)]
    table = jnp.concatenate(rows, axis=0).astype(BF16)
    groups, blocks, width = cols_ref.shape[2:]
    for c in range(groups):
        for k in range(blocks):
            cols = cols_ref[0, 0, c, k : k + 1, :]
            both = jnp.dot(table, onehot(cols & 255, 256), preferred_element_type=F32)
            upper = jnp.broadcast_to(cols >> 8, (nfield, width))
            picked = both[:nfield]
            for h in range(1, high):
                picked = jnp.where(upper == h, both[h * nfield : (h + 1) * nfield], picked)
            out_ref[c, :, k * width : (k + 1) * width] = picked.astype(BF16)


def pick(fields, cols):
    groups, blocks, width = cols.shape[2:]
    return pl.pallas_call(
        pick_kernel,
        grid=(1,),
        in_specs=[HBM, HBM],
        out_specs=pl.BlockSpec((groups, fields.shape[0], blocks * width), lambda i: (0, 0, 0)),
        out_shape=jax.ShapeDtypeStruct((groups, fields.shape[0], blocks * width + 128), BF16),
        scratch_shapes=[
            pltpu.VMEM(fields.shape, BF16),
            pltpu.VMEM(cols.shape, jnp.int32),
            pltpu.SemaphoreType.DMA((2,)),
        ],
        compiler_params=params(56),
    )(fields, cols)


def peak_of(depth, wet, east, north):
    return jnp.max(jnp.sqrt(depth) + wet * (jnp.abs(east) + jnp.abs(north)), keepdims=True)


def speed_kernel(depth_hbm, wet_hbm, east_hbm, north_hbm, peak_ref, real_ref, wet_ref, sems):
    copies = fetch(
        (depth_hbm, east_hbm, north_hbm, wet_hbm), (real_ref.at[0], real_ref.at[1], real_ref.at[2], wet_ref), sems
    )
    for copy in copies:
        copy.wait()
    peak = peak_of(real_ref[0], wet_ref[...].astype(F32), real_ref[1], real_ref[2])
    peak_ref[...] = jnp.broadcast_to(peak, peak_ref.shape)


def first_speed(depth, wet, east, north):
    return pl.pallas_call(
        speed_kernel,
        in_specs=[HBM] * 4,
        out_specs=VMEM,
        out_shape=jax.ShapeDtypeStruct((axes_size(DOM), 128), F32),
        scratch_shapes=[
            pltpu.VMEM((3, *depth.shape), F32),
            pltpu.VMEM(depth.shape, jnp.int32),
            pltpu.SemaphoreType.DMA((4,)),
        ],
        compiler_params=params(56),
    )(depth, wet, east, north)


def exchange(peak, axes):
    return lax.all_to_all(peak, axes, split_axis=0, concat_axis=0, tiled=True)


def insert_kernel(seen_ref, picked_ref, out_ref):
    peak = jnp.broadcast_to(jnp.max(seen_ref[...], keepdims=True), (1, 128))
    big = peak.astype(BF16).astype(F32)
    middle = (peak - big).astype(BF16).astype(F32)
    row = lax.broadcasted_iota(jnp.int32, out_ref.shape[1:], 0)
    three = jnp.where(row == 0, big, jnp.where(row == 1, middle, jnp.where(row == 2, peak - big - middle, 0.0)))
    for c in range(out_ref.shape[0]):
        out_ref[c] = three.astype(BF16)


def insert(seen, picked):
    groups, nfield, width = picked.shape
    return pl.pallas_call(
        insert_kernel,
        grid=(1,),
        in_specs=[pl.BlockSpec(seen.shape, lambda i: (0, 0)), HBM],
        out_specs=pl.BlockSpec((groups, nfield, 128), lambda i: (0, 0, width // 128 - 1)),
        out_shape=jax.ShapeDtypeStruct(picked.shape, picked.dtype),
        input_output_aliases={1: 0},
        compiler_params=params(56),
    )(seen, picked)


def spread_max(seen, axes):
    return jnp.broadcast_to(jnp.max(seen, axis=0, keepdims=True), (axes_size(axes), 128))


def remap_kernel(
    live_ref, picked_hbm, weights_hbm, cells_hbm, depth_hbm, wet_hbm, level_hbm, east_hbm, north_hbm,
    flux_ref, own_ref, head_ref, tail_ref, peak_ref,
    picked_ref, weights_ref, cells_ref, wet_ref, spread_ref, total_ref, sems,
):
    groups, nfield, width = picked_ref.shape
    blocks = weights_ref.shape[1]
    pair_rows = 2 * nfield
    lows = total_ref.shape[1]
    first = fetch((picked_hbm, cells_hbm), (picked_ref, cells_ref), sems)
    loads = fetch([weights_hbm.at[0, 0, c] for c in range(groups)], [weights_ref.at[c] for c in range(groups)], sems, 2)
    rest = fetch(
        (depth_hbm, level_hbm, east_hbm, north_hbm, wet_hbm),
        (own_ref.at[0], own_ref.at[2], own_ref.at[3], own_ref.at[4], wet_ref),
        sems,
        2 + groups,
    )
    for copy in first:
        copy.wait()
    peak = None
    for c in range(groups):
        three = picked_ref[c, :, blocks * 256 :].astype(F32)
        one = three[0:1] + (three[1:2] + three[2:3])
        peak = one if peak is None else jnp.maximum(peak, one)
    peak_ref[...] = jnp.broadcast_to(peak, peak_ref.shape)
    for c in range(groups):
        loads[c].wait()
        live = live_ref[0, 0, c]
        onehots = []
        for k in range(blocks):
            part = slice(k * 256, (k + 1) * 256)
            contrib = lax.dot_general(picked_ref[c, :, part], weights_ref[c, k], NT, preferred_element_type=F32)
            big = contrib.astype(BF16).astype(F32)
            pair = jnp.concatenate([big, contrib - big], axis=0).astype(BF16)
            cell = cells_ref[0, 0, c, k : k + 1, :]
            upper = rows16(jnp.where(jnp.int32(k) < live, (cell >> 7) & (HIGH - 1), -1), pair_rows)
            for h in range(HIGH):
                spread_ref[h * pair_rows : (h + 1) * pair_rows, part] = jnp.where(
                    upper == BF16(h), pair, jnp.zeros_like(pair)
                )
            row, column = cell >> 7, cell & 127
            low = (row // HIGH) * 128 + column
            tiles = [onehot(jnp.where(low >> 8 == t, low & 255, -1), 256) for t in range(lows // 256)]
            onehots.append(jnp.concatenate(tiles, axis=0))
        added = lax.dot_general(
            spread_ref[...], jnp.concatenate(onehots, axis=1), NT, preferred_element_type=F32
        )
        if c == 0:
            total_ref[...] = added
        else:
            total_ref[...] += added
    for h in range(HIGH):
        base = h * pair_rows
        both = total_ref[base : base + nfield, :] + total_ref[base + nfield : base + pair_rows, :]
        for r in range(lows // 128):
            flux_ref[:, r * HIGH + h, :] = both[:, r * 128 : (r + 1) * 128]
    for copy in rest:
        copy.wait()
    own_ref[1] = wet_ref[...].astype(F32)
    own_ref[5] = flux_ref[0] / own_ref[0]
    own_ref[6] = flux_ref[1] / own_ref[0]
    own_ref[7] = flux_ref[2]
    lane = lax.broadcasted_iota(jnp.int32, head_ref.shape, 1)
    head = own_ref[0]
    tail = pltpu.roll(own_ref[0], EDGE, 1)
    for at in range(1, KEPT):
        here = lane // EDGE == at
        head = jnp.where(here, pltpu.roll(own_ref[at], at * EDGE, 1), head)
        tail = jnp.where(here, pltpu.roll(own_ref[at], (at + 1) * EDGE, 1), tail)
    head_ref[...] = head
    tail_ref[...] = tail


def remap(live, picked, weights, cells, depth, wet, level, east, north):
    groups, nfield, width = picked.shape
    rows, cols = depth.shape
    tile = jax.ShapeDtypeStruct((rows, cols), F32)
    return pl.pallas_call(
        remap_kernel,
        in_specs=[SMEM] + [HBM] * 8,
        out_specs=[VMEM] * 5,
        out_shape=[
            jax.ShapeDtypeStruct((nfield, rows, cols), F32),
            jax.ShapeDtypeStruct((KEPT, rows, cols), F32),
            tile,
            tile,
            jax.ShapeDtypeStruct((8, 128), F32),
        ],
        scratch_shapes=[
            pltpu.VMEM(picked.shape, BF16),
            pltpu.VMEM(weights.shape[2:], BF16),
            pltpu.VMEM(cells.shape, jnp.int32),
            pltpu.VMEM((rows, cols), jnp.int32),
            pltpu.VMEM((HIGH * 2 * nfield, cells.shape[3] * cells.shape[4]), BF16),
            pltpu.VMEM((HIGH * 2 * nfield, rows // HIGH * cols), F32),
            pltpu.SemaphoreType.DMA((groups + 7,)),
        ],
        compiler_params=params(56),
    )(live, picked, weights, cells, depth, wet, level, east, north)


def edges_kernel(own_ref, east_ref, west_ref, top_ref, bottom_ref):
    rows = own_ref.shape[1]
    for ref, part in ((top_ref, slice(0, EDGE)), (bottom_ref, slice(rows - EDGE, rows))):
        ref[:KEPT] = own_ref[:, part, :]
        ref[KEPT] = east_ref[part, :]
        ref[KEPT + 1] = west_ref[part, :]


def beside(at, east, west):
    lane = lax.broadcasted_iota(jnp.int32, east.shape, 1)
    return jnp.where(
        lane < 64,
        pltpu.roll(east, (128 - at * EDGE) % 128, 1),
        pltpu.roll(west, (128 - EDGE - at * EDGE) % 128, 1),
    )


def extended(at, own_ref, east_ref, west_ref, after_ref, before_ref):
    left = jnp.concatenate([own_ref[at], after_ref[at], before_ref[at]], axis=0)
    right = [beside(at, east_ref[...], west_ref[...])]
    right += [beside(at, ref[KEPT], ref[KEPT + 1]) for ref in (after_ref, before_ref)]
    return jnp.concatenate([left, jnp.concatenate(right, axis=0)], axis=1)


def subcycle(first_row, total_rows, depth, wet, level, east, north, push_x, push_y, fresh, peak):
    nrow, ncol = depth.shape
    rows = nrow - 2 * EDGE
    step_dt = courant / peak
    row = lax.broadcasted_iota(jnp.int32, depth.shape, 0)
    row = first_row + jnp.where(row < rows + EDGE, row, row - nrow)
    rotation = 0.1 + 0.4 * (row.astype(F32) + 0.5) / total_rows

    def across(x):
        return pltpu.roll(x, ncol - 1, 1) - pltpu.roll(x, 1, 1)

    def along(x):
        return pltpu.roll(x, nrow - 1, 0) - pltpu.roll(x, 1, 0)

    flux_x = depth * east * wet
    flux_y = depth * north * wet
    diverge = 0.5 * (across(flux_x) + along(flux_y))
    level = wet * (level + step_dt * (fresh - diverge))
    grad_x = 0.5 * across(level)
    grad_y = 0.5 * along(level)
    new_east = wet * (east + step_dt * (rotation * north - grad_x + push_x - friction * east))
    new_north = wet * (north + step_dt * (-rotation * east - grad_y + push_y - friction * north))
    return level, new_east, new_north


def finish(depth, wet, new, state_ref, peak_ref):
    for at in range(3):
        state_ref[at] = new[at]
    own = (slice(0, depth.shape[0] - 2 * EDGE), slice(0, 128))
    peak = peak_of(depth[own], wet[own], new[1][own], new[2][own])
    peak_ref[...] = jnp.broadcast_to(peak, peak_ref.shape)


def first_kernel(
    total_rows, row_ref, own_ref, east_ref, west_ref, after_ref, before_ref, seen_ref, kept_ref, state_ref, peak_ref
):
    full = [extended(at, own_ref, east_ref, west_ref, after_ref, before_ref) for at in range(KEPT)]
    depth, wet, level, east, north, push_x, push_y, fresh = full
    for at, array in enumerate((depth, wet, push_x, push_y, fresh)):
        kept_ref[at] = array
    peak = jnp.max(seen_ref[...], keepdims=True)
    finish(depth, wet, subcycle(row_ref[0], total_rows, *full, peak), state_ref, peak_ref)


def next_state(total_rows, row_ref, kept_ref, old_ref, seen_ref):
    peak = jnp.max(seen_ref[...], keepdims=True)
    return subcycle(
        row_ref[0], total_rows, kept_ref[0], kept_ref[1], old_ref[0], old_ref[1], old_ref[2],
        kept_ref[2], kept_ref[3], kept_ref[4], peak,
    )


def middle_kernel(total_rows, row_ref, kept_ref, old_ref, seen_ref, state_ref, peak_ref):
    new = next_state(total_rows, row_ref, kept_ref, old_ref, seen_ref)
    finish(kept_ref[0], kept_ref[1], new, state_ref, peak_ref)


def last_kernel(total_rows, row_ref, kept_ref, old_ref, seen_ref, out_ref):
    new = next_state(total_rows, row_ref, kept_ref, old_ref, seen_ref)
    for at in range(3):
        out_ref[at] = new[at][: out_ref.shape[1], :128]


def call_small(kernel, scalars, arrays, out_shape):
    return pl.pallas_call(
        kernel, in_specs=[SMEM] * len(scalars) + [VMEM] * len(arrays), out_shape=out_shape, compiler_params=params(8)
    )(*scalars, *arrays)


def shards(
    atm_fields,
    send_cols,
    live_blocks,
    remap_weights,
    row_map,
    ocean_depth,
    wet_mask,
    sea_level,
    east_vel,
    north_vel,
):
    rows, cols = ocean_depth.shape
    total_rows = rows * axes_size(DOM)
    first_row = (lax.axis_index(DOM) * rows).reshape(1).astype(jnp.int32)
    wide = (rows + 2 * EDGE, 2 * cols)
    three = jax.ShapeDtypeStruct((3, *wide), F32)
    five = jax.ShapeDtypeStruct((5, *wide), F32)
    rim = jax.ShapeDtypeStruct((KEPT + 2, EDGE, cols), F32)
    peak_shape = jax.ShapeDtypeStruct((axes_size(PLANE), 128), F32)

    seen = exchange(first_speed(ocean_depth, wet_mask, east_vel, north_vel), DOM)
    picked = pick(atm_fields, send_cols)
    picked = insert(seen, picked)
    received = lax.all_to_all(picked, "comp", split_axis=0, concat_axis=0, tiled=True)
    fluxes, own, head, tail, seen = remap(
        live_blocks, received, remap_weights, row_map, ocean_depth, wet_mask, sea_level, east_vel, north_vel
    )
    east, west = neighbours(head, tail, ("comp",))
    top, bottom = call_small(edges_kernel, (), (own, east, west), [rim, rim])
    after, before = neighbours(top, bottom, DOM)
    kept, state, peak = call_small(
        functools.partial(first_kernel, total_rows),
        (first_row,),
        (own, east, west, after, before, seen),
        [five, three, peak_shape],
    )
    for substep in range(1, NSUB):
        seen = exchange(spread_max(exchange(peak, PLANE), COLUMN), COLUMN)
        if substep < NSUB - 1:
            state, peak = call_small(
                functools.partial(middle_kernel, total_rows), (first_row,), (kept, state, seen), [three, peak_shape]
            )
    state = call_small(
        functools.partial(last_kernel, total_rows), (first_row,), (kept, state, seen),
        jax.ShapeDtypeStruct((3, rows, cols), F32),
    )
    return fluxes, state


def solution(mesh):
    split = Mesh(mesh.devices.reshape(mesh.shape["comp"], *DOM_SHAPE), COMP_DOM)
    return jax.shard_map(
        shards,
        mesh=split,
        in_specs=(
            P(None, COMP_DOM),
            P("comp", DOM, None, None, None),
            P("comp", DOM, None),
            P("comp", DOM, None, None, None, None),
            P("comp", DOM, None, None, None),
            P(DOM, "comp"),
            P(DOM, "comp"),
            P(DOM, "comp"),
            P(DOM, "comp"),
            P(DOM, "comp"),
        ),
        out_specs=(P(None, DOM, "comp"), P(None, DOM, "comp")),
        check_vma=False,
    )
```

time: 408 us -> 171 us (0.42)
  blocking collectives: 239 us -> 106 us
  other arithmetic: 51.7 us -> 0.15 us
  local copies, waits for them, and re-layouts: 34.8 us -> 3.14 us
  starting transfers between devices: 55.5 us -> 32.1 us
  Pallas kernels: 0 us -> 15.9 us
  waiting for transfers between devices: 18.8 us -> 11.7 us
    pmax x16 -> x0, blocking collectives: 239 us -> none  [by_axis(): return functools.reduce(lax.pmax, axes, array)]
    all_to_all x0 -> x7, blocking collectives: none -> 106 us  [the longest x6 84.2 us: exchange(): return lax.all_to_all(peak, axes, split_axis=0, concat_axis=0, tiled=True)]
    scatter-add x1 -> x0, other arithmetic: 44.8 us -> none  [deposit(): return total.at[:, targets.reshape(-1)].add(flat)]
    ppermute x20 -> x4, starting transfers between devices: 47.8 us -> 12 us  [the longest x2 6.08 us: neighbours(): before = lax.ppermute(tail, axes, [(i, i + 1) for i in range(count - 1)])]
    gather x2 -> x0, local copies, waits for them, and re-layouts: 24.8 us -> none  [shards(): picked = jnp.take(atm_fields, columns.reshape(-1), axis=1)]
    ppermute x20 -> x4, waiting for transfers between devices: 18.8 us -> 2.11 us  [the longest x2 2.11 us: neighbours(): before = lax.ppermute(tail, axes, [(i, i + 1) for i in range(count - 1)])]
    pallas_call x0 -> x9, Pallas kernels: none -> 15.9 us  [the longest x1 8.17 us: remap(): pl.pallas_call(remap_kernel, in_specs=[SMEM] + [HBM] * 8, out_specs=[VMEM...]
    all_to_all x1, starting transfers between devices: 7.65 us -> 20 us  [exchange(): return lax.all_to_all(peak, axes, split_axis=0, concat_axis=0, tiled=True)]
  transfers between devices with their start and end apart: 21 -> 5, of which waited for: 5 -> 3; matrix products, arithmetic and copies ran while one was open for 14% -> 0% of each run, Pallas kernels for 0% -> 2%
where the time goes in v2:
time: 171 us; the launch traced here: 170 us
  blocking collectives  106 us (62%)
  starting transfers between devices  32.1 us (19%)
  Pallas kernels  15.9 us (9%)
  waiting for transfers between devices  11.7 us (7%)
  local copies, waits for them, and re-layouts  3.14 us (2%)
    all_to_all x6, blocking collectives, exchange(): return lax.all_to_all(peak, axes, split_axis=0, concat_axis=0, tiled=True)  84.2 us
    all_to_all x1, blocking collectives, shards(): lax.all_to_all(picked, 'comp', split_axis=0, concat_axis=0, tiled=True)  22 us
    all_to_all x1, starting transfers between devices, exchange(): return lax.all_to_all(peak, axes, split_axis=0, concat_axis=0, tiled=True)  20 us
    all_to_all x1, waiting for transfers between devices, exchange(): return lax.all_to_all(peak, axes, split_axis=0, concat_axis=0, tiled=True)  9.54 us
    pallas_call x1, Pallas kernels, remap(): pl.pallas_call(remap_kernel, in_specs=[SMEM] + [HBM] * 8, out_specs=[VMEM...  8.17 us
    ppermute x2, starting transfers between devices, neighbours(): before = lax.ppermute(tail, axes, [(i, i + 1) for i in range(count - 1)])  6.08 us
    ppermute x2, starting transfers between devices, neighbours(): after = lax.ppermute(head, axes, [(i + 1, i) for i in range(count - 1)])  5.96 us
  transfers between devices with their start and end apart: 5, of which 3 were waited for; matrix products, arithmetic and copies ran while one was open for 0% of the time, Pallas kernels for 2%

profile of v2, /device:TPU:1, one launch (start us, length us, event | category | flops | bytes accessed | tf_op | source)
XLA Modules:
  0.0 169.8 jit_solution(13126875746925055014)
XLA Ops:
  0.6 1.6 shard_map.113
  2.2 20.0 %all-to-all-start = ((f32[96,1,128]{2,1,0:T(1,128)}), f32[96,1,128]{2,1,0:T(1,128)S(1)}, u32[]{:S(2)}, u32[]{:S(2)}) async-start(f32[96,1,128]{2,1,0:T(1,128)} %bitcast.24), calls=%async_computation | async-start | bytes 98304 | tf_op jit(solution)/shard_map/all_to_all | solution.py:130
  22.2 2.7 %shard_map.114.picked_ref = bf16[8,24,1152]{2,1,0:T(8,128)(2,1)} custom-call(bf16[24,2048]{1,0:T(8,128)(2,1)} %fields_hbm.1, s32[1,1,8,4,256]{4,3,2,1,0:T(4,128)} %cols_hbm.1), custom_call_target="tpu_custom_call" | custom-call | tf_op jit(solution)/shard_map/pallas_call | solution.py:85
  24.9 9.5 %all-to-all-done = f32[96,1,128]{2,1,0:T(1,128)S(1)} async-done(((f32[96,1,128]{2,1,0:T(1,128)}), f32[96,1,128]{2,1,0:T(1,128)S(1)}, u32[]{:S(2)}, u32[]{:S(2)}) %all-to-all-start) | async-done | bytes 49184 | tf_op jit(solution)/shard_map/all_to_all | solution.py:130
  34.5 0.0 copy-start.3
  34.5 0.6 copy-done.3
  35.1 1.5 shard_map.115
  36.6 22.0 %all_to_all.67.picked_hbm = bf16[8,24,1152]{2,1,0:T(8,128)(2,1)} all-to-all(bf16[8,24,1152]{2,1,0:T(8,128)(2,1)} %shard_map.115), channel_id=1, replica_groups=mesh['comp'=8,'dom_0'=12,'dom_1'=4,'dom_2'=2] {'comp'}, dimensions={0} | all-to-all | bytes 884736 | tf_op jit(solution)/shard_map/all_to_all | solution.py:378
  58.6 8.2 %shard_map.116 = (f32[24,32,128]{2,1,0:T(8,128)}, f32[8,32,128]{2,1,0:T(8,128)}, f32[32,128]{1,0:T(8,128)}, f32[32,128]{1,0:T(8,128)}, f32[8,128]{1,0:T(8,128)}) custom-call(s32[1,1,8]{2,1,0:T(1,128)} %live_ref.1, bf16[8,24,1152]{2,1,0:T(8,128)(2,1)} %all_to_all.67.picked_hbm, bf16[1,1,8,4,256,256]{5,4,3,2,1,0:T(8,128)(2,1)} %weights_hbm.1, ...), custom_call_target="tpu_custom_call" | custom-call | tf_op jit(solution)/shard_map/pallas_call | solution.py:237
  66.8 1.3 collective-permute-start
  68.1 4.0 %collective-permute-start.1 = (f32[32,128]{1,0:T(8,128)}, f32[32,128]{1,0:T(8,128)S(1)}, u32[]{:S(2)}, u32[]{:S(2)}) collective-permute-start(f32[32,128]{1,0:T(8,128)} %get-tuple-element.19), channel_id=1, source_target_pairs={{0,96},{96,192},{192,288},{288,384},{384,480},{480,576},{576,672},... | collective-permute-start | bytes 49160 | tf_op jit(solution)/shard_map/ppermute | solution.py:43
  72.1 0.0 collective-permute-done.east_ref
  72.1 1.1 collective-permute-done.1.west_ref
  73.1 0.0 copy-start
  73.1 0.9 copy-done
  74.0 4.7 %collective-permute-start.2 = (f32[10,8,128]{2,1,0:T(8,128)S(1)}, f32[10,8,128]{2,1,0:T(8,128)S(1)}, u32[]{:S(2)}, u32[]{:S(2)}) collective-permute-start(f32[10,8,128]{2,1,0:T(8,128)S(1)} %get-tuple-element.20), channel_id=1, source_target_pairs={{1,0},{2,1},{3,2},{4,3},{5,4},{6,5},{7,6},{8,7},{9,8},{10,9},{11,1... | collective-permute-start | bytes 122888 | tf_op jit(solution)/shard_map/ppermute | solution.py:42
  78.7 2.1 %collective-permute-start.3 = (f32[10,8,128]{2,1,0:T(8,128)S(1)}, f32[10,8,128]{2,1,0:T(8,128)S(1)}, u32[]{:S(2)}, u32[]{:S(2)}) collective-permute-start(f32[10,8,128]{2,1,0:T(8,128)S(1)} %get-tuple-element.21), channel_id=1, source_target_pairs={{0,1},{1,2},{2,3},{3,4},{4,5},{5,6},{6,7},{7,8},{8,9},{9,10},{10,1... | collective-permute-start | bytes 122888 | tf_op jit(solution)/shard_map/ppermute | solution.py:43
  80.8 0.0 collective-permute-done.2.after_ref
  80.9 1.1 collective-permute-done.3.before_ref
  81.9 0.0 copy-start.1
  81.9 0.9 copy-done.1
  82.8 0.0 copy-start.2
  82.8 0.7 copy-done.2
  83.5 0.4 shard_map.118
  83.9 16.3 %all_to_all.68 = f32[32,1,128]{2,1,0:T(1,128)S(1)} all-to-all(f32[32,1,128]{2,1,0:T(1,128)S(1)} %bitcast.20), channel_id=1, replica_groups=mesh['comp'=8,'dom_0'=12,'dom_1'=4,'dom_2'=2] {'comp','dom_1'}, dimensions={0} | all-to-all | bytes 32768 | tf_op jit(solution)/shard_map/all_to_all | solution.py:130
  100.2 0.1 reduce_max.27
  100.3 16.8 %all_to_all.69 = f32[24,1,128]{2,1,0:T(1,128)S(1)} all-to-all(f32[24,1,128]{2,1,0:T(1,128)S(1)} %broadcast_in_dim.6), channel_id=1, replica_groups=mesh['comp'=8,'dom_0'=12,'dom_1'=4,'dom_2'=2] {'dom_0','dom_2'}, dimensions={0} | all-to-all | bytes 24576 | tf_op jit(solution)/shard_map/all_to_all | solution.py:130
  117.1 0.3 shard_map.119
  117.4 11.6 %all_to_all.70 = f32[32,1,128]{2,1,0:T(1,128)S(1)} all-to-all(f32[32,1,128]{2,1,0:T(1,128)S(1)} %bitcast.21), channel_id=1, replica_groups=mesh['comp'=8,'dom_0'=12,'dom_1'=4,'dom_2'=2] {'comp','dom_1'}, dimensions={0} | all-to-all | bytes 32768 | tf_op jit(solution)/shard_map/all_to_all | solution.py:130
  129.0 0.1 reduce_max.28
  129.1 14.0 %all_to_all.71 = f32[24,1,128]{2,1,0:T(1,128)S(1)} all-to-all(f32[24,1,128]{2,1,0:T(1,128)S(1)} %broadcast_in_dim.7), channel_id=1, replica_groups=mesh['comp'=8,'dom_0'=12,'dom_1'=4,'dom_2'=2] {'dom_0','dom_2'}, dimensions={0} | all-to-all | bytes 24576 | tf_op jit(solution)/shard_map/all_to_all | solution.py:130
  143.1 0.3 shard_map.120
  143.4 11.6 %all_to_all.72 = f32[32,1,128]{2,1,0:T(1,128)S(1)} all-to-all(f32[32,1,128]{2,1,0:T(1,128)S(1)} %bitcast.22), channel_id=1, replica_groups=mesh['comp'=8,'dom_0'=12,'dom_1'=4,'dom_2'=2] {'comp','dom_1'}, dimensions={0} | all-to-all | bytes 32768 | tf_op jit(solution)/shard_map/all_to_all | solution.py:130
  155.0 0.1 reduce_max.29
  155.0 14.0 %all_to_all.73 = f32[24,1,128]{2,1,0:T(1,128)S(1)} all-to-all(f32[24,1,128]{2,1,0:T(1,128)S(1)} %broadcast_in_dim.8), channel_id=1, replica_groups=mesh['comp'=8,'dom_0'=12,'dom_1'=4,'dom_2'=2] {'dom_0','dom_2'}, dimensions={0} | all-to-all | bytes 24576 | tf_op jit(solution)/shard_map/all_to_all | solution.py:130
  169.0 0.8 shard_map.121
  (4 shorter events, 0.0 us)
Async XLA Ops:
  2.2 32.3 %all-to-all-start = ((f32[96,1,128]{2,1,0:T(1,128)}), f32[96,1,128]{2,1,0:T(1,128)S(1)}, u32[]{:S(2)}, u32[]{:S(2)}) async-start(f32[96,1,128]{2,1,0:T(1,128)} %bitcast.24), calls=%async_computation | async-start | bytes 98304 | tf_op jit(solution)/shard_map/all_to_all | solution.py:130
  34.5 0.6 copy-start.3
  66.8 5.3 %collective-permute-start = (f32[32,128]{1,0:T(8,128)}, f32[32,128]{1,0:T(8,128)S(1)}, u32[]{:S(2)}, u32[]{:S(2)}) collective-permute-start(f32[32,128]{1,0:T(8,128)} %get-tuple-element.18), channel_id=1, source_target_pairs={{96,0},{192,96},{288,192},{384,288},{480,384},{576,480},{672,576},... | collective-permute-start | bytes 49160 | tf_op jit(solution)/shard_map/ppermute | solution.py:42
  68.1 5.1 %collective-permute-start.1 = (f32[32,128]{1,0:T(8,128)}, f32[32,128]{1,0:T(8,128)S(1)}, u32[]{:S(2)}, u32[]{:S(2)}) collective-permute-start(f32[32,128]{1,0:T(8,128)} %get-tuple-element.19), channel_id=1, source_target_pairs={{0,96},{96,192},{192,288},{288,384},{384,480},{480,576},{576,672},... | collective-permute-start | bytes 49160 | tf_op jit(solution)/shard_map/ppermute | solution.py:43
  73.1 0.9 copy-start
  74.0 6.8 %collective-permute-start.2 = (f32[10,8,128]{2,1,0:T(8,128)S(1)}, f32[10,8,128]{2,1,0:T(8,128)S(1)}, u32[]{:S(2)}, u32[]{:S(2)}) collective-permute-start(f32[10,8,128]{2,1,0:T(8,128)S(1)} %get-tuple-element.20), channel_id=1, source_target_pairs={{1,0},{2,1},{3,2},{4,3},{5,4},{6,5},{7,6},{8,7},{9,8},{10,9},{11,1... | collective-permute-start | bytes 122888 | tf_op jit(solution)/shard_map/ppermute | solution.py:42
  78.7 3.2 %collective-permute-start.3 = (f32[10,8,128]{2,1,0:T(8,128)S(1)}, f32[10,8,128]{2,1,0:T(8,128)S(1)}, u32[]{:S(2)}, u32[]{:S(2)}) collective-permute-start(f32[10,8,128]{2,1,0:T(8,128)S(1)} %get-tuple-element.21), channel_id=1, source_target_pairs={{0,1},{1,2},{2,3},{3,4},{4,5},{5,6},{6,7},{7,8},{8,9},{9,10},{10,1... | collective-permute-start | bytes 122888 | tf_op jit(solution)/shard_map/ppermute | solution.py:43
  81.9 0.9 copy-start.1
  82.8 0.7 copy-start.2

commit v3 on v2

--- a/solution.py
+++ b/solution.py
@@ -8,7 +8,6 @@
 from jax.sharding import Mesh
 from jax.sharding import PartitionSpec as P
 
-NSUB = 4
 DOM_SHAPE = (12, 4, 2)
 COMP_DOM = ("comp", "dom_0", "dom_1", "dom_2")
 DOM = ("dom_0", "dom_1", "dom_2")
@@ -151,6 +150,10 @@
         input_output_aliases={1: 0},
         compiler_params=params(56),
     )(seen, picked)
+
+
+def everyone(peak):
+    return exchange(spread_max(exchange(peak, PLANE), COLUMN), COLUMN)
 
 
 def spread_max(seen, axes):
@@ -282,20 +285,15 @@
     return jnp.concatenate([left, jnp.concatenate(right, axis=0)], axis=1)
 
 
+def turning(first_row, total_rows, shape):
+    row = lax.broadcasted_iota(jnp.int32, shape, 0)
+    row = first_row + jnp.where(row < shape[0] - EDGE, row, row - shape[0])
+    return 0.1 + 0.4 * (row.astype(F32) + 0.5) / total_rows
+
+
 def subcycle(first_row, total_rows, depth, wet, level, east, north, push_x, push_y, fresh, peak):
-    nrow, ncol = depth.shape
-    rows = nrow - 2 * EDGE
     step_dt = courant / peak
-    row = lax.broadcasted_iota(jnp.int32, depth.shape, 0)
-    row = first_row + jnp.where(row < rows + EDGE, row, row - nrow)
-    rotation = 0.1 + 0.4 * (row.astype(F32) + 0.5) / total_rows
-
-    def across(x):
-        return pltpu.roll(x, ncol - 1, 1) - pltpu.roll(x, 1, 1)
-
-    def along(x):
-        return pltpu.roll(x, nrow - 1, 0) - pltpu.roll(x, 1, 0)
-
+    rotation = turning(first_row, total_rows, depth.shape)
     flux_x = depth * east * wet
     flux_y = depth * north * wet
     diverge = 0.5 * (across(flux_x) + along(flux_y))
@@ -307,12 +305,88 @@
     return level, new_east, new_north
 
 
+def across(x):
+    return pltpu.roll(x, x.shape[1] - 1, 1) - pltpu.roll(x, 1, 1)
+
+
+def along(x):
+    return pltpu.roll(x, x.shape[0] - 1, 0) - pltpu.roll(x, 1, 0)
+
+
+SAMPLES = (1.2, 0.8, 0.5, 0.3, 0.12)
+CLOSE = 4e-6
+
+
+def curve(terms, dt):
+    root, east0, east1, east2, north0, north1, north2 = terms
+    return root + jnp.abs(east0 + dt * (east1 + dt * east2)) + jnp.abs(north0 + dt * (north1 + dt * north2))
+
+
+def offers(rotation, depth, wet, level, east, north, push_x, push_y, fresh, dt):
+    drift = wet * (fresh - 0.5 * (across(depth * east * wet) + along(depth * north * wet)))
+    still = wet * level
+    own = (slice(0, depth.shape[0] - 2 * EDGE), slice(0, 128))
+    terms = [
+        term[own]
+        for term in (
+            jnp.sqrt(depth),
+            wet * east,
+            wet * (rotation * north - 0.5 * across(still) + push_x - friction * east),
+            wet * (-0.5 * across(drift)),
+            wet * north,
+            wet * (-rotation * east - 0.5 * along(still) + push_y - friction * north),
+            wet * (-0.5 * along(drift)),
+        )
+    ]
+    shape = terms[0].shape
+    index = lax.broadcasted_iota(jnp.int32, shape, 0) * 128 + lax.broadcasted_iota(jnp.int32, shape, 1)
+    lane = lax.broadcasted_iota(jnp.int32, (1, 128), 1)
+    row = jnp.where(lane == 0, peak_of(depth[own], wet[own], east[own], north[own]), 0.0)
+    for j, ratio in enumerate(SAMPLES):
+        speed = curve(terms, ratio * dt)
+        fastest = speed == jnp.max(speed, keepdims=True)
+        first = jnp.min(jnp.where(fastest, index, shape[0] * 128), keepdims=True)
+        for i, term in enumerate(terms):
+            value = jnp.sum(jnp.where(index == first, term, 0.0), keepdims=True)
+            row = jnp.where(lane == 8 + 8 * j + i, value, row)
+    return row
+
+
+def offered(rows, dt):
+    lane = lax.broadcasted_iota(jnp.int32, rows.shape, 1)
+    terms = [rows] + [pltpu.roll(rows, 128 - i, 1) for i in range(1, 7)]
+    here = (lane % 8 == 0) & (lane >= 8) & (lane < 8 + 8 * len(SAMPLES))
+    return jnp.where(here, curve(terms, dt), 0.0)
+
+
+def choose_kernel(rows_ref, seen_ref, out_ref):
+    rows = rows_ref[...]
+    count = rows.shape[0]
+    lane = lax.broadcasted_iota(jnp.int32, rows.shape, 1)
+    ratio = jnp.zeros(rows.shape, F32)
+    for j, sample in enumerate(SAMPLES):
+        ratio = jnp.where(lane // 8 == j + 1, sample, ratio)
+    speed = offered(rows, ratio * (courant / jnp.max(seen_ref[...], keepdims=True)))
+    number = lax.broadcasted_iota(jnp.int32, rows.shape, 0)
+    best = jnp.min(jnp.where(speed == jnp.max(speed, axis=0, keepdims=True), number, count), axis=0, keepdims=True)
+    chosen = jnp.where((number == best) & (lane % 8 == 0), 1.0, 0.0)
+    for shift in (1, 2, 4):
+        chosen = chosen + pltpu.roll(chosen, shift, 1)
+    row = jnp.sum(jnp.where(chosen > 0.0, rows, 0.0), axis=0, keepdims=True)
+    row = jnp.where(lane[:1] == 0, jnp.max(rows, axis=0, keepdims=True), row)
+    out_ref[...] = jnp.broadcast_to(row, out_ref.shape)
+
+
+def lane_max(rows, at):
+    lane = lax.broadcasted_iota(jnp.int32, rows.shape, 1)
+    return jnp.max(jnp.where(lane == at, rows, 0.0), keepdims=True)
+
+
 def finish(depth, wet, new, state_ref, peak_ref):
     for at in range(3):
         state_ref[at] = new[at]
     own = (slice(0, depth.shape[0] - 2 * EDGE), slice(0, 128))
-    peak = peak_of(depth[own], wet[own], new[1][own], new[2][own])
-    peak_ref[...] = jnp.broadcast_to(peak, peak_ref.shape)
+    return peak_of(depth[own], wet[own], new[1][own], new[2][own])
 
 
 def first_kernel(
@@ -323,26 +397,48 @@
     for at, array in enumerate((depth, wet, push_x, push_y, fresh)):
         kept_ref[at] = array
     peak = jnp.max(seen_ref[...], keepdims=True)
-    finish(depth, wet, subcycle(row_ref[0], total_rows, *full, peak), state_ref, peak_ref)
-
-
-def next_state(total_rows, row_ref, kept_ref, old_ref, seen_ref):
-    peak = jnp.max(seen_ref[...], keepdims=True)
+    new = subcycle(row_ref[0], total_rows, *full, peak)
+    for at in range(3):
+        state_ref[at] = new[at]
+    rotation = turning(row_ref[0], total_rows, depth.shape)
+    row = offers(rotation, depth, wet, *new, push_x, push_y, fresh, courant / peak)
+    peak_ref[...] = jnp.broadcast_to(row, peak_ref.shape)
+
+
+def step_from(total_rows, row_ref, kept_ref, old, peak):
     return subcycle(
-        row_ref[0], total_rows, kept_ref[0], kept_ref[1], old_ref[0], old_ref[1], old_ref[2],
-        kept_ref[2], kept_ref[3], kept_ref[4], peak,
-    )
-
-
-def middle_kernel(total_rows, row_ref, kept_ref, old_ref, seen_ref, state_ref, peak_ref):
-    new = next_state(total_rows, row_ref, kept_ref, old_ref, seen_ref)
-    finish(kept_ref[0], kept_ref[1], new, state_ref, peak_ref)
-
-
-def last_kernel(total_rows, row_ref, kept_ref, old_ref, seen_ref, out_ref):
-    new = next_state(total_rows, row_ref, kept_ref, old_ref, seen_ref)
+        row_ref[0], total_rows, kept_ref[0], kept_ref[1], *old, kept_ref[2], kept_ref[3], kept_ref[4], peak
+    )
+
+
+def middle_kernel(total_rows, row_ref, kept_ref, old_ref, rows_ref, second_ref, third_ref, peak_ref, guess_ref):
+    rows = rows_ref[...]
+    peak = lane_max(rows, 0)
+    guess = jnp.max(offered(rows, courant / peak), keepdims=True)
+    second = step_from(total_rows, row_ref, kept_ref, [old_ref[at] for at in range(3)], peak)
+    third = step_from(total_rows, row_ref, kept_ref, second, guess)
+    true_second = finish(kept_ref[0], kept_ref[1], second, second_ref, peak_ref)
+    true_third = finish(kept_ref[0], kept_ref[1], third, third_ref, peak_ref)
+    lane = lax.broadcasted_iota(jnp.int32, peak_ref.shape, 1)
+    peak_ref[...] = jnp.where(lane == 0, true_second, jnp.where(lane == 1, true_third, 0.0))
+    guess_ref[...] = jnp.broadcast_to(guess, guess_ref.shape)
+
+
+def last_kernel(total_rows, row_ref, kept_ref, old_ref, rows_ref, guess_ref, out_ref, good_ref):
+    rows = rows_ref[...]
+    new = step_from(total_rows, row_ref, kept_ref, [old_ref[at] for at in range(3)], lane_max(rows, 1))
     for at in range(3):
         out_ref[at] = new[at][: out_ref.shape[1], :128]
+    true = lane_max(rows, 0)
+    good = jnp.abs(true - guess_ref[0:1, 0:1]) <= CLOSE * true
+    good_ref[...] = jnp.broadcast_to(jnp.where(good, 1, 0), good_ref.shape)
+
+
+def redo_kernel(total_rows, row_ref, kept_ref, old_ref, rows_ref, state_ref, peak_ref):
+    new = step_from(total_rows, row_ref, kept_ref, [old_ref[at] for at in range(3)], lane_max(rows_ref[...], 0))
+    peak = finish(kept_ref[0], kept_ref[1], new, state_ref, peak_ref)
+    lane = lax.broadcasted_iota(jnp.int32, peak_ref.shape, 1)
+    peak_ref[...] = jnp.where(lane == 1, peak, 0.0)
 
 
 def call_small(kernel, scalars, arrays, out_shape):
@@ -388,16 +484,31 @@
         (own, east, west, after, before, seen),
         [five, three, peak_shape],
     )
-    for substep in range(1, NSUB):
-        seen = exchange(spread_max(exchange(peak, PLANE), COLUMN), COLUMN)
-        if substep < NSUB - 1:
-            state, peak = call_small(
-                functools.partial(middle_kernel, total_rows), (first_row,), (kept, state, seen), [three, peak_shape]
-            )
-    state = call_small(
-        functools.partial(last_kernel, total_rows), (first_row,), (kept, state, seen),
-        jax.ShapeDtypeStruct((3, rows, cols), F32),
-    )
+    (chosen,) = call_small(
+        choose_kernel, (), (exchange(peak, PLANE), seen), [jax.ShapeDtypeStruct((axes_size(COLUMN), 128), F32)]
+    )
+    second, third, peak, guess = call_small(
+        functools.partial(middle_kernel, total_rows),
+        (first_row,),
+        (kept, state, exchange(chosen, COLUMN)),
+        [three, three, peak_shape, jax.ShapeDtypeStruct((8, 128), F32)],
+    )
+    result = jax.ShapeDtypeStruct((3, rows, cols), F32)
+    flag = jax.ShapeDtypeStruct((8, 128), jnp.int32)
+    seen = everyone(peak)
+    state, good = call_small(
+        functools.partial(last_kernel, total_rows), (first_row,), (kept, third, seen, guess), [result, flag]
+    )
+
+    def again():
+        state, peak = call_small(
+            functools.partial(redo_kernel, total_rows), (first_row,), (kept, second, seen), [three, peak_shape]
+        )
+        return call_small(
+            functools.partial(last_kernel, total_rows), (first_row,), (kept, state, everyone(peak), guess), [result, flag]
+        )[0]
+
+    state = lax.cond(good[0, 0] == 1, lambda: state, again)
     return fluxes, state
 
 

time: 171 us -> 148 us (0.87)
  blocking collectives: 106 us -> 80.7 us
  Pallas kernels: 15.9 us -> 17.9 us
    all_to_all x6 -> x4, blocking collectives: 84.2 us -> 58.7 us  [exchange(): return lax.all_to_all(peak, axes, split_axis=0, concat_axis=0, tiled=True)]
    pallas_call x5, Pallas kernels: 1.93 us -> 3.94 us  [call_small(): pl.pallas_call(kernel, in_specs=[SMEM] * len(scalars) + [VMEM] * len(arra...]
where the time goes in v3:
time: 148 us; the launch traced here: 147 us
  blocking collectives  80.7 us (55%)
  starting transfers between devices  32.1 us (22%)
  Pallas kernels  17.9 us (12%)
  waiting for transfers between devices  11.7 us (8%)
  local copies, waits for them, and re-layouts  3.62 us (2%)
    all_to_all x4, blocking collectives, exchange(): return lax.all_to_all(peak, axes, split_axis=0, concat_axis=0, tiled=True)  58.7 us
    all_to_all x1, blocking collectives, shards(): lax.all_to_all(picked, 'comp', split_axis=0, concat_axis=0, tiled=True)  22 us
    all_to_all x1, starting transfers between devices, exchange(): return lax.all_to_all(peak, axes, split_axis=0, concat_axis=0, tiled=True)  20 us
    all_to_all x1, waiting for transfers between devices, exchange(): return lax.all_to_all(peak, axes, split_axis=0, concat_axis=0, tiled=True)  9.55 us
    pallas_call x1, Pallas kernels, remap(): pl.pallas_call(remap_kernel, in_specs=[SMEM] + [HBM] * 8, out_specs=[VMEM...  8.17 us
    ppermute x2, starting transfers between devices, neighbours(): before = lax.ppermute(tail, axes, [(i, i + 1) for i in range(count - 1)])  6.08 us
    ppermute x2, starting transfers between devices, neighbours(): after = lax.ppermute(head, axes, [(i + 1, i) for i in range(count - 1)])  5.96 us
    pallas_call x5, Pallas kernels, call_small(): pl.pallas_call(kernel, in_specs=[SMEM] * len(scalars) + [VMEM] * len(arra...  3.94 us
  transfers between devices with their start and end apart: 5, of which 3 were waited for; matrix products, arithmetic and copies ran while one was open for 0% of the time, Pallas kernels for 2%

profile of v3, /device:TPU:1, one launch (start us, length us, event | category | flops | bytes accessed | tf_op | source)
XLA Modules:
  0.0 147.3 jit_solution(8636112567978148905)
XLA Ops:
  0.6 1.6 %shard_map.113 = f32[96,128]{1,0:T(8,128)} custom-call(f32[32,128]{1,0:T(8,128)} %depth_hbm.3, s32[32,128]{1,0:T(8,128)} %wet_hbm.3, f32[32,128]{1,0:T(8,128)} %east_hbm.3, f32[32,128]{1,0:T(8,128)} %north_hbm.3), custom_call_target="tpu_custom_call" | custom-call | tf_op jit(solution)/shard_map/pallas_call | solution.py:114
  2.2 20.0 %all-to-all-start.2 = ((f32[96,1,128]{2,1,0:T(1,128)}), f32[96,1,128]{2,1,0:T(1,128)S(1)}, u32[]{:S(2)}, u32[]{:S(2)}) async-start(f32[96,1,128]{2,1,0:T(1,128)} %bitcast.30), calls=%async_computation.2 | async-start | bytes 98304 | tf_op jit(solution)/shard_map/all_to_all | solution.py:129
  22.2 2.7 %shard_map.114.picked_ref = bf16[8,24,1152]{2,1,0:T(8,128)(2,1)} custom-call(bf16[24,2048]{1,0:T(8,128)(2,1)} %fields_hbm.1, s32[1,1,8,4,256]{4,3,2,1,0:T(4,128)} %cols_hbm.1), custom_call_target="tpu_custom_call" | custom-call | tf_op jit(solution)/shard_map/pallas_call | solution.py:84
  24.9 9.5 %all-to-all-done.2 = f32[96,1,128]{2,1,0:T(1,128)S(1)} async-done(((f32[96,1,128]{2,1,0:T(1,128)}), f32[96,1,128]{2,1,0:T(1,128)S(1)}, u32[]{:S(2)}, u32[]{:S(2)}) %all-to-all-start.2) | async-done | bytes 49184 | tf_op jit(solution)/shard_map/all_to_all | solution.py:129
  34.5 0.0 copy-start.3
  34.5 0.6 copy-done.3
  35.1 1.6 %shard_map.115 = bf16[8,24,1152]{2,1,0:T(8,128)(2,1)} custom-call(f32[96,128]{1,0:T(8,128)} %bitcast.29, bf16[8,24,1152]{2,1,0:T(8,128)(2,1)} %shard_map.114.picked_ref), custom_call_target="tpu_custom_call", output_to_operand_aliasing={{}: (1, {})} | custom-call | tf_op jit(solution)/shard_map/pallas_call | solution.py:144
  36.6 22.0 %all_to_all.70.picked_hbm = bf16[8,24,1152]{2,1,0:T(8,128)(2,1)} all-to-all(bf16[8,24,1152]{2,1,0:T(8,128)(2,1)} %shard_map.115), channel_id=1, replica_groups=mesh['comp'=8,'dom_0'=12,'dom_1'=4,'dom_2'=2] {'comp'}, dimensions={0} | all-to-all | bytes 884736 | tf_op jit(solution)/shard_map/all_to_all | solution.py:474
  58.6 8.2 %shard_map.116 = (f32[24,32,128]{2,1,0:T(8,128)}, f32[8,32,128]{2,1,0:T(8,128)}, f32[32,128]{1,0:T(8,128)}, f32[32,128]{1,0:T(8,128)}, f32[8,128]{1,0:T(8,128)}) custom-call(s32[1,1,8]{2,1,0:T(1,128)} %live_ref.1, bf16[8,24,1152]{2,1,0:T(8,128)(2,1)} %all_to_all.70.picked_hbm, bf16[1,1,8,4,256,256]{5,4,3,2,1,0:T(8,128)(2,1)} %weights_hbm.1, ...), custom_call_target="tpu_custom_call" | custom-call | tf_op jit(solution)/shard_map/pallas_call | solution.py:240
  66.8 1.3 collective-permute-start
  68.1 4.0 %collective-permute-start.1 = (f32[32,128]{1,0:T(8,128)}, f32[32,128]{1,0:T(8,128)S(1)}, u32[]{:S(2)}, u32[]{:S(2)}) collective-permute-start(f32[32,128]{1,0:T(8,128)} %get-tuple-element.43), channel_id=1, source_target_pairs={{0,96},{96,192},{192,288},{288,384},{384,480},{480,576},{576,672},... | collective-permute-start | bytes 49160 | tf_op jit(solution)/shard_map/ppermute | solution.py:42
  72.1 0.0 collective-permute-done.east_ref
  72.1 1.1 collective-permute-done.1.west_ref
  73.2 0.0 copy-start
  73.2 0.9 copy-done
  74.1 4.7 %collective-permute-start.2 = (f32[10,8,128]{2,1,0:T(8,128)S(1)}, f32[10,8,128]{2,1,0:T(8,128)S(1)}, u32[]{:S(2)}, u32[]{:S(2)}) collective-permute-start(f32[10,8,128]{2,1,0:T(8,128)S(1)} %get-tuple-element.44), channel_id=1, source_target_pairs={{1,0},{2,1},{3,2},{4,3},{5,4},{6,5},{7,6},{8,7},{9,8},{10,9},{11,1... | collective-permute-start | bytes 122888 | tf_op jit(solution)/shard_map/ppermute | solution.py:41
  78.8 2.1 %collective-permute-start.3 = (f32[10,8,128]{2,1,0:T(8,128)S(1)}, f32[10,8,128]{2,1,0:T(8,128)S(1)}, u32[]{:S(2)}, u32[]{:S(2)}) collective-permute-start(f32[10,8,128]{2,1,0:T(8,128)S(1)} %get-tuple-element.45), channel_id=1, source_target_pairs={{0,1},{1,2},{2,3},{3,4},{4,5},{5,6},{6,7},{7,8},{8,9},{9,10},{10,1... | collective-permute-start | bytes 122888 | tf_op jit(solution)/shard_map/ppermute | solution.py:42
  80.9 0.0 collective-permute-done.2.after_ref
  80.9 1.1 collective-permute-done.3.before_ref
  81.9 0.0 copy-start.1
  81.9 0.9 copy-done.1
  82.8 0.0 copy-start.2
  82.8 0.7 copy-done.2
  83.5 2.2 %shard_map.118 = (f32[5,48,256]{2,1,0:T(8,128)S(1)}, f32[3,48,256]{2,1,0:T(8,128)S(1)}, f32[32,128]{1,0:T(8,128)S(1)}) custom-call(s32[1]{0:T(128)} %bitcast.7.row_ref, f32[8,32,128]{2,1,0:T(8,128)S(1)} %copy-done.1, f32[32,128]{1,0:T(8,128)S(1)} %collective-permute-done.east_ref, f32[32,128]{1,0:T(8,128)S(1)} %collective-permute-done.1.west_ref, ...), custom_call_target="tpu_custom_call" | custom-call | tf_op jit(solution)/shard_map/pallas_call | solution.py:445
  85.7 16.3 %all_to_all.71 = f32[32,1,128]{2,1,0:T(1,128)S(1)} all-to-all(f32[32,1,128]{2,1,0:T(1,128)S(1)} %bitcast.26), channel_id=1, replica_groups=mesh['comp'=8,'dom_0'=12,'dom_1'=4,'dom_2'=2] {'comp','dom_1'}, dimensions={0} | all-to-all | bytes 32768 | tf_op jit(solution)/shard_map/all_to_all | solution.py:129
  102.0 0.4 shard_map.119
  102.4 16.8 %all_to_all.72 = f32[24,1,128]{2,1,0:T(1,128)S(1)} all-to-all(f32[24,1,128]{2,1,0:T(1,128)S(1)} %bitcast.25), channel_id=1, replica_groups=mesh['comp'=8,'dom_0'=12,'dom_1'=4,'dom_2'=2] {'dom_0','dom_2'}, dimensions={0} | all-to-all | bytes 24576 | tf_op jit(solution)/shard_map/all_to_all | solution.py:129
  119.2 0.5 shard_map.120
  119.8 11.6 %all_to_all.73 = f32[32,1,128]{2,1,0:T(1,128)S(1)} all-to-all(f32[32,1,128]{2,1,0:T(1,128)S(1)} %bitcast.27), channel_id=1, replica_groups=mesh['comp'=8,'dom_0'=12,'dom_1'=4,'dom_2'=2] {'comp','dom_1'}, dimensions={0} | all-to-all | bytes 32768 | tf_op jit(solution)/shard_map/all_to_all | solution.py:129
  131.3 0.1 reduce_max.18
  131.4 14.0 %all_to_all.74 = f32[24,1,128]{2,1,0:T(1,128)S(1)} all-to-all(f32[24,1,128]{2,1,0:T(1,128)S(1)} %broadcast_in_dim.4), channel_id=1, replica_groups=mesh['comp'=8,'dom_0'=12,'dom_1'=4,'dom_2'=2] {'dom_0','dom_2'}, dimensions={0} | all-to-all | bytes 24576 | tf_op jit(solution)/shard_map/all_to_all | solution.py:129
  145.4 0.8 shard_map.121
  146.2 0.5 slice.3
  (3 shorter events, 0.0 us)
Async XLA Ops:
  2.2 32.3 %all-to-all-start.2 = ((f32[96,1,128]{2,1,0:T(1,128)}), f32[96,1,128]{2,1,0:T(1,128)S(1)}, u32[]{:S(2)}, u32[]{:S(2)}) async-start(f32[96,1,128]{2,1,0:T(1,128)} %bitcast.30), calls=%async_computation.2 | async-start | bytes 98304 | tf_op jit(solution)/shard_map/all_to_all | solution.py:129
  34.5 0.6 copy-start.3
  66.8 5.3 %collective-permute-start = (f32[32,128]{1,0:T(8,128)}, f32[32,128]{1,0:T(8,128)S(1)}, u32[]{:S(2)}, u32[]{:S(2)}) collective-permute-start(f32[32,128]{1,0:T(8,128)} %get-tuple-element.42), channel_id=1, source_target_pairs={{96,0},{192,96},{288,192},{384,288},{480,384},{576,480},{672,576},... | collective-permute-start | bytes 49160 | tf_op jit(solution)/shard_map/ppermute | solution.py:41
  68.1 5.1 %collective-permute-start.1 = (f32[32,128]{1,0:T(8,128)}, f32[32,128]{1,0:T(8,128)S(1)}, u32[]{:S(2)}, u32[]{:S(2)}) collective-permute-start(f32[32,128]{1,0:T(8,128)} %get-tuple-element.43), channel_id=1, source_target_pairs={{0,96},{96,192},{192,288},{288,384},{384,480},{480,576},{576,672},... | collective-permute-start | bytes 49160 | tf_op jit(solution)/shard_map/ppermute | solution.py:42
  73.2 0.9 copy-start
  74.1 6.8 %collective-permute-start.2 = (f32[10,8,128]{2,1,0:T(8,128)S(1)}, f32[10,8,128]{2,1,0:T(8,128)S(1)}, u32[]{:S(2)}, u32[]{:S(2)}) collective-permute-start(f32[10,8,128]{2,1,0:T(8,128)S(1)} %get-tuple-element.44), channel_id=1, source_target_pairs={{1,0},{2,1},{3,2},{4,3},{5,4},{6,5},{7,6},{8,7},{9,8},{10,9},{11,1... | collective-permute-start | bytes 122888 | tf_op jit(solution)/shard_map/ppermute | solution.py:41
  78.8 3.2 %collective-permute-start.3 = (f32[10,8,128]{2,1,0:T(8,128)S(1)}, f32[10,8,128]{2,1,0:T(8,128)S(1)}, u32[]{:S(2)}, u32[]{:S(2)}) collective-permute-start(f32[10,8,128]{2,1,0:T(8,128)S(1)} %get-tuple-element.45), channel_id=1, source_target_pairs={{0,1},{1,2},{2,3},{3,4},{4,5},{5,6},{6,7},{7,8},{8,9},{9,10},{10,1... | collective-permute-start | bytes 122888 | tf_op jit(solution)/shard_map/ppermute | solution.py:42
  81.9 0.9 copy-start.1
  82.8 0.7 copy-start.2

commit v4 on v2

--- a/solution.py
+++ b/solution.py
@@ -8,7 +8,6 @@
 from jax.sharding import Mesh
 from jax.sharding import PartitionSpec as P
 
-NSUB = 4
 DOM_SHAPE = (12, 4, 2)
 COMP_DOM = ("comp", "dom_0", "dom_1", "dom_2")
 DOM = ("dom_0", "dom_1", "dom_2")
@@ -61,14 +60,27 @@
     return jnp.where(at == rows16(row, count), jnp.ones_like(at), jnp.zeros_like(at))
 
 
-def pick_kernel(fields_hbm, cols_hbm, out_ref, fields_ref, cols_ref, sems):
-    for copy in fetch((fields_hbm, cols_hbm), (fields_ref, cols_ref), sems):
+def pick_kernel(
+    fields_hbm, cols_hbm, depth_hbm, wet_hbm, east_hbm, north_hbm, out_ref, fields_ref, cols_ref, real_ref, wet_ref, sems
+):
+    copies = fetch(
+        (fields_hbm, cols_hbm, depth_hbm, east_hbm, north_hbm, wet_hbm),
+        (fields_ref, cols_ref, real_ref.at[0], real_ref.at[1], real_ref.at[2], wet_ref),
+        sems,
+    )
+    for copy in copies:
         copy.wait()
     nfield, ncol = fields_ref.shape
     high = ncol // 256
     rows = [fields_ref[:, h * 256 : (h + 1) * 256].astype(F32) for h in range(high)]
     table = jnp.concatenate(rows, axis=0).astype(BF16)
     groups, blocks, width = cols_ref.shape[2:]
+    peak = peak_of(real_ref[0], wet_ref[...].astype(F32), real_ref[1], real_ref[2])
+    peak = jnp.broadcast_to(peak, (nfield, 128))
+    big = peak.astype(BF16).astype(F32)
+    middle = (peak - big).astype(BF16).astype(F32)
+    row = lax.broadcasted_iota(jnp.int32, peak.shape, 0)
+    three = jnp.where(row == 0, big, jnp.where(row == 1, middle, jnp.where(row == 2, peak - big - middle, 0.0)))
     for c in range(groups):
         for k in range(blocks):
             cols = cols_ref[0, 0, c, k : k + 1, :]
@@ -78,79 +90,37 @@
             for h in range(1, high):
                 picked = jnp.where(upper == h, both[h * nfield : (h + 1) * nfield], picked)
             out_ref[c, :, k * width : (k + 1) * width] = picked.astype(BF16)
-
-
-def pick(fields, cols):
+        out_ref[c, :, blocks * width :] = three.astype(BF16)
+
+
+def pick(fields, cols, depth, wet, east, north):
     groups, blocks, width = cols.shape[2:]
     return pl.pallas_call(
         pick_kernel,
-        grid=(1,),
-        in_specs=[HBM, HBM],
-        out_specs=pl.BlockSpec((groups, fields.shape[0], blocks * width), lambda i: (0, 0, 0)),
+        in_specs=[HBM] * 6,
+        out_specs=VMEM,
         out_shape=jax.ShapeDtypeStruct((groups, fields.shape[0], blocks * width + 128), BF16),
         scratch_shapes=[
             pltpu.VMEM(fields.shape, BF16),
             pltpu.VMEM(cols.shape, jnp.int32),
-            pltpu.SemaphoreType.DMA((2,)),
+            pltpu.VMEM((3, *depth.shape), F32),
+            pltpu.VMEM(depth.shape, jnp.int32),
+            pltpu.SemaphoreType.DMA((6,)),
         ],
         compiler_params=params(56),
-    )(fields, cols)
+    )(fields, cols, depth, wet, east, north)
 
 
 def peak_of(depth, wet, east, north):
     return jnp.max(jnp.sqrt(depth) + wet * (jnp.abs(east) + jnp.abs(north)), keepdims=True)
 
 
-def speed_kernel(depth_hbm, wet_hbm, east_hbm, north_hbm, peak_ref, real_ref, wet_ref, sems):
-    copies = fetch(
-        (depth_hbm, east_hbm, north_hbm, wet_hbm), (real_ref.at[0], real_ref.at[1], real_ref.at[2], wet_ref), sems
-    )
-    for copy in copies:
-        copy.wait()
-    peak = peak_of(real_ref[0], wet_ref[...].astype(F32), real_ref[1], real_ref[2])
-    peak_ref[...] = jnp.broadcast_to(peak, peak_ref.shape)
-
-
-def first_speed(depth, wet, east, north):
-    return pl.pallas_call(
-        speed_kernel,
-        in_specs=[HBM] * 4,
-        out_specs=VMEM,
-        out_shape=jax.ShapeDtypeStruct((axes_size(DOM), 128), F32),
-        scratch_shapes=[
-            pltpu.VMEM((3, *depth.shape), F32),
-            pltpu.VMEM(depth.shape, jnp.int32),
-            pltpu.SemaphoreType.DMA((4,)),
-        ],
-        compiler_params=params(56),
-    )(depth, wet, east, north)
-
-
 def exchange(peak, axes):
     return lax.all_to_all(peak, axes, split_axis=0, concat_axis=0, tiled=True)
 
 
-def insert_kernel(seen_ref, picked_ref, out_ref):
-    peak = jnp.broadcast_to(jnp.max(seen_ref[...], keepdims=True), (1, 128))
-    big = peak.astype(BF16).astype(F32)
-    middle = (peak - big).astype(BF16).astype(F32)
-    row = lax.broadcasted_iota(jnp.int32, out_ref.shape[1:], 0)
-    three = jnp.where(row == 0, big, jnp.where(row == 1, middle, jnp.where(row == 2, peak - big - middle, 0.0)))
-    for c in range(out_ref.shape[0]):
-        out_ref[c] = three.astype(BF16)
-
-
-def insert(seen, picked):
-    groups, nfield, width = picked.shape
-    return pl.pallas_call(
-        insert_kernel,
-        grid=(1,),
-        in_specs=[pl.BlockSpec(seen.shape, lambda i: (0, 0)), HBM],
-        out_specs=pl.BlockSpec((groups, nfield, 128), lambda i: (0, 0, width // 128 - 1)),
-        out_shape=jax.ShapeDtypeStruct(picked.shape, picked.dtype),
-        input_output_aliases={1: 0},
-        compiler_params=params(56),
-    )(seen, picked)
+def everyone(peak):
+    return exchange(spread_max(exchange(peak, PLANE), COLUMN), COLUMN)
 
 
 def spread_max(seen, axes):
@@ -282,20 +252,15 @@
     return jnp.concatenate([left, jnp.concatenate(right, axis=0)], axis=1)
 
 
+def turning(first_row, total_rows, shape):
+    row = lax.broadcasted_iota(jnp.int32, shape, 0)
+    row = first_row + jnp.where(row < shape[0] - EDGE, row, row - shape[0])
+    return 0.1 + 0.4 * (row.astype(F32) + 0.5) / total_rows
+
+
 def subcycle(first_row, total_rows, depth, wet, level, east, north, push_x, push_y, fresh, peak):
-    nrow, ncol = depth.shape
-    rows = nrow - 2 * EDGE
     step_dt = courant / peak
-    row = lax.broadcasted_iota(jnp.int32, depth.shape, 0)
-    row = first_row + jnp.where(row < rows + EDGE, row, row - nrow)
-    rotation = 0.1 + 0.4 * (row.astype(F32) + 0.5) / total_rows
-
-    def across(x):
-        return pltpu.roll(x, ncol - 1, 1) - pltpu.roll(x, 1, 1)
-
-    def along(x):
-        return pltpu.roll(x, nrow - 1, 0) - pltpu.roll(x, 1, 0)
-
+    rotation = turning(first_row, total_rows, depth.shape)
     flux_x = depth * east * wet
     flux_y = depth * north * wet
     diverge = 0.5 * (across(flux_x) + along(flux_y))
@@ -307,42 +272,160 @@
     return level, new_east, new_north
 
 
-def finish(depth, wet, new, state_ref, peak_ref):
-    for at in range(3):
-        state_ref[at] = new[at]
+def across(x):
+    return pltpu.roll(x, x.shape[1] - 1, 1) - pltpu.roll(x, 1, 1)
+
+
+def along(x):
+    return pltpu.roll(x, x.shape[0] - 1, 0) - pltpu.roll(x, 1, 0)
+
+
+SAMPLES = ((1.0, 0.0), (0.6, 0.0), (1.0, 0.5), (0.6, 0.25))
+SLOT = 32
+TERMS = 19
+CLOSE = 4e-6
+
+
+def curve(terms, p, q):
+    def one(c):
+        parts = [c[3 * a] + q * (c[3 * a + 1] + q * c[3 * a + 2]) for a in range(3)]
+        return jnp.abs(parts[0] + p * (parts[1] + p * parts[2]))
+
+    return terms[0] + one(terms[1:10]) + one(terms[10:19])
+
+
+def powers(depth, wet, rotation, level, east, north, push_x=None, push_y=None, fresh=None):
+    drift = -0.5 * (across(depth * east * wet) + along(depth * north * wet))
+    turn_x, turn_y = rotation * north - friction * east, -rotation * east - friction * north
+    if fresh is not None:
+        drift, turn_x, turn_y = drift + fresh, turn_x + push_x, turn_y + push_y
+    drift = wet * drift
+    if level is not None:
+        still = wet * level
+        turn_x, turn_y = turn_x - 0.5 * across(still), turn_y - 0.5 * along(still)
+    else:
+        still = None
+    return (
+        (still, wet * east, wet * north),
+        (drift, wet * turn_x, wet * turn_y),
+        (None, wet * (-0.5 * across(drift)), wet * (-0.5 * along(drift))),
+    )
+
+
+def offers(rotation, depth, wet, level, east, north, push_x, push_y, fresh, peak):
     own = (slice(0, depth.shape[0] - 2 * EDGE), slice(0, 128))
-    peak = peak_of(depth[own], wet[own], new[1][own], new[2][own])
-    peak_ref[...] = jnp.broadcast_to(peak, peak_ref.shape)
-
-
-def first_kernel(
-    total_rows, row_ref, own_ref, east_ref, west_ref, after_ref, before_ref, seen_ref, kept_ref, state_ref, peak_ref
+    forcing = (push_x, push_y, fresh)
+    u, v = [], []
+    for a, part in enumerate(powers(depth, wet, rotation, level, east, north, *forcing)):
+        for two in powers(depth, wet, rotation, *part, *(forcing if a == 0 else ())):
+            u.append(two[1][own])
+            v.append(two[2][own])
+    terms = [jnp.sqrt(depth[own])] + u + v
+    shape = terms[0].shape
+    index = lax.broadcasted_iota(jnp.int32, shape, 0) * 128 + lax.broadcasted_iota(jnp.int32, shape, 1)
+    lane = lax.broadcasted_iota(jnp.int32, (1, 128), 1)
+    dt = courant / peak
+    row = jnp.where(lane == SLOT - 1, peak, 0.0)
+    for j, (p, q) in enumerate(SAMPLES):
+        speed = curve(terms, p * dt, q * dt)
+        fastest = speed == jnp.max(speed, keepdims=True)
+        first = jnp.min(jnp.where(fastest, index, shape[0] * 128), keepdims=True)
+        for i, term in enumerate(terms):
+            value = jnp.sum(jnp.where(index == first, term, 0.0), keepdims=True)
+            row = jnp.where(lane == SLOT * j + i, value, row)
+    return row
+
+
+def offered(rows, p, q):
+    lane = lax.broadcasted_iota(jnp.int32, rows.shape, 1)
+    terms = [rows] + [pltpu.roll(rows, 128 - i, 1) for i in range(1, TERMS)]
+    return jnp.where(lane % SLOT == 0, curve(terms, p, q), 0.0)
+
+
+def choose_kernel(rows_ref, out_ref):
+    rows = rows_ref[...]
+    count = rows.shape[0]
+    lane = lax.broadcasted_iota(jnp.int32, rows.shape, 1)
+    dt = courant / lane_max(rows, SLOT - 1)
+    p, q = jnp.zeros(rows.shape, F32), jnp.zeros(rows.shape, F32)
+    for j, (first, second) in enumerate(SAMPLES):
+        p = jnp.where(lane // SLOT == j, first, p)
+        q = jnp.where(lane // SLOT == j, second, q)
+    speed = offered(rows, p * dt, q * dt)
+    number = lax.broadcasted_iota(jnp.int32, rows.shape, 0)
+    best = jnp.min(jnp.where(speed == jnp.max(speed, axis=0, keepdims=True), number, count), axis=0, keepdims=True)
+    chosen = jnp.where((number == best) & (lane % SLOT == 0), 1.0, 0.0)
+    for shift in (1, 2, 4, 8, 16):
+        chosen = chosen + pltpu.roll(chosen, shift, 1)
+    row = jnp.sum(jnp.where(chosen > 0.0, rows, 0.0), axis=0, keepdims=True)
+    row = jnp.where(lane[:1] == SLOT - 1, jnp.max(rows, axis=0, keepdims=True), row)
+    out_ref[...] = jnp.broadcast_to(row, out_ref.shape)
+
+
+def lane_max(rows, at):
+    lane = lax.broadcasted_iota(jnp.int32, rows.shape, 1)
+    return jnp.max(jnp.where(lane == at, rows, 0.0), keepdims=True)
+
+
+def offer_kernel(
+    total_rows, row_ref, own_ref, east_ref, west_ref, after_ref, before_ref, seen_ref, kept_ref, state_ref, row_out_ref
 ):
     full = [extended(at, own_ref, east_ref, west_ref, after_ref, before_ref) for at in range(KEPT)]
     depth, wet, level, east, north, push_x, push_y, fresh = full
     for at, array in enumerate((depth, wet, push_x, push_y, fresh)):
         kept_ref[at] = array
-    peak = jnp.max(seen_ref[...], keepdims=True)
-    finish(depth, wet, subcycle(row_ref[0], total_rows, *full, peak), state_ref, peak_ref)
-
-
-def next_state(total_rows, row_ref, kept_ref, old_ref, seen_ref):
-    peak = jnp.max(seen_ref[...], keepdims=True)
+    for at, array in enumerate((level, east, north)):
+        state_ref[at] = array
+    rotation = turning(row_ref[0], total_rows, depth.shape)
+    row = offers(rotation, depth, wet, level, east, north, push_x, push_y, fresh, jnp.max(seen_ref[...], keepdims=True))
+    row_out_ref[...] = jnp.broadcast_to(row, row_out_ref.shape)
+
+
+def step_from(total_rows, row_ref, kept_ref, old, peak):
     return subcycle(
-        row_ref[0], total_rows, kept_ref[0], kept_ref[1], old_ref[0], old_ref[1], old_ref[2],
-        kept_ref[2], kept_ref[3], kept_ref[4], peak,
-    )
-
-
-def middle_kernel(total_rows, row_ref, kept_ref, old_ref, seen_ref, state_ref, peak_ref):
-    new = next_state(total_rows, row_ref, kept_ref, old_ref, seen_ref)
-    finish(kept_ref[0], kept_ref[1], new, state_ref, peak_ref)
-
-
-def last_kernel(total_rows, row_ref, kept_ref, old_ref, seen_ref, out_ref):
-    new = next_state(total_rows, row_ref, kept_ref, old_ref, seen_ref)
+        row_ref[0], total_rows, kept_ref[0], kept_ref[1], *old, kept_ref[2], kept_ref[3], kept_ref[4], peak
+    )
+
+
+def local_peak(kept_ref, state):
+    depth, wet = kept_ref[0], kept_ref[1]
+    own = (slice(0, depth.shape[0] - 2 * EDGE), slice(0, 128))
+    return peak_of(depth[own], wet[own], state[1][own], state[2][own])
+
+
+def middle_kernel(total_rows, row_ref, kept_ref, old_ref, rows_ref, third_ref, peak_ref, guess_ref):
+    rows = rows_ref[...]
+    peaks = [lane_max(rows, SLOT - 1)]
+    peaks.append(jnp.max(offered(rows, courant / peaks[0], 0.0), keepdims=True))
+    peaks.append(jnp.max(offered(rows, courant / peaks[0], courant / peaks[1]), keepdims=True))
+    state = [old_ref[at] for at in range(3)]
+    lane = lax.broadcasted_iota(jnp.int32, (1, 128), 1)
+    row = jnp.zeros((1, 128), F32)
+    for at in range(3):
+        state = step_from(total_rows, row_ref, kept_ref, state, peaks[at])
+        row = jnp.where(lane == at, local_peak(kept_ref, state), row)
+    for at in range(3):
+        third_ref[at] = state[at]
+    peak_ref[...] = jnp.broadcast_to(row, peak_ref.shape)
+    guess_ref[...] = jnp.broadcast_to(jnp.where(lane == 0, peaks[1], peaks[2]), guess_ref.shape)
+
+
+def last_kernel(total_rows, row_ref, kept_ref, old_ref, rows_ref, guess_ref, out_ref, good_ref):
+    rows = rows_ref[...]
+    new = step_from(total_rows, row_ref, kept_ref, [old_ref[at] for at in range(3)], lane_max(rows, 2))
     for at in range(3):
         out_ref[at] = new[at][: out_ref.shape[1], :128]
+    lane = lax.broadcasted_iota(jnp.int32, (1, 128), 1)
+    true = jnp.max(rows, axis=0, keepdims=True)
+    off = jnp.where(lane < 2, jnp.abs(true - guess_ref[0:1, :]) - CLOSE * true, -1.0)
+    good_ref[...] = jnp.broadcast_to(jnp.where(jnp.max(off, keepdims=True) <= 0.0, 1, 0), good_ref.shape)
+
+
+def redo_kernel(total_rows, at, row_ref, kept_ref, old_ref, rows_ref, state_ref, peak_ref):
+    new = step_from(total_rows, row_ref, kept_ref, [old_ref[i] for i in range(3)], lane_max(rows_ref[...], at))
+    for i in range(3):
+        state_ref[i] = new[i]
+    peak_ref[...] = jnp.broadcast_to(local_peak(kept_ref, new), peak_ref.shape)
 
 
 def call_small(kernel, scalars, arrays, out_shape):
@@ -372,9 +455,7 @@
     rim = jax.ShapeDtypeStruct((KEPT + 2, EDGE, cols), F32)
     peak_shape = jax.ShapeDtypeStruct((axes_size(PLANE), 128), F32)
 
-    seen = exchange(first_speed(ocean_depth, wet_mask, east_vel, north_vel), DOM)
-    picked = pick(atm_fields, send_cols)
-    picked = insert(seen, picked)
+    picked = pick(atm_fields, send_cols, ocean_depth, wet_mask, east_vel, north_vel)
     received = lax.all_to_all(picked, "comp", split_axis=0, concat_axis=0, tiled=True)
     fluxes, own, head, tail, seen = remap(
         live_blocks, received, remap_weights, row_map, ocean_depth, wet_mask, sea_level, east_vel, north_vel
@@ -382,22 +463,43 @@
     east, west = neighbours(head, tail, ("comp",))
     top, bottom = call_small(edges_kernel, (), (own, east, west), [rim, rim])
     after, before = neighbours(top, bottom, DOM)
-    kept, state, peak = call_small(
-        functools.partial(first_kernel, total_rows),
+    kept, start, row = call_small(
+        functools.partial(offer_kernel, total_rows),
         (first_row,),
         (own, east, west, after, before, seen),
         [five, three, peak_shape],
     )
-    for substep in range(1, NSUB):
-        seen = exchange(spread_max(exchange(peak, PLANE), COLUMN), COLUMN)
-        if substep < NSUB - 1:
+    (row,) = call_small(
+        choose_kernel, (), (exchange(row, PLANE),), [jax.ShapeDtypeStruct((axes_size(COLUMN), 128), F32)]
+    )
+    first = exchange(row, COLUMN)
+    third, peak, guess = call_small(
+        functools.partial(middle_kernel, total_rows),
+        (first_row,),
+        (kept, start, first),
+        [three, peak_shape, jax.ShapeDtypeStruct((8, 128), F32)],
+    )
+
+    def last(third, seen):
+        return call_small(
+            functools.partial(last_kernel, total_rows),
+            (first_row,),
+            (kept, third, seen, guess),
+            [jax.ShapeDtypeStruct((3, rows, cols), F32), jax.ShapeDtypeStruct((8, 128), jnp.int32)],
+        )
+
+    state, good = last(third, everyone(peak))
+
+    def again():
+        state, seen, at = start, first, SLOT - 1
+        for _ in range(3):
             state, peak = call_small(
-                functools.partial(middle_kernel, total_rows), (first_row,), (kept, state, seen), [three, peak_shape]
+                functools.partial(redo_kernel, total_rows, at), (first_row,), (kept, state, seen), [three, peak_shape]
             )
-    state = call_small(
-        functools.partial(last_kernel, total_rows), (first_row,), (kept, state, seen),
-        jax.ShapeDtypeStruct((3, rows, cols), F32),
-    )
+            seen, at = everyone(peak), 2
+        return last(state, seen)[0]
+
+    state = lax.cond(good[0, 0] == 1, lambda: state, again)
     return fluxes, state
 
 

time: 171 us -> 129 us (0.75)
  blocking collectives: 106 us -> 73.2 us
  starting transfers between devices: 32.1 us -> 23.5 us
    all_to_all x6 -> x3, blocking collectives: 84.2 us -> 54.2 us  [exchange(): return lax.all_to_all(peak, axes, split_axis=0, concat_axis=0, tiled=True)]
    all_to_all x1, starting transfers between devices: 20 us -> 5.3 us  [exchange(): return lax.all_to_all(peak, axes, split_axis=0, concat_axis=0, tiled=True)]
    ppermute x2, starting transfers between devices: 5.96 us -> 12.3 us  [neighbours(): after = lax.ppermute(head, axes, [(i + 1, i) for i in range(count - 1)])]
    pallas_call x3 -> x1, Pallas kernels: 5.77 us -> 2.73 us  [pick(): pl.pallas_call(pick_kernel, in_specs=[HBM] * 6, out_specs=VMEM, out_shape...]
    all_to_all x1, blocking collectives: 22 us -> 19 us  [shards(): lax.all_to_all(picked, 'comp', split_axis=0, concat_axis=0, tiled=True)]
    pallas_call x5, Pallas kernels: 1.93 us -> 4.14 us  [call_small(): pl.pallas_call(kernel, in_specs=[SMEM] * len(scalars) + [VMEM] * len(arra...]
  transfers between devices with their start and end apart: 5 -> 5, of which waited for: 3 -> 3; matrix products, arithmetic and copies ran while one was open for 0% -> 0% of each run, Pallas kernels for 2% -> 0%
where the time goes in v4:
time: 129 us
  blocking collectives  73.2 us (57%)
  starting transfers between devices  23.5 us (18%)
  Pallas kernels  15 us (12%)
  waiting for transfers between devices  11.7 us (9%)
  local copies, waits for them, and re-layouts  3.68 us (3%)
  between operations  1.43 us (1%)
    all_to_all x3, blocking collectives, exchange(): return lax.all_to_all(peak, axes, split_axis=0, concat_axis=0, tiled=True)  54.2 us
    all_to_all x1, blocking collectives, shards(): lax.all_to_all(picked, 'comp', split_axis=0, concat_axis=0, tiled=True)  19 us
    ppermute x2, starting transfers between devices, neighbours(): after = lax.ppermute(head, axes, [(i + 1, i) for i in range(count - 1)])  12.3 us
    all_to_all x1, waiting for transfers between devices, exchange(): return lax.all_to_all(peak, axes, split_axis=0, concat_axis=0, tiled=True)  9.47 us
    pallas_call x1, Pallas kernels, remap(): pl.pallas_call(remap_kernel, in_specs=[SMEM] + [HBM] * 8, out_specs=[VMEM...  8.17 us
    ppermute x2, starting transfers between devices, neighbours(): before = lax.ppermute(tail, axes, [(i, i + 1) for i in range(count - 1)])  5.91 us
    all_to_all x1, starting transfers between devices, exchange(): return lax.all_to_all(peak, axes, split_axis=0, concat_axis=0, tiled=True)  5.3 us
    pallas_call x5, Pallas kernels, call_small(): pl.pallas_call(kernel, in_specs=[SMEM] * len(scalars) + [VMEM] * len(arra...  4.14 us
  transfers between devices with their start and end apart: 5, of which 3 were waited for; matrix products, arithmetic and copies ran while one was open for 0% of the time, Pallas kernels for 0%

profile of v4, /device:TPU:1, one launch (start us, length us, event | category | flops | bytes accessed | tf_op | source)
XLA Modules:
  0.0 128.6 jit_solution(3260438329033058904)
XLA Ops:
  0.6 2.7 %shard_map.113 = bf16[8,24,1152]{2,1,0:T(8,128)(2,1)} custom-call(bf16[24,2048]{1,0:T(8,128)(2,1)} %fields_hbm.1, s32[1,1,8,4,256]{4,3,2,1,0:T(4,128)} %cols_hbm.1, f32[32,128]{1,0:T(8,128)} %depth_hbm.3, s32[32,128]{1,0:T(8,128)} %wet_hbm.3, f32[32,128]{1,0:T(8,128)} %east_hbm.3, f32[32,128]{1,0:T(8,128)} %north_hbm.3), custom_call_target="tpu_custom_call" | custom-call | tf_op jit(solution)/shard_map/pallas_call | solution.py:98
  3.4 19.0 %all_to_all.89.picked_hbm = bf16[8,24,1152]{2,1,0:T(8,128)(2,1)} all-to-all(bf16[8,24,1152]{2,1,0:T(8,128)(2,1)} %shard_map.113), channel_id=1, replica_groups=mesh['comp'=8,'dom_0'=12,'dom_1'=4,'dom_2'=2] {'comp'}, dimensions={0} | all-to-all | bytes 884736 | tf_op jit(solution)/shard_map/all_to_all | solution.py:459
  22.4 8.2 %shard_map.114 = (f32[24,32,128]{2,1,0:T(8,128)}, f32[8,32,128]{2,1,0:T(8,128)}, f32[32,128]{1,0:T(8,128)}, f32[32,128]{1,0:T(8,128)}, f32[8,128]{1,0:T(8,128)}) custom-call(s32[1,1,8]{2,1,0:T(1,128)} %live_ref.1, bf16[8,24,1152]{2,1,0:T(8,128)(2,1)} %all_to_all.89.picked_hbm, bf16[1,1,8,4,256,256]{5,4,3,2,1,0:T(8,128)(2,1)} %weights_hbm.1, ...), custom_call_target="tpu_custom_call" | custom-call | tf_op jit(solution)/shard_map/pallas_call | solution.py:207
  30.6 1.3 %collective-permute-start = (f32[32,128]{1,0:T(8,128)}, f32[32,128]{1,0:T(8,128)S(1)}, u32[]{:S(2)}, u32[]{:S(2)}) collective-permute-start(f32[32,128]{1,0:T(8,128)} %get-tuple-element.45), channel_id=1, source_target_pairs={{96,0},{192,96},{288,192},{384,288},{480,384},{576,480},{672,576},... | collective-permute-start | bytes 49160 | tf_op jit(solution)/shard_map/ppermute | solution.py:41
  31.9 4.0 %collective-permute-start.1 = (f32[32,128]{1,0:T(8,128)}, f32[32,128]{1,0:T(8,128)S(1)}, u32[]{:S(2)}, u32[]{:S(2)}) collective-permute-start(f32[32,128]{1,0:T(8,128)} %get-tuple-element.46), channel_id=1, source_target_pairs={{0,96},{96,192},{192,288},{288,384},{384,480},{480,576},{576,672},... | collective-permute-start | bytes 49160 | tf_op jit(solution)/shard_map/ppermute | solution.py:42
  35.9 0.0 collective-permute-done.east_ref
  35.9 1.1 collective-permute-done.1.west_ref
  36.9 0.0 copy-start
  37.0 0.9 copy-done
  37.9 11.0 %collective-permute-start.2 = (f32[10,8,128]{2,1,0:T(8,128)S(1)}, f32[10,8,128]{2,1,0:T(8,128)S(1)}, u32[]{:S(2)}, u32[]{:S(2)}) collective-permute-start(f32[10,8,128]{2,1,0:T(8,128)S(1)} %get-tuple-element.47), channel_id=1, source_target_pairs={{1,0},{2,1},{3,2},{4,3},{5,4},{6,5},{7,6},{8,7},{9,8},{10,9},{11,1... | collective-permute-start | bytes 122888 | tf_op jit(solution)/shard_map/ppermute | solution.py:41
  48.9 1.9 %collective-permute-start.3 = (f32[10,8,128]{2,1,0:T(8,128)S(1)}, f32[10,8,128]{2,1,0:T(8,128)S(1)}, u32[]{:S(2)}, u32[]{:S(2)}) collective-permute-start(f32[10,8,128]{2,1,0:T(8,128)S(1)} %get-tuple-element.48), channel_id=1, source_target_pairs={{0,1},{1,2},{2,3},{3,4},{4,5},{5,6},{6,7},{7,8},{8,9},{9,10},{10,1... | collective-permute-start | bytes 122888 | tf_op jit(solution)/shard_map/ppermute | solution.py:42
  50.8 0.0 collective-permute-done.2.after_ref
  50.8 1.2 collective-permute-done.3.before_ref
  52.0 0.0 copy-start.1
  52.0 0.9 copy-done.1
  52.9 0.0 copy-start.2
  52.9 0.7 copy-done.2
  53.6 2.0 %shard_map.116 = (f32[5,48,256]{2,1,0:T(8,128)S(1)}, f32[3,48,256]{2,1,0:T(8,128)S(1)}, f32[32,128]{1,0:T(8,128)S(1)}) custom-call(s32[1]{0:T(128)} %bitcast.12.row_ref, f32[8,32,128]{2,1,0:T(8,128)S(1)} %copy-done.1, f32[32,128]{1,0:T(8,128)S(1)} %collective-permute-done.east_ref, f32[32,128]{1,0:T(8,128)S(1)} %collective-permute-done.1.west_ref, ...), custom_call_target="tpu_custom_call" | custom-call | tf_op jit(solution)/shard_map/pallas_call | solution.py:432
  55.6 15.7 %all_to_all.90 = f32[32,1,128]{2,1,0:T(1,128)S(1)} all-to-all(f32[32,1,128]{2,1,0:T(1,128)S(1)} %bitcast.32), channel_id=1, replica_groups=mesh['comp'=8,'dom_0'=12,'dom_1'=4,'dom_2'=2] {'comp','dom_1'}, dimensions={0} | all-to-all | bytes 32768 | tf_op jit(solution)/shard_map/all_to_all | solution.py:119
  71.3 0.5 shard_map.117
  71.8 26.9 %all_to_all.91 = f32[24,1,128]{2,1,0:T(1,128)S(1)} all-to-all(f32[24,1,128]{2,1,0:T(1,128)S(1)} %bitcast.31), channel_id=1, replica_groups=mesh['comp'=8,'dom_0'=12,'dom_1'=4,'dom_2'=2] {'dom_0','dom_2'}, dimensions={0} | all-to-all | bytes 24576 | tf_op jit(solution)/shard_map/all_to_all | solution.py:119
  98.7 0.7 shard_map.118
  99.5 11.6 %all_to_all.92 = f32[32,1,128]{2,1,0:T(1,128)S(1)} all-to-all(f32[32,1,128]{2,1,0:T(1,128)S(1)} %bitcast.35), channel_id=1, replica_groups=mesh['comp'=8,'dom_0'=12,'dom_1'=4,'dom_2'=2] {'comp','dom_1'}, dimensions={0} | all-to-all | bytes 32768 | tf_op jit(solution)/shard_map/all_to_all | solution.py:119
  111.0 0.1 reduce_max.36
  111.1 0.6 broadcast_in_dim.8
  111.7 5.3 %all-to-all-start.10 = ((f32[24,1,128]{2,1,0:T(1,128)}), f32[24,1,128]{2,1,0:T(1,128)S(1)}, u32[]{:S(2)}, u32[]{:S(2)}) async-start(f32[24,1,128]{2,1,0:T(1,128)} %broadcast_in_dim.8), calls=%async_computation.10 | async-start | bytes 24576 | tf_op jit(solution)/shard_map/all_to_all | solution.py:119
  117.0 9.5 %all-to-all-done.10 = f32[24,1,128]{2,1,0:T(1,128)S(1)} async-done(((f32[24,1,128]{2,1,0:T(1,128)}), f32[24,1,128]{2,1,0:T(1,128)S(1)}, u32[]{:S(2)}, u32[]{:S(2)}) %all-to-all-start.10) | async-done | bytes 12320 | tf_op jit(solution)/shard_map/all_to_all | solution.py:119
  126.5 0.8 shard_map.119
  127.3 0.6 slice.3
  (2 shorter events, 0.0 us)
Async XLA Ops:
  30.6 5.3 %collective-permute-start = (f32[32,128]{1,0:T(8,128)}, f32[32,128]{1,0:T(8,128)S(1)}, u32[]{:S(2)}, u32[]{:S(2)}) collective-permute-start(f32[32,128]{1,0:T(8,128)} %get-tuple-element.45), channel_id=1, source_target_pairs={{96,0},{192,96},{288,192},{384,288},{480,384},{576,480},{672,576},... | collective-permute-start | bytes 49160 | tf_op jit(solution)/shard_map/ppermute | solution.py:41
  31.9 5.1 %collective-permute-start.1 = (f32[32,128]{1,0:T(8,128)}, f32[32,128]{1,0:T(8,128)S(1)}, u32[]{:S(2)}, u32[]{:S(2)}) collective-permute-start(f32[32,128]{1,0:T(8,128)} %get-tuple-element.46), channel_id=1, source_target_pairs={{0,96},{96,192},{192,288},{288,384},{384,480},{480,576},{576,672},... | collective-permute-start | bytes 49160 | tf_op jit(solution)/shard_map/ppermute | solution.py:42
  36.9 0.9 copy-start
  37.9 13.0 %collective-permute-start.2 = (f32[10,8,128]{2,1,0:T(8,128)S(1)}, f32[10,8,128]{2,1,0:T(8,128)S(1)}, u32[]{:S(2)}, u32[]{:S(2)}) collective-permute-start(f32[10,8,128]{2,1,0:T(8,128)S(1)} %get-tuple-element.47), channel_id=1, source_target_pairs={{1,0},{2,1},{3,2},{4,3},{5,4},{6,5},{7,6},{8,7},{9,8},{10,9},{11,1... | collective-permute-start | bytes 122888 | tf_op jit(solution)/shard_map/ppermute | solution.py:41
  48.9 3.1 %collective-permute-start.3 = (f32[10,8,128]{2,1,0:T(8,128)S(1)}, f32[10,8,128]{2,1,0:T(8,128)S(1)}, u32[]{:S(2)}, u32[]{:S(2)}) collective-permute-start(f32[10,8,128]{2,1,0:T(8,128)S(1)} %get-tuple-element.48), channel_id=1, source_target_pairs={{0,1},{1,2},{2,3},{3,4},{4,5},{5,6},{6,7},{7,8},{8,9},{9,10},{10,1... | collective-permute-start | bytes 122888 | tf_op jit(solution)/shard_map/ppermute | solution.py:42
  52.0 0.9 copy-start.1
  52.9 0.7 copy-start.2
  111.7 14.8 %all-to-all-start.10 = ((f32[24,1,128]{2,1,0:T(1,128)}), f32[24,1,128]{2,1,0:T(1,128)S(1)}, u32[]{:S(2)}, u32[]{:S(2)}) async-start(f32[24,1,128]{2,1,0:T(1,128)} %broadcast_in_dim.8), calls=%async_computation.10 | async-start | bytes 24576 | tf_op jit(solution)/shard_map/all_to_all | solution.py:119

commit v5 on v4

--- a/solution.py
+++ b/solution.py
@@ -60,27 +60,14 @@
     return jnp.where(at == rows16(row, count), jnp.ones_like(at), jnp.zeros_like(at))
 
 
-def pick_kernel(
-    fields_hbm, cols_hbm, depth_hbm, wet_hbm, east_hbm, north_hbm, out_ref, fields_ref, cols_ref, real_ref, wet_ref, sems
-):
-    copies = fetch(
-        (fields_hbm, cols_hbm, depth_hbm, east_hbm, north_hbm, wet_hbm),
-        (fields_ref, cols_ref, real_ref.at[0], real_ref.at[1], real_ref.at[2], wet_ref),
-        sems,
-    )
-    for copy in copies:
+def pick_kernel(fields_hbm, cols_hbm, out_ref, fields_ref, cols_ref, sems):
+    for copy in fetch((fields_hbm, cols_hbm), (fields_ref, cols_ref), sems):
         copy.wait()
     nfield, ncol = fields_ref.shape
     high = ncol // 256
     rows = [fields_ref[:, h * 256 : (h + 1) * 256].astype(F32) for h in range(high)]
     table = jnp.concatenate(rows, axis=0).astype(BF16)
     groups, blocks, width = cols_ref.shape[2:]
-    peak = peak_of(real_ref[0], wet_ref[...].astype(F32), real_ref[1], real_ref[2])
-    peak = jnp.broadcast_to(peak, (nfield, 128))
-    big = peak.astype(BF16).astype(F32)
-    middle = (peak - big).astype(BF16).astype(F32)
-    row = lax.broadcasted_iota(jnp.int32, peak.shape, 0)
-    three = jnp.where(row == 0, big, jnp.where(row == 1, middle, jnp.where(row == 2, peak - big - middle, 0.0)))
     for c in range(groups):
         for k in range(blocks):
             cols = cols_ref[0, 0, c, k : k + 1, :]
@@ -90,25 +77,22 @@
             for h in range(1, high):
                 picked = jnp.where(upper == h, both[h * nfield : (h + 1) * nfield], picked)
             out_ref[c, :, k * width : (k + 1) * width] = picked.astype(BF16)
-        out_ref[c, :, blocks * width :] = three.astype(BF16)
-
-
-def pick(fields, cols, depth, wet, east, north):
+
+
+def pick(fields, cols):
     groups, blocks, width = cols.shape[2:]
     return pl.pallas_call(
         pick_kernel,
-        in_specs=[HBM] * 6,
+        in_specs=[HBM] * 2,
         out_specs=VMEM,
-        out_shape=jax.ShapeDtypeStruct((groups, fields.shape[0], blocks * width + 128), BF16),
+        out_shape=jax.ShapeDtypeStruct((groups, fields.shape[0], blocks * width), BF16),
         scratch_shapes=[
             pltpu.VMEM(fields.shape, BF16),
             pltpu.VMEM(cols.shape, jnp.int32),
-            pltpu.VMEM((3, *depth.shape), F32),
-            pltpu.VMEM(depth.shape, jnp.int32),
-            pltpu.SemaphoreType.DMA((6,)),
+            pltpu.SemaphoreType.DMA((2,)),
         ],
         compiler_params=params(56),
-    )(fields, cols, depth, wet, east, north)
+    )(fields, cols)
 
 
 def peak_of(depth, wet, east, north):
@@ -119,17 +103,9 @@
     return lax.all_to_all(peak, axes, split_axis=0, concat_axis=0, tiled=True)
 
 
-def everyone(peak):
-    return exchange(spread_max(exchange(peak, PLANE), COLUMN), COLUMN)
-
-
-def spread_max(seen, axes):
-    return jnp.broadcast_to(jnp.max(seen, axis=0, keepdims=True), (axes_size(axes), 128))
-
-
 def remap_kernel(
     live_ref, picked_hbm, weights_hbm, cells_hbm, depth_hbm, wet_hbm, level_hbm, east_hbm, north_hbm,
-    flux_ref, own_ref, head_ref, tail_ref, peak_ref,
+    flux_ref, own_ref, head_ref, tail_ref,
     picked_ref, weights_ref, cells_ref, wet_ref, spread_ref, total_ref, sems,
 ):
     groups, nfield, width = picked_ref.shape
@@ -146,12 +122,6 @@
     )
     for copy in first:
         copy.wait()
-    peak = None
-    for c in range(groups):
-        three = picked_ref[c, :, blocks * 256 :].astype(F32)
-        one = three[0:1] + (three[1:2] + three[2:3])
-        peak = one if peak is None else jnp.maximum(peak, one)
-    peak_ref[...] = jnp.broadcast_to(peak, peak_ref.shape)
     for c in range(groups):
         loads[c].wait()
         live = live_ref[0, 0, c]
@@ -207,13 +177,12 @@
     return pl.pallas_call(
         remap_kernel,
         in_specs=[SMEM] + [HBM] * 8,
-        out_specs=[VMEM] * 5,
+        out_specs=[VMEM] * 4,
         out_shape=[
             jax.ShapeDtypeStruct((nfield, rows, cols), F32),
             jax.ShapeDtypeStruct((KEPT, rows, cols), F32),
             tile,
             tile,
-            jax.ShapeDtypeStruct((8, 128), F32),
         ],
         scratch_shapes=[
             pltpu.VMEM(picked.shape, BF16),
@@ -280,7 +249,7 @@
     return pltpu.roll(x, x.shape[0] - 1, 0) - pltpu.roll(x, 1, 0)
 
 
-SAMPLES = ((1.0, 0.0), (0.6, 0.0), (1.0, 0.5), (0.6, 0.25))
+SAMPLES = ((0.5, 0.0), (0.25, 0.0), (0.5, 0.25), (0.25, 0.12))
 SLOT = 32
 TERMS = 19
 CLOSE = 4e-6
@@ -312,7 +281,7 @@
     )
 
 
-def offers(rotation, depth, wet, level, east, north, push_x, push_y, fresh, peak):
+def offers(rotation, depth, wet, level, east, north, push_x, push_y, fresh):
     own = (slice(0, depth.shape[0] - 2 * EDGE), slice(0, 128))
     forcing = (push_x, push_y, fresh)
     u, v = [], []
@@ -324,6 +293,7 @@
     shape = terms[0].shape
     index = lax.broadcasted_iota(jnp.int32, shape, 0) * 128 + lax.broadcasted_iota(jnp.int32, shape, 1)
     lane = lax.broadcasted_iota(jnp.int32, (1, 128), 1)
+    peak = peak_of(depth[own], wet[own], east[own], north[own])
     dt = courant / peak
     row = jnp.where(lane == SLOT - 1, peak, 0.0)
     for j, (p, q) in enumerate(SAMPLES):
@@ -368,7 +338,7 @@
 
 
 def offer_kernel(
-    total_rows, row_ref, own_ref, east_ref, west_ref, after_ref, before_ref, seen_ref, kept_ref, state_ref, row_out_ref
+    total_rows, row_ref, own_ref, east_ref, west_ref, after_ref, before_ref, kept_ref, state_ref, row_out_ref
 ):
     full = [extended(at, own_ref, east_ref, west_ref, after_ref, before_ref) for at in range(KEPT)]
     depth, wet, level, east, north, push_x, push_y, fresh = full
@@ -377,8 +347,17 @@
     for at, array in enumerate((level, east, north)):
         state_ref[at] = array
     rotation = turning(row_ref[0], total_rows, depth.shape)
-    row = offers(rotation, depth, wet, level, east, north, push_x, push_y, fresh, jnp.max(seen_ref[...], keepdims=True))
+    row = offers(rotation, depth, wet, level, east, north, push_x, push_y, fresh)
     row_out_ref[...] = jnp.broadcast_to(row, row_out_ref.shape)
+
+
+def most_kernel(rows_ref, out_ref):
+    out_ref[...] = jnp.broadcast_to(jnp.max(rows_ref[...], axis=0, keepdims=True), out_ref.shape)
+
+
+def everyone(peak):
+    row = jax.ShapeDtypeStruct((axes_size(COLUMN), 128), F32)
+    return exchange(call_small(most_kernel, (), (exchange(peak, PLANE),), row), COLUMN)
 
 
 def step_from(total_rows, row_ref, kept_ref, old, peak):
@@ -418,7 +397,7 @@
     lane = lax.broadcasted_iota(jnp.int32, (1, 128), 1)
     true = jnp.max(rows, axis=0, keepdims=True)
     off = jnp.where(lane < 2, jnp.abs(true - guess_ref[0:1, :]) - CLOSE * true, -1.0)
-    good_ref[...] = jnp.broadcast_to(jnp.where(jnp.max(off, keepdims=True) <= 0.0, 1, 0), good_ref.shape)
+    good_ref[0] = jnp.where(jnp.max(off) <= 0.0, 1, 0)
 
 
 def redo_kernel(total_rows, at, row_ref, kept_ref, old_ref, rows_ref, state_ref, peak_ref):
@@ -428,9 +407,13 @@
     peak_ref[...] = jnp.broadcast_to(local_peak(kept_ref, new), peak_ref.shape)
 
 
-def call_small(kernel, scalars, arrays, out_shape):
+def call_small(kernel, scalars, arrays, out_shape, out_specs=None):
     return pl.pallas_call(
-        kernel, in_specs=[SMEM] * len(scalars) + [VMEM] * len(arrays), out_shape=out_shape, compiler_params=params(8)
+        kernel,
+        in_specs=[SMEM] * len(scalars) + [VMEM] * len(arrays),
+        out_shape=out_shape,
+        out_specs=jax.tree.map(lambda _: VMEM, out_shape) if out_specs is None else out_specs,
+        compiler_params=params(8),
     )(*scalars, *arrays)
 
 
@@ -455,9 +438,9 @@
     rim = jax.ShapeDtypeStruct((KEPT + 2, EDGE, cols), F32)
     peak_shape = jax.ShapeDtypeStruct((axes_size(PLANE), 128), F32)
 
-    picked = pick(atm_fields, send_cols, ocean_depth, wet_mask, east_vel, north_vel)
+    picked = pick(atm_fields, send_cols)
     received = lax.all_to_all(picked, "comp", split_axis=0, concat_axis=0, tiled=True)
-    fluxes, own, head, tail, seen = remap(
+    fluxes, own, head, tail = remap(
         live_blocks, received, remap_weights, row_map, ocean_depth, wet_mask, sea_level, east_vel, north_vel
     )
     east, west = neighbours(head, tail, ("comp",))
@@ -466,7 +449,7 @@
     kept, start, row = call_small(
         functools.partial(offer_kernel, total_rows),
         (first_row,),
-        (own, east, west, after, before, seen),
+        (own, east, west, after, before),
         [five, three, peak_shape],
     )
     (row,) = call_small(
@@ -485,7 +468,8 @@
             functools.partial(last_kernel, total_rows),
             (first_row,),
             (kept, third, seen, guess),
-            [jax.ShapeDtypeStruct((3, rows, cols), F32), jax.ShapeDtypeStruct((8, 128), jnp.int32)],
+            [jax.ShapeDtypeStruct((3, rows, cols), F32), jax.ShapeDtypeStruct((1,), jnp.int32)],
+            [VMEM, SMEM],
         )
 
     state, good = last(third, everyone(peak))
@@ -499,7 +483,7 @@
             seen, at = everyone(peak), 2
         return last(state, seen)[0]
 
-    state = lax.cond(good[0, 0] == 1, lambda: state, again)
+    state = lax.cond(good[0] == 1, lambda: state, again)
     return fluxes, state
 
 

time: 129 us -> 127 us (0.984)
  local copies, waits for them, and re-layouts: 3.68 us -> 1.81 us
    pallas_call x5 -> x6, Pallas kernels: 4.14 us -> 4.76 us  [call_small(): pl.pallas_call(kernel, in_specs=[SMEM] * len(scalars) + [VMEM] * len(arra...]
where the time goes in v5:
time: 127 us; the launch traced here: 126 us
  blocking collectives  72 us (57%)
  starting transfers between devices  23.5 us (19%)
  Pallas kernels  15.6 us (12%)
  waiting for transfers between devices  11.7 us (9%)
  local copies, waits for them, and re-layouts  1.81 us (1%)
  between operations  1.44 us (1%)
    all_to_all x3, blocking collectives, exchange(): return lax.all_to_all(peak, axes, split_axis=0, concat_axis=0, tiled=True)  53.5 us
    all_to_all x1, blocking collectives, shards(): lax.all_to_all(picked, 'comp', split_axis=0, concat_axis=0, tiled=True)  18.5 us
    ppermute x2, starting transfers between devices, neighbours(): after = lax.ppermute(head, axes, [(i + 1, i) for i in range(count - 1)])  12.3 us
    all_to_all x1, waiting for transfers between devices, exchange(): return lax.all_to_all(peak, axes, split_axis=0, concat_axis=0, tiled=True)  9.47 us
    pallas_call x1, Pallas kernels, remap(): pl.pallas_call(remap_kernel, in_specs=[SMEM] + [HBM] * 8, out_specs=[VMEM...  8.15 us
    ppermute x2, starting transfers between devices, neighbours(): before = lax.ppermute(tail, axes, [(i, i + 1) for i in range(count - 1)])  5.91 us
    all_to_all x1, starting transfers between devices, exchange(): return lax.all_to_all(peak, axes, split_axis=0, concat_axis=0, tiled=True)  5.3 us
    pallas_call x6, Pallas kernels, call_small(): pl.pallas_call(kernel, in_specs=[SMEM] * len(scalars) + [VMEM] * len(arra...  4.76 us
  transfers between devices with their start and end apart: 5, of which 3 were waited for; matrix products, arithmetic and copies ran while one was open for 0% of the time, Pallas kernels for 0%

profile of v5, /device:TPU:1, one launch (start us, length us, event | category | flops | bytes accessed | tf_op | source)
XLA Modules:
  0.0 126.0 jit_solution(6928123279312288478)
XLA Ops:
  0.6 2.7 %shard_map.113 = bf16[8,24,1024]{2,1,0:T(8,128)(2,1)} custom-call(bf16[24,2048]{1,0:T(8,128)(2,1)} %fields_hbm.1, s32[1,1,8,4,256]{4,3,2,1,0:T(4,128)} %cols_hbm.1), custom_call_target="tpu_custom_call" | custom-call | tf_op jit(solution)/shard_map/pallas_call | solution.py:84
  3.3 18.5 %all_to_all.103.picked_hbm = bf16[8,24,1024]{2,1,0:T(8,128)(2,1)} all-to-all(bf16[8,24,1024]{2,1,0:T(8,128)(2,1)} %shard_map.113), channel_id=1, replica_groups=mesh['comp'=8,'dom_0'=12,'dom_1'=4,'dom_2'=2] {'comp'}, dimensions={0} | all-to-all | bytes 786432 | tf_op jit(solution)/shard_map/all_to_all | solution.py:442
  21.8 8.1 %shard_map.114 = (f32[24,32,128]{2,1,0:T(8,128)}, f32[8,32,128]{2,1,0:T(8,128)}, f32[32,128]{1,0:T(8,128)}, f32[32,128]{1,0:T(8,128)}) custom-call(s32[1,1,8]{2,1,0:T(1,128)} %live_ref.1, bf16[8,24,1024]{2,1,0:T(8,128)(2,1)} %all_to_all.103.picked_hbm, bf16[1,1,8,4,256,256]{5,4,3,2,1,0:T(8,128)(2,1)} %weights_hbm.1, s32[1,1,8,4,256]{4,3,2,1,0:T(4,128)} %cells_hbm.1, ...), custom_call_target="tpu_custom_call" | custom-call | tf_op jit(solution)/shard_map/pallas_call | solution.py:177
  30.0 1.3 %collective-permute-start = (f32[32,128]{1,0:T(8,128)}, f32[32,128]{1,0:T(8,128)S(1)}, u32[]{:S(2)}, u32[]{:S(2)}) collective-permute-start(f32[32,128]{1,0:T(8,128)} %get-tuple-element.44), channel_id=1, source_target_pairs={{96,0},{192,96},{288,192},{384,288},{480,384},{576,480},{672,576},... | collective-permute-start | bytes 49160 | tf_op jit(solution)/shard_map/ppermute | solution.py:41
  31.3 4.0 %collective-permute-start.1 = (f32[32,128]{1,0:T(8,128)}, f32[32,128]{1,0:T(8,128)S(1)}, u32[]{:S(2)}, u32[]{:S(2)}) collective-permute-start(f32[32,128]{1,0:T(8,128)} %get-tuple-element.45), channel_id=1, source_target_pairs={{0,96},{96,192},{192,288},{288,384},{384,480},{480,576},{576,672},... | collective-permute-start | bytes 49160 | tf_op jit(solution)/shard_map/ppermute | solution.py:42
  35.2 0.0 collective-permute-done.east_ref
  35.3 1.1 collective-permute-done.1.west_ref
  36.3 0.0 copy-start
  36.3 0.9 copy-done
  37.2 11.0 %collective-permute-start.2 = (f32[10,8,128]{2,1,0:T(8,128)S(1)}, f32[10,8,128]{2,1,0:T(8,128)S(1)}, u32[]{:S(2)}, u32[]{:S(2)}) collective-permute-start(f32[10,8,128]{2,1,0:T(8,128)S(1)} %get-tuple-element.46), channel_id=1, source_target_pairs={{1,0},{2,1},{3,2},{4,3},{5,4},{6,5},{7,6},{8,7},{9,8},{10,9},{11,1... | collective-permute-start | bytes 122888 | tf_op jit(solution)/shard_map/ppermute | solution.py:41
  48.3 1.9 %collective-permute-start.3 = (f32[10,8,128]{2,1,0:T(8,128)S(1)}, f32[10,8,128]{2,1,0:T(8,128)S(1)}, u32[]{:S(2)}, u32[]{:S(2)}) collective-permute-start(f32[10,8,128]{2,1,0:T(8,128)S(1)} %get-tuple-element.47), channel_id=1, source_target_pairs={{0,1},{1,2},{2,3},{3,4},{4,5},{5,6},{6,7},{7,8},{8,9},{9,10},{10,1... | collective-permute-start | bytes 122888 | tf_op jit(solution)/shard_map/ppermute | solution.py:42
  50.2 0.0 collective-permute-done.2.after_ref
  50.2 1.2 collective-permute-done.3.before_ref
  51.4 0.0 copy-start.1
  51.4 0.9 copy-done.1
  52.3 2.0 %shard_map.116 = (f32[5,48,256]{2,1,0:T(8,128)S(1)}, f32[3,48,256]{2,1,0:T(8,128)S(1)}, f32[32,128]{1,0:T(8,128)S(1)}) custom-call(s32[1]{0:T(128)} %bitcast.24.row_ref, f32[8,32,128]{2,1,0:T(8,128)S(1)} %copy-done.1, f32[32,128]{1,0:T(8,128)S(1)} %collective-permute-done.east_ref, f32[32,128]{1,0:T(8,128)S(1)} %collective-permute-done.1.west_ref, ...), custom_call_target="tpu_custom_call" | custom-call | tf_op jit(solution)/shard_map/pallas_call | solution.py:411
  54.3 15.2 %all_to_all.104 = f32[32,1,128]{2,1,0:T(1,128)S(1)} all-to-all(f32[32,1,128]{2,1,0:T(1,128)S(1)} %bitcast.55), channel_id=1, replica_groups=mesh['comp'=8,'dom_0'=12,'dom_1'=4,'dom_2'=2] {'comp','dom_1'}, dimensions={0} | all-to-all | bytes 32768 | tf_op jit(solution)/shard_map/all_to_all | solution.py:103
  69.5 0.5 shard_map.117
  70.0 26.7 %all_to_all.105 = f32[24,1,128]{2,1,0:T(1,128)S(1)} all-to-all(f32[24,1,128]{2,1,0:T(1,128)S(1)} %bitcast.51), channel_id=1, replica_groups=mesh['comp'=8,'dom_0'=12,'dom_1'=4,'dom_2'=2] {'dom_0','dom_2'}, dimensions={0} | all-to-all | bytes 24576 | tf_op jit(solution)/shard_map/all_to_all | solution.py:103
  96.7 0.7 shard_map.118
  97.5 11.6 %all_to_all.106 = f32[32,1,128]{2,1,0:T(1,128)S(1)} all-to-all(f32[32,1,128]{2,1,0:T(1,128)S(1)} %bitcast.58), channel_id=1, replica_groups=mesh['comp'=8,'dom_0'=12,'dom_1'=4,'dom_2'=2] {'comp','dom_1'}, dimensions={0} | all-to-all | bytes 32768 | tf_op jit(solution)/shard_map/all_to_all | solution.py:103
  109.0 0.6 shard_map.119
  109.7 5.3 %all-to-all-start.10 = ((f32[24,1,128]{2,1,0:T(1,128)}), f32[24,1,128]{2,1,0:T(1,128)S(1)}, u32[]{:S(2)}, u32[]{:S(2)}) async-start(f32[24,1,128]{2,1,0:T(1,128)} %bitcast.35), calls=%async_computation.10 | async-start | bytes 24576 | tf_op jit(solution)/shard_map/all_to_all | solution.py:103
  115.0 9.5 %all-to-all-done.10 = f32[24,1,128]{2,1,0:T(1,128)S(1)} async-done(((f32[24,1,128]{2,1,0:T(1,128)}), f32[24,1,128]{2,1,0:T(1,128)S(1)}, u32[]{:S(2)}, u32[]{:S(2)}) %all-to-all-start.10) | async-done | bytes 12320 | tf_op jit(solution)/shard_map/all_to_all | solution.py:103
  124.4 0.9 shard_map.120
  (2 shorter events, 0.0 us)
Async XLA Ops:
  30.0 5.3 %collective-permute-start = (f32[32,128]{1,0:T(8,128)}, f32[32,128]{1,0:T(8,128)S(1)}, u32[]{:S(2)}, u32[]{:S(2)}) collective-permute-start(f32[32,128]{1,0:T(8,128)} %get-tuple-element.44), channel_id=1, source_target_pairs={{96,0},{192,96},{288,192},{384,288},{480,384},{576,480},{672,576},... | collective-permute-start | bytes 49160 | tf_op jit(solution)/shard_map/ppermute | solution.py:41
  31.3 5.1 %collective-permute-start.1 = (f32[32,128]{1,0:T(8,128)}, f32[32,128]{1,0:T(8,128)S(1)}, u32[]{:S(2)}, u32[]{:S(2)}) collective-permute-start(f32[32,128]{1,0:T(8,128)} %get-tuple-element.45), channel_id=1, source_target_pairs={{0,96},{96,192},{192,288},{288,384},{384,480},{480,576},{576,672},... | collective-permute-start | bytes 49160 | tf_op jit(solution)/shard_map/ppermute | solution.py:42
  36.3 0.9 copy-start
  37.2 13.0 %collective-permute-start.2 = (f32[10,8,128]{2,1,0:T(8,128)S(1)}, f32[10,8,128]{2,1,0:T(8,128)S(1)}, u32[]{:S(2)}, u32[]{:S(2)}) collective-permute-start(f32[10,8,128]{2,1,0:T(8,128)S(1)} %get-tuple-element.46), channel_id=1, source_target_pairs={{1,0},{2,1},{3,2},{4,3},{5,4},{6,5},{7,6},{8,7},{9,8},{10,9},{11,1... | collective-permute-start | bytes 122888 | tf_op jit(solution)/shard_map/ppermute | solution.py:41
  48.3 3.1 %collective-permute-start.3 = (f32[10,8,128]{2,1,0:T(8,128)S(1)}, f32[10,8,128]{2,1,0:T(8,128)S(1)}, u32[]{:S(2)}, u32[]{:S(2)}) collective-permute-start(f32[10,8,128]{2,1,0:T(8,128)S(1)} %get-tuple-element.47), channel_id=1, source_target_pairs={{0,1},{1,2},{2,3},{3,4},{4,5},{5,6},{6,7},{7,8},{8,9},{9,10},{10,1... | collective-permute-start | bytes 122888 | tf_op jit(solution)/shard_map/ppermute | solution.py:42
  51.4 0.9 copy-start.1
  109.7 14.8 %all-to-all-start.10 = ((f32[24,1,128]{2,1,0:T(1,128)}), f32[24,1,128]{2,1,0:T(1,128)S(1)}, u32[]{:S(2)}, u32[]{:S(2)}) async-start(f32[24,1,128]{2,1,0:T(1,128)} %bitcast.35), calls=%async_computation.10 | async-start | bytes 24576 | tf_op jit(solution)/shard_map/all_to_all | solution.py:103

commit v6 on v5

--- a/solution.py
+++ b/solution.py
@@ -103,25 +103,14 @@
     return lax.all_to_all(peak, axes, split_axis=0, concat_axis=0, tiled=True)
 
 
-def remap_kernel(
-    live_ref, picked_hbm, weights_hbm, cells_hbm, depth_hbm, wet_hbm, level_hbm, east_hbm, north_hbm,
-    flux_ref, own_ref, head_ref, tail_ref,
-    picked_ref, weights_ref, cells_ref, wet_ref, spread_ref, total_ref, sems,
-):
-    groups, nfield, width = picked_ref.shape
+FORCED = 8
+
+
+def accumulate(fields, live_ref, picked_ref, weights_ref, cells_ref, spread_ref, total_ref, loads):
+    groups = picked_ref.shape[0]
     blocks = weights_ref.shape[1]
-    pair_rows = 2 * nfield
+    pair_rows = 2 * (fields.stop - fields.start)
     lows = total_ref.shape[1]
-    first = fetch((picked_hbm, cells_hbm), (picked_ref, cells_ref), sems)
-    loads = fetch([weights_hbm.at[0, 0, c] for c in range(groups)], [weights_ref.at[c] for c in range(groups)], sems, 2)
-    rest = fetch(
-        (depth_hbm, level_hbm, east_hbm, north_hbm, wet_hbm),
-        (own_ref.at[0], own_ref.at[2], own_ref.at[3], own_ref.at[4], wet_ref),
-        sems,
-        2 + groups,
-    )
-    for copy in first:
-        copy.wait()
     for c in range(groups):
         loads[c].wait()
         live = live_ref[0, 0, c]
@@ -129,6 +118,7 @@
         for k in range(blocks):
             part = slice(k * 256, (k + 1) * 256)
             contrib = lax.dot_general(picked_ref[c, :, part], weights_ref[c, k], NT, preferred_element_type=F32)
+            contrib = contrib[fields]
             big = contrib.astype(BF16).astype(F32)
             pair = jnp.concatenate([big, contrib - big], axis=0).astype(BF16)
             cell = cells_ref[0, 0, c, k : k + 1, :]
@@ -148,17 +138,49 @@
             total_ref[...] = added
         else:
             total_ref[...] += added
+
+
+def lay_out(total_ref, part_ref):
+    count = part_ref.shape[0]
     for h in range(HIGH):
-        base = h * pair_rows
-        both = total_ref[base : base + nfield, :] + total_ref[base + nfield : base + pair_rows, :]
-        for r in range(lows // 128):
-            flux_ref[:, r * HIGH + h, :] = both[:, r * 128 : (r + 1) * 128]
+        base = h * 2 * count
+        both = total_ref[base : base + count, :] + total_ref[base + count : base + 2 * count, :]
+        for r in range(total_ref.shape[1] // 128):
+            part_ref[:, r * HIGH + h, :] = both[:, r * 128 : (r + 1) * 128]
+
+
+def load_blocks(picked_hbm, cells_hbm, weights_hbm, picked_ref, cells_ref, weights_ref, sems):
+    groups = picked_ref.shape[0]
+    first = fetch((picked_hbm, cells_hbm), (picked_ref, cells_ref), sems)
+    loads = fetch([weights_hbm.at[0, 0, c] for c in range(groups)], [weights_ref.at[c] for c in range(groups)], sems, 2)
+    return first, loads
+
+
+def forced_kernel(
+    live_ref, picked_hbm, weights_hbm, cells_hbm, depth_hbm, wet_hbm, level_hbm, east_hbm, north_hbm,
+    flux_hbm, own_ref, head_ref, tail_ref,
+    picked_ref, weights_ref, cells_ref, wet_ref, part_ref, spread_ref, total_ref, sems,
+):
+    groups = picked_ref.shape[0]
+    first, loads = load_blocks(picked_hbm, cells_hbm, weights_hbm, picked_ref, cells_ref, weights_ref, sems)
+    rest = fetch(
+        (depth_hbm, level_hbm, east_hbm, north_hbm, wet_hbm),
+        (own_ref.at[0], own_ref.at[2], own_ref.at[3], own_ref.at[4], wet_ref),
+        sems,
+        2 + groups,
+    )
+    for copy in first:
+        copy.wait()
+    accumulate(slice(0, FORCED), live_ref, picked_ref, weights_ref, cells_ref, spread_ref, total_ref, loads)
+    lay_out(total_ref, part_ref)
+    store = pltpu.make_async_copy(part_ref, flux_hbm.at[pl.ds(0, FORCED)], sems.at[7 + groups])
+    store.start()
     for copy in rest:
         copy.wait()
     own_ref[1] = wet_ref[...].astype(F32)
-    own_ref[5] = flux_ref[0] / own_ref[0]
-    own_ref[6] = flux_ref[1] / own_ref[0]
-    own_ref[7] = flux_ref[2]
+    own_ref[5] = part_ref[0] / own_ref[0]
+    own_ref[6] = part_ref[1] / own_ref[0]
+    own_ref[7] = part_ref[2]
     lane = lax.broadcasted_iota(jnp.int32, head_ref.shape, 1)
     head = own_ref[0]
     tail = pltpu.roll(own_ref[0], EDGE, 1)
@@ -168,16 +190,50 @@
         tail = jnp.where(here, pltpu.roll(own_ref[at], (at + 1) * EDGE, 1), tail)
     head_ref[...] = head
     tail_ref[...] = tail
-
-
-def remap(live, picked, weights, cells, depth, wet, level, east, north):
+    store.wait()
+
+
+def others_kernel(
+    start, live_ref, picked_hbm, weights_hbm, cells_hbm, old_hbm,
+    flux_hbm, done_ref,
+    picked_ref, weights_ref, cells_ref, part_ref, spread_ref, total_ref, sems,
+):
+    groups = picked_ref.shape[0]
+    first, loads = load_blocks(picked_hbm, cells_hbm, weights_hbm, picked_ref, cells_ref, weights_ref, sems)
+    for copy in first:
+        copy.wait()
+    accumulate(slice(start, start + FORCED), live_ref, picked_ref, weights_ref, cells_ref, spread_ref, total_ref, loads)
+    lay_out(total_ref, part_ref)
+    store = pltpu.make_async_copy(part_ref, flux_hbm.at[pl.ds(start, FORCED)], sems.at[2 + groups])
+    store.start()
+    done_ref[0] = start
+    store.wait()
+
+
+def block_scratch(picked, weights, cells):
+    return [
+        pltpu.VMEM(picked.shape, BF16),
+        pltpu.VMEM(weights.shape[2:], BF16),
+        pltpu.VMEM(cells.shape, jnp.int32),
+    ]
+
+
+def sum_scratch(count, width, rows, cols):
+    return [
+        pltpu.VMEM((count, rows, cols), F32),
+        pltpu.VMEM((HIGH * 2 * count, width), BF16),
+        pltpu.VMEM((HIGH * 2 * count, rows // HIGH * cols), F32),
+    ]
+
+
+def remap_forced(live, picked, weights, cells, depth, wet, level, east, north):
     groups, nfield, width = picked.shape
     rows, cols = depth.shape
     tile = jax.ShapeDtypeStruct((rows, cols), F32)
     return pl.pallas_call(
-        remap_kernel,
+        forced_kernel,
         in_specs=[SMEM] + [HBM] * 8,
-        out_specs=[VMEM] * 4,
+        out_specs=[HBM] + [VMEM] * 3,
         out_shape=[
             jax.ShapeDtypeStruct((nfield, rows, cols), F32),
             jax.ShapeDtypeStruct((KEPT, rows, cols), F32),
@@ -185,16 +241,35 @@
             tile,
         ],
         scratch_shapes=[
-            pltpu.VMEM(picked.shape, BF16),
-            pltpu.VMEM(weights.shape[2:], BF16),
-            pltpu.VMEM(cells.shape, jnp.int32),
+            *block_scratch(picked, weights, cells),
             pltpu.VMEM((rows, cols), jnp.int32),
-            pltpu.VMEM((HIGH * 2 * nfield, cells.shape[3] * cells.shape[4]), BF16),
-            pltpu.VMEM((HIGH * 2 * nfield, rows // HIGH * cols), F32),
-            pltpu.SemaphoreType.DMA((groups + 7,)),
+            *sum_scratch(FORCED, width, rows, cols),
+            pltpu.SemaphoreType.DMA((groups + 8,)),
         ],
         compiler_params=params(56),
     )(live, picked, weights, cells, depth, wet, level, east, north)
+
+
+def remap_others(start, live, picked, weights, cells, fluxes):
+    groups, _, width = picked.shape
+    return pl.pallas_call(
+        functools.partial(others_kernel, start),
+        in_specs=[SMEM] + [HBM] * 4,
+        out_specs=[HBM, SMEM],
+        out_shape=[jax.ShapeDtypeStruct(fluxes.shape, F32), jax.ShapeDtypeStruct((1,), jnp.int32)],
+        input_output_aliases={4: 0},
+        scratch_shapes=[
+            *block_scratch(picked, weights, cells),
+            *sum_scratch(FORCED, width, *fluxes.shape[1:]),
+            pltpu.SemaphoreType.DMA((groups + 3,)),
+        ],
+        cost_estimate=pl.CostEstimate(flops=2_000_000_000, bytes_accessed=8_000_000, transcendentals=0),
+        compiler_params=params(56),
+    )(live, picked, weights, cells, fluxes)
+
+
+def relay_kernel(after_ref, in_ref, out_ref):
+    out_ref[...] = in_ref[...]
 
 
 def edges_kernel(own_ref, east_ref, west_ref, top_ref, bottom_ref):
@@ -440,12 +515,16 @@
 
     picked = pick(atm_fields, send_cols)
     received = lax.all_to_all(picked, "comp", split_axis=0, concat_axis=0, tiled=True)
-    fluxes, own, head, tail = remap(
+    fluxes, own, head, tail = remap_forced(
         live_blocks, received, remap_weights, row_map, ocean_depth, wet_mask, sea_level, east_vel, north_vel
     )
     east, west = neighbours(head, tail, ("comp",))
+    blocks = (live_blocks, received, remap_weights, row_map)
+    fluxes, done = remap_others(FORCED, *blocks, fluxes)
+    own = call_small(relay_kernel, (done,), (own,), jax.ShapeDtypeStruct(own.shape, F32))
     top, bottom = call_small(edges_kernel, (), (own, east, west), [rim, rim])
     after, before = neighbours(top, bottom, DOM)
+    fluxes, _ = remap_others(2 * FORCED, *blocks, fluxes)
     kept, start, row = call_small(
         functools.partial(offer_kernel, total_rows),
         (first_row,),

time: 127 us -> 129 us (1.016)
  Pallas kernels: 15.6 us -> 30.4 us
  waiting for transfers between devices: 11.7 us -> 3.2 us
  blocking collectives: 72 us -> 70 us
  local copies, waits for them, and re-layouts: 1.81 us -> 0.01 us
    pallas_call x1 -> x3, Pallas kernels: 8.15 us -> 22.4 us  [the longest x2 14.8 us: remap_others(): pl.pallas_call(functools.partial(others_kernel, start), in_specs=[SMEM] +...]
    all_to_all x1, waiting for transfers between devices: 9.47 us -> 2.03 us  [exchange(): return lax.all_to_all(peak, axes, split_axis=0, concat_axis=0, tiled=True)]
    all_to_all x3, blocking collectives: 53.5 us -> 51.4 us  [exchange(): return lax.all_to_all(peak, axes, split_axis=0, concat_axis=0, tiled=True)]
    unnamed x4 -> x2, local copies, waits for them, and re-layouts: 1.81 us -> 0.01 us
    pallas_call x6 -> x7, Pallas kernels: 4.76 us -> 5.39 us  [call_small(): pl.pallas_call(kernel, in_specs=[SMEM] * len(scalars) + [VMEM] * len(arra...]
  transfers between devices with their start and end apart: 5 -> 5, of which waited for: 3 -> 2; matrix products, arithmetic and copies ran while one was open for 0% -> 0% of each run, Pallas kernels for 0% -> 12%
where the time goes in v6:
time: 129 us
  blocking collectives  70 us (54%)
  Pallas kernels  30.4 us (24%)
  starting transfers between devices  23.1 us (18%)
  waiting for transfers between devices  3.2 us (2%)
  between operations  1.67 us (1%)
    all_to_all x3, blocking collectives, exchange(): return lax.all_to_all(peak, axes, split_axis=0, concat_axis=0, tiled=True)  51.4 us
    all_to_all x1, blocking collectives, shards(): lax.all_to_all(picked, 'comp', split_axis=0, concat_axis=0, tiled=True)  18.5 us
    pallas_call x2, Pallas kernels, remap_others(): pl.pallas_call(functools.partial(others_kernel, start), in_specs=[SMEM] +...  14.8 us
    ppermute x2, starting transfers between devices, neighbours(): after = lax.ppermute(head, axes, [(i + 1, i) for i in range(count - 1)])  11.9 us
    pallas_call x1, Pallas kernels, remap_forced(): pl.pallas_call(forced_kernel, in_specs=[SMEM] + [HBM] * 8, out_specs=[HBM...  7.59 us
    ppermute x2, starting transfers between devices, neighbours(): before = lax.ppermute(tail, axes, [(i, i + 1) for i in range(count - 1)])  5.91 us
    pallas_call x7, Pallas kernels, call_small(): pl.pallas_call(kernel, in_specs=[SMEM] * len(scalars) + [VMEM] * len(arra...  5.39 us
    all_to_all x1, starting transfers between devices, exchange(): return lax.all_to_all(peak, axes, split_axis=0, concat_axis=0, tiled=True)  5.3 us
  transfers between devices with their start and end apart: 5, of which 2 were waited for; matrix products, arithmetic and copies ran while one was open for 0% of the time, Pallas kernels for 12%

profile of v6, /device:TPU:1, one launch (start us, length us, event | category | flops | bytes accessed | tf_op | source)
XLA Modules:
  0.0 128.6 jit_solution(13929450075855525719)
XLA Ops:
  0.6 2.7 %shard_map.113 = bf16[8,24,1024]{2,1,0:T(8,128)(2,1)} custom-call(bf16[24,2048]{1,0:T(8,128)(2,1)} %fields_hbm.1, s32[1,1,8,4,256]{4,3,2,1,0:T(4,128)} %cols_hbm.1), custom_call_target="tpu_custom_call" | custom-call | tf_op jit(solution)/shard_map/pallas_call | solution.py:84
  3.3 18.5 %all_to_all.103.picked_hbm = bf16[8,24,1024]{2,1,0:T(8,128)(2,1)} all-to-all(bf16[8,24,1024]{2,1,0:T(8,128)(2,1)} %shard_map.113), channel_id=1, replica_groups=mesh['comp'=8,'dom_0'=12,'dom_1'=4,'dom_2'=2] {'comp'}, dimensions={0} | all-to-all | bytes 786432 | tf_op jit(solution)/shard_map/all_to_all | solution.py:517
  21.8 7.6 %shard_map.114 = (f32[24,32,128]{2,1,0:T(8,128)}, f32[8,32,128]{2,1,0:T(8,128)}, f32[32,128]{1,0:T(8,128)}, f32[32,128]{1,0:T(8,128)}) custom-call(s32[1,1,8]{2,1,0:T(1,128)} %live_ref.5, bf16[8,24,1024]{2,1,0:T(8,128)(2,1)} %all_to_all.103.picked_hbm, bf16[1,1,8,4,256,256]{5,4,3,2,1,0:T(8,128)(2,1)} %weights_hbm.5, s32[1,1,8,4,256]{4,3,2,1,0:T(4,128)} %cells_hbm.5, ...), custom_call_target="tpu_custom_call" | custom-call | tf_op jit(solution)/shard_map/pallas_call | solution.py:233
  29.4 0.0 copy-start
  29.4 1.4 %collective-permute-start = (f32[32,128]{1,0:T(8,128)}, f32[32,128]{1,0:T(8,128)S(1)}, u32[]{:S(2)}, u32[]{:S(2)}) collective-permute-start(f32[32,128]{1,0:T(8,128)} %get-tuple-element.50), channel_id=1, source_target_pairs={{96,0},{192,96},{288,192},{384,288},{480,384},{576,480},{672,576},... | collective-permute-start | bytes 49160 | tf_op jit(solution)/shard_map/ppermute | solution.py:41
  30.8 4.0 %collective-permute-start.1 = (f32[32,128]{1,0:T(8,128)}, f32[32,128]{1,0:T(8,128)S(1)}, u32[]{:S(2)}, u32[]{:S(2)}) collective-permute-start(f32[32,128]{1,0:T(8,128)} %get-tuple-element.51), channel_id=1, source_target_pairs={{0,96},{96,192},{192,288},{288,384},{384,480},{480,576},{576,672},... | collective-permute-start | bytes 49160 | tf_op jit(solution)/shard_map/ppermute | solution.py:42
  34.8 7.4 %shard_map.115 = (f32[24,32,128]{2,1,0:T(8,128)}, s32[1]{0:T(128)}) custom-call(s32[1,1,8]{2,1,0:T(1,128)} %live_ref.5, bf16[8,24,1024]{2,1,0:T(8,128)(2,1)} %all_to_all.103.picked_hbm, bf16[1,1,8,4,256,256]{5,4,3,2,1,0:T(8,128)(2,1)} %weights_hbm.5, s32[1,1,8,4,256]{4,3,2,1,0:T(4,128)} %cells_hbm.5, ...), custom_call_target="tpu_custom_call", output_to_operand_aliasing={{0}: (4, {})} | custom-call | flops 2000000000 | bytes 8000000 | tf_op jit(solution)/shard_map/pallas_call | solution.py:255
  42.2 0.0 copy-done
  42.2 0.6 shard_map.117.own_ref
  42.9 0.0 collective-permute-done.east_ref
  42.9 0.0 collective-permute-done.1.west_ref
  42.9 10.5 %collective-permute-start.2 = (f32[10,8,128]{2,1,0:T(8,128)S(1)}, f32[10,8,128]{2,1,0:T(8,128)S(1)}, u32[]{:S(2)}, u32[]{:S(2)}) collective-permute-start(f32[10,8,128]{2,1,0:T(8,128)S(1)} %get-tuple-element.52), channel_id=1, source_target_pairs={{1,0},{2,1},{3,2},{4,3},{5,4},{6,5},{7,6},{8,7},{9,8},{10,9},{11,1... | collective-permute-start | bytes 122888 | tf_op jit(solution)/shard_map/ppermute | solution.py:41
  53.4 1.9 %collective-permute-start.3 = (f32[10,8,128]{2,1,0:T(8,128)S(1)}, f32[10,8,128]{2,1,0:T(8,128)S(1)}, u32[]{:S(2)}, u32[]{:S(2)}) collective-permute-start(f32[10,8,128]{2,1,0:T(8,128)S(1)} %get-tuple-element.53), channel_id=1, source_target_pairs={{0,1},{1,2},{2,3},{3,4},{4,5},{5,6},{6,7},{7,8},{8,9},{9,10},{10,1... | collective-permute-start | bytes 122888 | tf_op jit(solution)/shard_map/ppermute | solution.py:42
  55.3 0.0 collective-permute-done.2.after_ref
  55.3 1.2 collective-permute-done.3.before_ref
  56.5 2.0 %shard_map.119 = (f32[5,48,256]{2,1,0:T(8,128)S(1)}, f32[3,48,256]{2,1,0:T(8,128)S(1)}, f32[32,128]{1,0:T(8,128)S(1)}) custom-call(s32[1]{0:T(128)} %bitcast.24.row_ref, f32[8,32,128]{2,1,0:T(8,128)S(1)} %shard_map.117.own_ref, f32[32,128]{1,0:T(8,128)S(1)} %collective-permute-done.east_ref, f32[32,128]{1,0:T(8,128)S(1)} %collective-permute-done.1.west_ref, ...), custom_call_target="tpu_custom_call" | custom-call | tf_op jit(solution)/shard_map/pallas_call | solution.py:486
  58.5 12.3 %all_to_all.104 = f32[32,1,128]{2,1,0:T(1,128)S(1)} all-to-all(f32[32,1,128]{2,1,0:T(1,128)S(1)} %bitcast.55), channel_id=1, replica_groups=mesh['comp'=8,'dom_0'=12,'dom_1'=4,'dom_2'=2] {'comp','dom_1'}, dimensions={0} | all-to-all | bytes 32768 | tf_op jit(solution)/shard_map/all_to_all | solution.py:103
  70.8 0.5 shard_map.120
  71.3 27.6 %all_to_all.105 = f32[24,1,128]{2,1,0:T(1,128)S(1)} all-to-all(f32[24,1,128]{2,1,0:T(1,128)S(1)} %bitcast.51), channel_id=1, replica_groups=mesh['comp'=8,'dom_0'=12,'dom_1'=4,'dom_2'=2] {'dom_0','dom_2'}, dimensions={0} | all-to-all | bytes 24576 | tf_op jit(solution)/shard_map/all_to_all | solution.py:103
  98.9 0.7 shard_map.121
  99.7 11.6 %all_to_all.106 = f32[32,1,128]{2,1,0:T(1,128)S(1)} all-to-all(f32[32,1,128]{2,1,0:T(1,128)S(1)} %bitcast.58), channel_id=1, replica_groups=mesh['comp'=8,'dom_0'=12,'dom_1'=4,'dom_2'=2] {'comp','dom_1'}, dimensions={0} | all-to-all | bytes 32768 | tf_op jit(solution)/shard_map/all_to_all | solution.py:103
  111.3 0.6 shard_map.122
  111.9 5.3 %all-to-all-start.10 = ((f32[24,1,128]{2,1,0:T(1,128)}), f32[24,1,128]{2,1,0:T(1,128)S(1)}, u32[]{:S(2)}, u32[]{:S(2)}) async-start(f32[24,1,128]{2,1,0:T(1,128)} %bitcast.35), calls=%async_computation.10 | async-start | bytes 24576 | tf_op jit(solution)/shard_map/all_to_all | solution.py:103
  117.2 7.4 %shard_map.116 = (f32[24,32,128]{2,1,0:T(8,128)}, s32[1]{0:T(128)}) custom-call(s32[1,1,8]{2,1,0:T(1,128)} %live_ref.5, bf16[8,24,1024]{2,1,0:T(8,128)(2,1)} %all_to_all.103.picked_hbm, bf16[1,1,8,4,256,256]{5,4,3,2,1,0:T(8,128)(2,1)} %weights_hbm.5, s32[1,1,8,4,256]{4,3,2,1,0:T(4,128)} %cells_hbm.5, ...), custom_call_target="tpu_custom_call", output_to_operand_aliasing={{0}: (4, {})} | custom-call | flops 2000000000 | bytes 8000000 | tf_op jit(solution)/shard_map/pallas_call | solution.py:255
  124.6 2.0 %all-to-all-done.10 = f32[24,1,128]{2,1,0:T(1,128)S(1)} async-done(((f32[24,1,128]{2,1,0:T(1,128)}), f32[24,1,128]{2,1,0:T(1,128)S(1)}, u32[]{:S(2)}, u32[]{:S(2)}) %all-to-all-start.10) | async-done | bytes 12320 | tf_op jit(solution)/shard_map/all_to_all | solution.py:103
  126.6 0.9 shard_map.123
  128.2 0.2 conditional.1
  (1 shorter events, 0.0 us)
Async XLA Ops:
  29.4 12.8 %copy-start = (f32[8,32,128]{2,1,0:T(8,128)S(1)}, f32[8,32,128]{2,1,0:T(8,128)}, u32[]{:S(2)}) copy-start(f32[8,32,128]{2,1,0:T(8,128)} %get-tuple-element.49.in_ref) | copy-start | bytes 393220
  29.4 13.5 %collective-permute-start = (f32[32,128]{1,0:T(8,128)}, f32[32,128]{1,0:T(8,128)S(1)}, u32[]{:S(2)}, u32[]{:S(2)}) collective-permute-start(f32[32,128]{1,0:T(8,128)} %get-tuple-element.50), channel_id=1, source_target_pairs={{96,0},{192,96},{288,192},{384,288},{480,384},{576,480},{672,576},... | collective-permute-start | bytes 49160 | tf_op jit(solution)/shard_map/ppermute | solution.py:41
  30.8 12.0 %collective-permute-start.1 = (f32[32,128]{1,0:T(8,128)}, f32[32,128]{1,0:T(8,128)S(1)}, u32[]{:S(2)}, u32[]{:S(2)}) collective-permute-start(f32[32,128]{1,0:T(8,128)} %get-tuple-element.51), channel_id=1, source_target_pairs={{0,96},{96,192},{192,288},{288,384},{384,480},{480,576},{576,672},... | collective-permute-start | bytes 49160 | tf_op jit(solution)/shard_map/ppermute | solution.py:42
  42.9 12.4 %collective-permute-start.2 = (f32[10,8,128]{2,1,0:T(8,128)S(1)}, f32[10,8,128]{2,1,0:T(8,128)S(1)}, u32[]{:S(2)}, u32[]{:S(2)}) collective-permute-start(f32[10,8,128]{2,1,0:T(8,128)S(1)} %get-tuple-element.52), channel_id=1, source_target_pairs={{1,0},{2,1},{3,2},{4,3},{5,4},{6,5},{7,6},{8,7},{9,8},{10,9},{11,1... | collective-permute-start | bytes 122888 | tf_op jit(solution)/shard_map/ppermute | solution.py:41
  53.4 3.1 %collective-permute-start.3 = (f32[10,8,128]{2,1,0:T(8,128)S(1)}, f32[10,8,128]{2,1,0:T(8,128)S(1)}, u32[]{:S(2)}, u32[]{:S(2)}) collective-permute-start(f32[10,8,128]{2,1,0:T(8,128)S(1)} %get-tuple-element.53), channel_id=1, source_target_pairs={{0,1},{1,2},{2,3},{3,4},{4,5},{5,6},{6,7},{7,8},{8,9},{9,10},{10,1... | collective-permute-start | bytes 122888 | tf_op jit(solution)/shard_map/ppermute | solution.py:42
  111.9 14.8 %all-to-all-start.10 = ((f32[24,1,128]{2,1,0:T(1,128)}), f32[24,1,128]{2,1,0:T(1,128)S(1)}, u32[]{:S(2)}, u32[]{:S(2)}) async-start(f32[24,1,128]{2,1,0:T(1,128)} %bitcast.35), calls=%async_computation.10 | async-start | bytes 24576 | tf_op jit(solution)/shard_map/all_to_all | solution.py:103

commit v7 on v5

--- a/solution.py
+++ b/solution.py
@@ -197,6 +197,10 @@
     )(live, picked, weights, cells, depth, wet, level, east, north)
 
 
+def relay_kernel(in_ref, out_ref):
+    out_ref[...] = in_ref[...]
+
+
 def edges_kernel(own_ref, east_ref, west_ref, top_ref, bottom_ref):
     rows = own_ref.shape[1]
     for ref, part in ((top_ref, slice(0, EDGE)), (bottom_ref, slice(rows - EDGE, rows))):
@@ -444,6 +448,7 @@
         live_blocks, received, remap_weights, row_map, ocean_depth, wet_mask, sea_level, east_vel, north_vel
     )
     east, west = neighbours(head, tail, ("comp",))
+    own = call_small(relay_kernel, (), (own,), jax.ShapeDtypeStruct(own.shape, F32))
     top, bottom = call_small(edges_kernel, (), (own, east, west), [rim, rim])
     after, before = neighbours(top, bottom, DOM)
     kept, start, row = call_small(

time: 127 us -> 125 us (0.984)
    pallas_call x6 -> x7, Pallas kernels: 4.76 us -> 4.77 us  [call_small(): pl.pallas_call(kernel, in_specs=[SMEM] * len(scalars) + [VMEM] * len(arra...]
where the time goes in v7:
time: 125 us; the launch traced here: 124 us
  blocking collectives  72 us (58%)
  starting transfers between devices  23.5 us (19%)
  Pallas kernels  15.6 us (12%)
  waiting for transfers between devices  10.8 us (9%)
  between operations  1.44 us (1%)
    all_to_all x3, blocking collectives, exchange(): return lax.all_to_all(peak, axes, split_axis=0, concat_axis=0, tiled=True)  53.5 us
    all_to_all x1, blocking collectives, shards(): lax.all_to_all(picked, 'comp', split_axis=0, concat_axis=0, tiled=True)  18.5 us
    ppermute x2, starting transfers between devices, neighbours(): after = lax.ppermute(head, axes, [(i + 1, i) for i in range(count - 1)])  12.3 us
    all_to_all x1, waiting for transfers between devices, exchange(): return lax.all_to_all(peak, axes, split_axis=0, concat_axis=0, tiled=True)  9.47 us
    pallas_call x1, Pallas kernels, remap(): pl.pallas_call(remap_kernel, in_specs=[SMEM] + [HBM] * 8, out_specs=[VMEM...  8.15 us
    ppermute x2, starting transfers between devices, neighbours(): before = lax.ppermute(tail, axes, [(i, i + 1) for i in range(count - 1)])  5.91 us
    all_to_all x1, starting transfers between devices, exchange(): return lax.all_to_all(peak, axes, split_axis=0, concat_axis=0, tiled=True)  5.3 us
    pallas_call x7, Pallas kernels, call_small(): pl.pallas_call(kernel, in_specs=[SMEM] * len(scalars) + [VMEM] * len(arra...  4.77 us
  transfers between devices with their start and end apart: 5, of which 3 were waited for; matrix products, arithmetic and copies ran while one was open for 0% of the time, Pallas kernels for 0%

profile of v7, /device:TPU:1, one launch (start us, length us, event | category | flops | bytes accessed | tf_op | source)
XLA Modules:
  0.0 124.2 jit_solution(3656645887164463272)
XLA Ops:
  0.6 2.7 %shard_map.113 = bf16[8,24,1024]{2,1,0:T(8,128)(2,1)} custom-call(bf16[24,2048]{1,0:T(8,128)(2,1)} %fields_hbm.1, s32[1,1,8,4,256]{4,3,2,1,0:T(4,128)} %cols_hbm.1), custom_call_target="tpu_custom_call" | custom-call | tf_op jit(solution)/shard_map/pallas_call | solution.py:84
  3.3 18.5 %all_to_all.103.picked_hbm = bf16[8,24,1024]{2,1,0:T(8,128)(2,1)} all-to-all(bf16[8,24,1024]{2,1,0:T(8,128)(2,1)} %shard_map.113), channel_id=1, replica_groups=mesh['comp'=8,'dom_0'=12,'dom_1'=4,'dom_2'=2] {'comp'}, dimensions={0} | all-to-all | bytes 786432 | tf_op jit(solution)/shard_map/all_to_all | solution.py:446
  21.8 8.1 %shard_map.114 = (f32[24,32,128]{2,1,0:T(8,128)}, f32[8,32,128]{2,1,0:T(8,128)}, f32[32,128]{1,0:T(8,128)}, f32[32,128]{1,0:T(8,128)}) custom-call(s32[1,1,8]{2,1,0:T(1,128)} %live_ref.1, bf16[8,24,1024]{2,1,0:T(8,128)(2,1)} %all_to_all.103.picked_hbm, bf16[1,1,8,4,256,256]{5,4,3,2,1,0:T(8,128)(2,1)} %weights_hbm.1, s32[1,1,8,4,256]{4,3,2,1,0:T(4,128)} %cells_hbm.1, ...), custom_call_target="tpu_custom_call" | custom-call | tf_op jit(solution)/shard_map/pallas_call | solution.py:177
  30.0 1.3 %collective-permute-start = (f32[32,128]{1,0:T(8,128)}, f32[32,128]{1,0:T(8,128)S(1)}, u32[]{:S(2)}, u32[]{:S(2)}) collective-permute-start(f32[32,128]{1,0:T(8,128)} %get-tuple-element.44), channel_id=1, source_target_pairs={{96,0},{192,96},{288,192},{384,288},{480,384},{576,480},{672,576},... | collective-permute-start | bytes 49160 | tf_op jit(solution)/shard_map/ppermute | solution.py:41
  31.3 4.0 %collective-permute-start.1 = (f32[32,128]{1,0:T(8,128)}, f32[32,128]{1,0:T(8,128)S(1)}, u32[]{:S(2)}, u32[]{:S(2)}) collective-permute-start(f32[32,128]{1,0:T(8,128)} %get-tuple-element.45), channel_id=1, source_target_pairs={{0,96},{96,192},{192,288},{288,384},{384,480},{480,576},{576,672},... | collective-permute-start | bytes 49160 | tf_op jit(solution)/shard_map/ppermute | solution.py:42
  35.2 0.0 copy-start
  35.3 0.9 copy-done
  36.2 0.0 collective-permute-done.east_ref
  36.2 0.1 collective-permute-done.1.west_ref
  36.3 11.0 %collective-permute-start.2 = (f32[10,8,128]{2,1,0:T(8,128)S(1)}, f32[10,8,128]{2,1,0:T(8,128)S(1)}, u32[]{:S(2)}, u32[]{:S(2)}) collective-permute-start(f32[10,8,128]{2,1,0:T(8,128)S(1)} %get-tuple-element.46), channel_id=1, source_target_pairs={{1,0},{2,1},{3,2},{4,3},{5,4},{6,5},{7,6},{8,7},{9,8},{10,9},{11,1... | collective-permute-start | bytes 122888 | tf_op jit(solution)/shard_map/ppermute | solution.py:41
  47.3 1.9 %collective-permute-start.3 = (f32[10,8,128]{2,1,0:T(8,128)S(1)}, f32[10,8,128]{2,1,0:T(8,128)S(1)}, u32[]{:S(2)}, u32[]{:S(2)}) collective-permute-start(f32[10,8,128]{2,1,0:T(8,128)S(1)} %get-tuple-element.47), channel_id=1, source_target_pairs={{0,1},{1,2},{2,3},{3,4},{4,5},{5,6},{6,7},{7,8},{8,9},{9,10},{10,1... | collective-permute-start | bytes 122888 | tf_op jit(solution)/shard_map/ppermute | solution.py:42
  49.3 0.0 collective-permute-done.2.after_ref
  49.3 1.2 collective-permute-done.3.before_ref
  50.5 2.0 %shard_map.117 = (f32[5,48,256]{2,1,0:T(8,128)S(1)}, f32[3,48,256]{2,1,0:T(8,128)S(1)}, f32[32,128]{1,0:T(8,128)S(1)}) custom-call(s32[1]{0:T(128)} %bitcast.24.row_ref, f32[8,32,128]{2,1,0:T(8,128)S(1)} %shard_map.115.own_ref, f32[32,128]{1,0:T(8,128)S(1)} %collective-permute-done.east_ref, f32[32,128]{1,0:T(8,128)S(1)} %collective-permute-done.1.west_ref, ...), custom_call_target="tpu_custom_call" | custom-call | tf_op jit(solution)/shard_map/pallas_call | solution.py:415
  52.5 15.2 %all_to_all.104 = f32[32,1,128]{2,1,0:T(1,128)S(1)} all-to-all(f32[32,1,128]{2,1,0:T(1,128)S(1)} %bitcast.55), channel_id=1, replica_groups=mesh['comp'=8,'dom_0'=12,'dom_1'=4,'dom_2'=2] {'comp','dom_1'}, dimensions={0} | all-to-all | bytes 32768 | tf_op jit(solution)/shard_map/all_to_all | solution.py:103
  67.7 0.5 shard_map.118
  68.2 26.7 %all_to_all.105 = f32[24,1,128]{2,1,0:T(1,128)S(1)} all-to-all(f32[24,1,128]{2,1,0:T(1,128)S(1)} %bitcast.51), channel_id=1, replica_groups=mesh['comp'=8,'dom_0'=12,'dom_1'=4,'dom_2'=2] {'dom_0','dom_2'}, dimensions={0} | all-to-all | bytes 24576 | tf_op jit(solution)/shard_map/all_to_all | solution.py:103
  94.9 0.7 shard_map.119
  95.7 11.6 %all_to_all.106 = f32[32,1,128]{2,1,0:T(1,128)S(1)} all-to-all(f32[32,1,128]{2,1,0:T(1,128)S(1)} %bitcast.58), channel_id=1, replica_groups=mesh['comp'=8,'dom_0'=12,'dom_1'=4,'dom_2'=2] {'comp','dom_1'}, dimensions={0} | all-to-all | bytes 32768 | tf_op jit(solution)/shard_map/all_to_all | solution.py:103
  107.2 0.6 shard_map.120
  107.8 5.3 %all-to-all-start.10 = ((f32[24,1,128]{2,1,0:T(1,128)}), f32[24,1,128]{2,1,0:T(1,128)S(1)}, u32[]{:S(2)}, u32[]{:S(2)}) async-start(f32[24,1,128]{2,1,0:T(1,128)} %bitcast.35), calls=%async_computation.10 | async-start | bytes 24576 | tf_op jit(solution)/shard_map/all_to_all | solution.py:103
  113.1 9.5 %all-to-all-done.10 = f32[24,1,128]{2,1,0:T(1,128)S(1)} async-done(((f32[24,1,128]{2,1,0:T(1,128)}), f32[24,1,128]{2,1,0:T(1,128)S(1)}, u32[]{:S(2)}, u32[]{:S(2)}) %all-to-all-start.10) | async-done | bytes 12320 | tf_op jit(solution)/shard_map/all_to_all | solution.py:103
  122.6 0.9 shard_map.121
  (3 shorter events, 0.0 us)
Async XLA Ops:
  30.0 6.2 %collective-permute-start = (f32[32,128]{1,0:T(8,128)}, f32[32,128]{1,0:T(8,128)S(1)}, u32[]{:S(2)}, u32[]{:S(2)}) collective-permute-start(f32[32,128]{1,0:T(8,128)} %get-tuple-element.44), channel_id=1, source_target_pairs={{96,0},{192,96},{288,192},{384,288},{480,384},{576,480},{672,576},... | collective-permute-start | bytes 49160 | tf_op jit(solution)/shard_map/ppermute | solution.py:41
  31.3 5.1 %collective-permute-start.1 = (f32[32,128]{1,0:T(8,128)}, f32[32,128]{1,0:T(8,128)S(1)}, u32[]{:S(2)}, u32[]{:S(2)}) collective-permute-start(f32[32,128]{1,0:T(8,128)} %get-tuple-element.45), channel_id=1, source_target_pairs={{0,96},{96,192},{192,288},{288,384},{384,480},{480,576},{576,672},... | collective-permute-start | bytes 49160 | tf_op jit(solution)/shard_map/ppermute | solution.py:42
  35.2 0.9 copy-start
  36.3 13.0 %collective-permute-start.2 = (f32[10,8,128]{2,1,0:T(8,128)S(1)}, f32[10,8,128]{2,1,0:T(8,128)S(1)}, u32[]{:S(2)}, u32[]{:S(2)}) collective-permute-start(f32[10,8,128]{2,1,0:T(8,128)S(1)} %get-tuple-element.46), channel_id=1, source_target_pairs={{1,0},{2,1},{3,2},{4,3},{5,4},{6,5},{7,6},{8,7},{9,8},{10,9},{11,1... | collective-permute-start | bytes 122888 | tf_op jit(solution)/shard_map/ppermute | solution.py:41
  47.3 3.1 %collective-permute-start.3 = (f32[10,8,128]{2,1,0:T(8,128)S(1)}, f32[10,8,128]{2,1,0:T(8,128)S(1)}, u32[]{:S(2)}, u32[]{:S(2)}) collective-permute-start(f32[10,8,128]{2,1,0:T(8,128)S(1)} %get-tuple-element.47), channel_id=1, source_target_pairs={{0,1},{1,2},{2,3},{3,4},{4,5},{5,6},{6,7},{7,8},{8,9},{9,10},{10,1... | collective-permute-start | bytes 122888 | tf_op jit(solution)/shard_map/ppermute | solution.py:42
  107.8 14.8 %all-to-all-start.10 = ((f32[24,1,128]{2,1,0:T(1,128)}), f32[24,1,128]{2,1,0:T(1,128)S(1)}, u32[]{:S(2)}, u32[]{:S(2)}) async-start(f32[24,1,128]{2,1,0:T(1,128)} %bitcast.35), calls=%async_computation.10 | async-start | bytes 24576 | tf_op jit(solution)/shard_map/all_to_all | solution.py:103
